TPU v7x, 32 devices: a whole 2x2x4 slice. The times are simulated.
32 devices in a mesh: band: 16 (over z, y, x), head: 2 (over core).
Axes of the slice: x: 2, y: 2, z: 4, core: 2. Of those that a mesh axis runs over, the one named last changes fastest.
Arguments:
- grid_state: bfloat16 [65536, 100], P('band'), may hold values from -6 to 6
- hidden_state: bfloat16 [16384, 1024], P('band', 'head'), may hold values from -6 to 6
- encoder_sources: int32 [16384, 32], P('band'), may hold values from 0 to 12287, as said below
- encoder_counts: int32 [16384], P('band'), may hold values from 1 to 32
- decoder_sources: int32 [65536, 4], P('band'), may hold values from 0 to 16383, as said below
- decoder_counts: int32 [65536], P('band'), may hold values from 1 to 4
- encoder_keys: bfloat16 [100, 1024], P(None, 'head'), may hold values from -0.625 to 0.625
- encoder_values: bfloat16 [100, 1024], P(None, 'head'), may hold values from -0.625 to 0.625
- encoder_query: bfloat16 [1024, 1024], P(None, 'head'), may hold values from -0.1875 to 0.1875
- encoder_output: bfloat16 [1024, 1024], P('head'), may hold values from -0.1875 to 0.1875
- window_query: bfloat16 [1024, 1024], P(None, 'head'), may hold values from -0.1875 to 0.1875
- window_keys: bfloat16 [1024, 1024], P(None, 'head'), may hold values from -0.1875 to 0.1875
- window_values: bfloat16 [1024, 1024], P(None, 'head'), may hold values from -0.1875 to 0.1875
- window_output: bfloat16 [1024, 1024], P('head'), may hold values from -0.1875 to 0.1875
- feed_up: bfloat16 [1024, 4096], P(None, 'head'), may hold values from -0.1875 to 0.1875
- feed_down: bfloat16 [4096, 1024], P('head'), may hold values from -0.09375 to 0.09375
- decoder_query: bfloat16 [100, 1024], P(None, 'head'), may hold values from -0.625 to 0.625
- decoder_keys: bfloat16 [1024, 1024], P(None, 'head'), may hold values from -0.1875 to 0.1875
- decoder_values: bfloat16 [1024, 1024], P(None, 'head'), may hold values from -0.1875 to 0.1875
- decoder_output: bfloat16 [1024, 100], P('head'), may hold values from -0.1875 to 0.1875
Outputs:
- grid_next: bfloat16 [65536, 100], P(('band', 'head'))
- hidden_final: bfloat16 [16384, 1024], P('band', 'head')
Inputs may be any that keep to these rules, and one draw needn't show every extreme that they name: Grid band c holds the grid points c * 4096 to (c + 1) * 4096 - 1 and hidden band c the hidden nodes c * 1024 to (c + 1) * 1024 - 1; slot e of hidden node n names the grid point (n // 1024 - 1) * 4096 + encoder_sources[n, e], which lies in a band that exists. Only the first encoder_counts[n] slots are edges. `decoder_sources`: every slot of grid point g names a hidden node of the bands g // 4096 - 1 to g // 4096 + 1 that exist. Only the first decoder_counts[g] slots are edges.
All inputs are finite; a program needn't handle non-finite values.
Results may differ from a plain program's by a relative error of at most 0.015.
Values may be sent and summed in bfloat16 or wider, within the bound.
No kernel may reach another device: no remote copies, remote signals or barrier semaphores. Data moves between devices by JAX's collectives and lax.ppermute only.
A program may use at most 320 MiB of HBM per device.

v0:
```python
import jax
import jax.numpy as jnp
from jax import lax
from jax.sharding import PartitionSpec as P

HALF_WIN = 560
HEAD_DIM = 64


EPSILON = 1e-05
NEGATIVE = -1e30


def with_halo(cells, sides, width):
    for axis, dim in sides:
        count = lax.axis_size(axis)
        ends = count - 1
        head = lax.slice_in_dim(cells, 0, width, axis=dim)
        tail = lax.slice_in_dim(cells, cells.shape[dim] - width, cells.shape[dim], axis=dim)
        cells = jnp.concatenate(
            [
                lax.ppermute(tail, axis, [(i, (i + 1) % count) for i in range(ends)]),
                cells,
                lax.ppermute(head, axis, [((i + 1) % count, i) for i in range(ends)]),
            ],
            axis=dim,
        )
    return cells


def layer_norm(matrix):
    as_float = matrix.astype(jnp.float32)
    centred = as_float - jnp.mean(as_float, axis=-1, keepdims=True)
    variance = jnp.mean(centred * centred, axis=-1, keepdims=True)
    return (centred * lax.rsqrt(variance + EPSILON)).astype(jnp.bfloat16)


def project(matrix, weight):
    return jnp.dot(matrix, weight, preferred_element_type=jnp.float32).astype(jnp.bfloat16)


def softmax_weights(scores):
    powers = jnp.exp(scores)
    return (powers / jnp.sum(powers, axis=-1, keepdims=True)).astype(jnp.bfloat16)


def edge_attention(query, gathered, counts):
    row_count, slot_count, double_width = gathered.shape
    full_width = double_width // 2
    head_count = full_width // HEAD_DIM
    query_heads = query.reshape(row_count, head_count, HEAD_DIM)
    key_heads = gathered[:, :, :full_width].reshape(row_count, slot_count, head_count, HEAD_DIM)
    value_heads = gathered[:, :, full_width:].reshape(row_count, slot_count, head_count, HEAD_DIM)
    scores = jnp.einsum(
        "rhd,rehd->rhe", query_heads, key_heads, preferred_element_type=jnp.float32
    ) * HEAD_DIM ** (-0.5)
    slot_live = jnp.arange(slot_count, dtype=jnp.int32)[None, None, :] < counts[:, None, None]
    weights = softmax_weights(jnp.where(slot_live, scores, NEGATIVE))
    mixed = jnp.einsum("rhe,rehd->rhd", weights, value_heads, preferred_element_type=jnp.float32)
    return mixed.reshape(row_count, full_width).astype(jnp.bfloat16)


def slot_attention(query, table, sources, counts):
    row_count, full_width = query.shape
    head_count = full_width // HEAD_DIM
    query_heads = query.astype(jnp.float32).reshape(row_count, head_count, HEAD_DIM)
    slot_count = sources.shape[1]
    value_list = []
    power_list = []
    for slot in range(slot_count):
        picked = jnp.take(table, sources[:, slot], axis=0)
        key_heads = (
            picked[:, :full_width].astype(jnp.float32).reshape(row_count, head_count, HEAD_DIM)
        )
        value_list.append(picked[:, full_width:])
        score = jnp.sum(query_heads * key_heads, axis=-1) * HEAD_DIM ** (-0.5)
        score = jnp.where((slot < counts)[:, None], score, NEGATIVE)
        power_list.append(jnp.exp(score))
    total = power_list[0]
    for slot in range(1, slot_count):
        total = total + power_list[slot]
    mixed = jnp.zeros((row_count, head_count, HEAD_DIM), jnp.float32)
    for slot in range(slot_count):
        weight = (power_list[slot] / total).astype(jnp.bfloat16).astype(jnp.float32)
        value_heads = value_list[slot].astype(jnp.float32).reshape(row_count, head_count, HEAD_DIM)
        mixed = mixed + weight[:, :, None] * value_heads
    return mixed.reshape(row_count, full_width).astype(jnp.bfloat16)


def window_attention(query, pairs, live):
    query_count, full_width = query.shape
    span_count = pairs.shape[0]
    head_count = full_width // HEAD_DIM
    query_heads = query.reshape(query_count, head_count, HEAD_DIM)
    key_heads = pairs[:, :full_width].reshape(span_count, head_count, HEAD_DIM)
    value_heads = pairs[:, full_width:].reshape(span_count, head_count, HEAD_DIM)
    scores = jnp.einsum(
        "qhd,shd->hqs", query_heads, key_heads, preferred_element_type=jnp.float32
    ) * HEAD_DIM ** (-0.5)
    weights = softmax_weights(jnp.where(live[None], scores, NEGATIVE))
    mixed = jnp.einsum("hqs,shd->qhd", weights, value_heads, preferred_element_type=jnp.float32)
    return mixed.reshape(query_count, full_width).astype(jnp.bfloat16)


def local(
    grid_state,
    hidden_state,
    encoder_sources,
    encoder_counts,
    decoder_sources,
    decoder_counts,
    encoder_keys,
    encoder_values,
    encoder_query,
    encoder_output,
    window_query,
    window_keys,
    window_values,
    window_output,
    feed_up,
    feed_down,
    decoder_query,
    decoder_keys,
    decoder_values,
    decoder_output,
):
    band_index = lax.axis_index("band")
    grid_count = grid_state.shape[0]
    node_count = hidden_state.shape[0]
    grid_pair_weight = jnp.concatenate((encoder_keys, encoder_values), axis=1)
    near_grid = with_halo(grid_state, (("band", 0),), grid_count)
    near_grid_pairs = project(near_grid, grid_pair_weight)
    whole_state = lax.all_gather(hidden_state, "head", axis=1, tiled=True)
    enc_query = project(layer_norm(whole_state), encoder_query)
    enc_mix = edge_attention(
        enc_query, jnp.take(near_grid_pairs, encoder_sources, axis=0), encoder_counts
    )
    enc_update = lax.psum_scatter(
        jnp.dot(enc_mix, encoder_output, preferred_element_type=jnp.float32).astype(jnp.bfloat16),
        "head",
        scatter_dimension=1,
        tiled=True,
    ).astype(jnp.float32)
    hidden_mid = (hidden_state.astype(jnp.float32) + enc_update).astype(jnp.bfloat16)
    whole_mid = lax.all_gather(hidden_mid, "head", axis=1, tiled=True)
    normed_mid = layer_norm(whole_mid)
    win_query = project(normed_mid, window_query)
    win_pairs = project(normed_mid, jnp.concatenate((window_keys, window_values), axis=1))
    padded_pairs = with_halo(win_pairs, (("band", 0),), HALF_WIN)
    total_nodes = node_count * lax.axis_size("band")
    first_node = band_index * node_count
    block_rows = min(512, node_count)
    span_rows = block_rows + 2 * HALF_WIN

    def attend(start):
        block_query = lax.dynamic_slice_in_dim(win_query, start, block_rows, 0)
        block_pairs = lax.dynamic_slice_in_dim(padded_pairs, start, span_rows, 0)
        query_pos = first_node + start + jnp.arange(block_rows, dtype=jnp.int32)
        key_pos = first_node + start - HALF_WIN + jnp.arange(span_rows, dtype=jnp.int32)
        distance = jnp.abs(query_pos[:, None] - key_pos[None, :])
        live = (distance <= HALF_WIN) & (key_pos[None, :] >= 0) & (key_pos[None, :] < total_nodes)
        return window_attention(block_query, block_pairs, live)

    starts = jnp.arange(node_count // block_rows, dtype=jnp.int32) * block_rows
    win_mix = lax.map(attend, starts).reshape(node_count, win_query.shape[1])
    win_update = lax.psum_scatter(
        jnp.dot(win_mix, window_output, preferred_element_type=jnp.float32).astype(jnp.bfloat16),
        "head",
        scatter_dimension=1,
        tiled=True,
    ).astype(jnp.float32)
    hidden_att = (hidden_mid.astype(jnp.float32) + win_update).astype(jnp.bfloat16)
    whole_att = lax.all_gather(hidden_att, "head", axis=1, tiled=True)
    inner = jax.nn.gelu(
        jnp.dot(layer_norm(whole_att), feed_up, preferred_element_type=jnp.float32),
        approximate=True,
    ).astype(jnp.bfloat16)
    feed_update = lax.psum_scatter(
        jnp.dot(inner, feed_down, preferred_element_type=jnp.float32).astype(jnp.bfloat16),
        "head",
        scatter_dimension=1,
        tiled=True,
    ).astype(jnp.float32)
    hidden_final = (hidden_att.astype(jnp.float32) + feed_update).astype(jnp.bfloat16)
    whole_final = lax.all_gather(hidden_final, "head", axis=1, tiled=True)
    query_weight, key_weight, value_weight, out_weight = (
        decoder_query,
        decoder_keys,
        decoder_values,
        decoder_output,
    )
    own_grid, own_sources, own_counts = (grid_state, decoder_sources, decoder_counts)
    node_pair_weight = jnp.concatenate((key_weight, value_weight), axis=1)
    near_final = with_halo(whole_final, (("band", 0),), node_count)
    near_node_pairs = project(layer_norm(near_final), node_pair_weight)
    node_local = own_sources - (band_index - 1) * node_count
    dec_query = project(own_grid, query_weight)
    dec_mix = slot_attention(dec_query, near_node_pairs, node_local, own_counts)
    dec_terms = jnp.dot(dec_mix, out_weight, preferred_element_type=jnp.float32)
    dec_update = lax.psum_scatter(
        dec_terms.astype(jnp.bfloat16), "head", scatter_dimension=0, tiled=True
    ).astype(jnp.float32)
    part_count = dec_update.shape[0]
    part_grid = lax.dynamic_slice_in_dim(
        grid_state, lax.axis_index("head") * part_count, part_count, 0
    )
    grid_next = (part_grid.astype(jnp.float32) + dec_update).astype(jnp.bfloat16)
    return (grid_next, hidden_final)


def solution(mesh):
    in_specs = (
        P("band", None),
        P("band", "head"),
        P("band", None),
        P("band"),
        P("band", None),
        P("band"),
        P(None, "head"),
        P(None, "head"),
        P(None, "head"),
        P("head", None),
        P(None, "head"),
        P(None, "head"),
        P(None, "head"),
        P("head", None),
        P(None, "head"),
        P("head", None),
        P(None, "head"),
        P(None, "head"),
        P(None, "head"),
        P("head", None),
    )
    out_specs = (P(("band", "head"), None), P("band", "head"))
    return jax.shard_map(local, mesh=mesh, in_specs=in_specs, out_specs=out_specs, check_vma=False)
```

profile of v0, /device:TPU:23, one launch (start us, length us, event | category | flops | bytes accessed | tf_op | source)
XLA Modules:
  0.0 1019.0 jit_solution(3701907884185238331)
XLA Ops:
  18.7 27.0 %collective-permute-done.1 = bf16[4096,100]{0,1:T(8,128)(2,1)S(1)} collective-permute-done((bf16[4096,100]{0,1:T(8,128)(2,1)}, bf16[4096,100]{0,1:T(8,128)(2,1)S(1)}, u32[]{:S(2)}, u32[]{:S(2)}) %collective-permute-start.1) | collective-permute-done | bytes 819232 | tf_op jit(solution)/shard_map/ppermute | solution.py:24
  47.5 13.1 %convolution_convert_fusion = bf16[12288,1024]{1,0:T(8,128)(2,1)} fusion(bf16[4096,100]{0,1:T(8,128)(2,1)S(1)} %collective-permute-done.1, bf16[4096,100]{0,1:T(8,128)(2,1)} %param.24, bf16[4096,100]{0,1:T(8,128)(2,1)S(1)} %collective-permute-done, bf16[100,512]{1,0:T(8,128)(2,1)} %param.31, bf16[100,512]{1,0:T(8,128)(2,1)} %param.30), kind=kOutput, calls=%fused_computation.26 | convolution fusion | flops 2536947712 | bytes 27828224 | tf_op jit(solution)/shard_map/dot_general | solution.py:39
  60.6 170.5 %gather_fusion = bf16[32768,1024]{1,0:T(8,128)(2,1)} fusion(bf16[12288,1024]{1,0:T(8,128)(2,1)} %convolution_convert_fusion, s32[32768]{0:T(1024)S(1)} %broadcast_clamp_fusion), kind=kCustom, calls=%fused_computation.4 | custom fusion | bytes 134348800 | tf_op jit(solution)/shard_map/jit(_take)/gather | solution.py:136
  231.1 89.0 %copy.39 = bf16[1024,32,1024]{0,2,1:T(8,128)(2,1)} copy(bf16[1024,32,1024]{2,1,0:T(8,128)(2,1)} %bitcast.10) | data formatting | bytes 134217728 | tf_op jit(solution)/shard_map/jit(_take)/gather | solution.py:136
  320.2 44.7 %broadcast_select_fusion = bf16[1024,32,1024]{0,2,1:T(8,128)(2,1)} fusion(bf16[1024,32,1024]{0,2,1:T(8,128)(2,1)} %copy.39, pred[1024,32]{0,1:T(8,128)(4,1)S(1)} %copy-done.9), kind=kLoop, calls=%fused_computation.25 | loop fusion | flops 33554432 | bytes 134250496 | tf_op jit(solution)/shard_map/jit(_take)/select_n | solution.py:136
  364.9 43.9 %fusion.112 = (bf16[1024,32,512]{0,2,1:T(8,128)(2,1)}, bf16[1024,32,512]{0,2,1:T(8,128)(2,1)}) fusion(bf16[1024,32,1024]{0,2,1:T(8,128)(2,1)} %broadcast_select_fusion), kind=kLoop, calls=%fused_computation.183 | loop fusion | bytes 134217728 | tf_op jit(solution)/shard_map/slice | solution.py:52
  416.3 11.7 %multiply_reduce_fusion.1 = f32[1024,8,32]{0,1,2:T(8,128)S(1)} fusion(f32[1024,8,64]{0,2,1:T(8,128)S(1)} %bitcast_convert_fusion, bf16[1024,32,512]{0,2,1:T(8,128)(2,1)} %get-tuple-element.123), kind=kLoop, calls=%fused_computation.24 | loop fusion | flops 50069504 | bytes 36700160
  429.8 12.5 %multiply_reduce_fusion = bf16[1024,8,64]{0,2,1:T(8,128)(2,1)S(1)} fusion(bf16[1024,8,32,64]{0,3,1,2:T(8,128)(2,1)} %bitcast.84, f32[1024,8,32]{0,1,2:T(8,128)S(1)} %copy.65), kind=kLoop, calls=%fused_computation.23 | loop fusion | flops 49807360 | bytes 35651584 | tf_op jit(solution)/shard_map/rhe,rehd->rhd/dot_general | solution.py:59
  445.0 12.3 %reduce-scatter.5.cloned.1.call-done = bf16[1024,512]{1,0:T(8,128)(2,1)} async-done(((bf16[1024,1024]{1,0:T(8,128)(2,1)}), bf16[1024,512]{1,0:T(8,128)(2,1)}) %reduce-scatter.5.cloned.1.call-update) | async-done | bytes 1048592 | tf_op jit(solution)/shard_map/reduce_scatter | solution.py:138
  459.9 11.9 %all-gather.7.cloned.1.call-done = bf16[1024,1024]{1,0:T(8,128)(2,1)} async-done(((bf16[1024,512]{1,0:T(8,128)(2,1)}), bf16[1024,1024]{1,0:T(8,128)(2,1)}) %all-gather.7.cloned.1.call-update) | async-done | bytes 2097168 | tf_op jit(solution)/shard_map/all_gather | solution.py:145
  494.0 39.7 %collective-permute-done.3 = bf16[560,1024]{1,0:T(8,128)(2,1)} collective-permute-done((bf16[560,1024]{1,0:T(8,128)(2,1)}, bf16[560,1024]{1,0:T(8,128)(2,1)}, u32[]{:S(2)}, u32[]{:S(2)}) %collective-permute-start.3) | collective-permute-done | bytes 1146912 | tf_op jit(solution)/shard_map/ppermute | solution.py:24
  539.6 89.0 %while.12 = (s32[]{:T(128)}, bf16[2,512,512]{2,1,0:T(8,128)(2,1)}, s32[2]{0:T(128)}, bf16[2144,1024]{1,0:T(8,128)(2,1)}, s32[]{:T(128)}, /*index=5*/bf16[1024,51...) while((s32[]{:T(128)}, bf16[2,512,512]{2,1,0:T(8,128)(2,1)}, ...), condition=%wide.region_8.9_spmd, body=%wide.region_6.8_spmd.sunk | while | flops 1762511744 | bytes 93068752 | solution.py:165
  557.3 13.6 %fusion.142 = (f32[8,512]{1,0:T(8,128)S(1)}, f32[8,512,1632]{1,2,0:T(8,128)}) fusion(pred[512,1632]{0,1:T(8,128)(4,1)S(1)} %fusion.141, bf16[512,8,64]{0,2,1:T(8,128)(2,1)S(1)} %bitcast.87, bf16[1632,8,64]{0,2,1:T(8,128)(2,1)} %bitcast.86), kind=kOutput, calls=%fused_computation.7.clone.1 | convolution fusion | flops 875687936 | bytes 29786112 | tf_op jit(solution)/shard_map/while/body/eval_jaxpr/qhd,shd->hqs/dot_general | solution.py:97
  570.9 11.9 %fusion.143 = bf16[8,64,512]{2,1,0:T(8,128)(2,1)S(1)} fusion(bf16[1632,8,64]{0,2,1:T(8,128)(2,1)S(1)} %bitcast.85, f32[8,512,1632]{1,2,0:T(8,128)} %get-tuple-element.189, f32[8,512]{1,0:T(8,128)S(1)} %get-tuple-element.190, pred[512,1632]{0,1:T(8,128)(4,1)S(1)} %fusion.141), kind=kOutput, calls=%fused_computation.12.clone.1 | convolution fusion | flops 882638848 | bytes 29786112 | tf_op jit(solution)/shard_map/while/body/eval_jaxpr/hqs,shd->qhd/dot_general | solution.py:101
  601.8 13.6 %fusion.142 = (f32[8,512]{1,0:T(8,128)S(1)}, f32[8,512,1632]{1,2,0:T(8,128)}) fusion(pred[512,1632]{0,1:T(8,128)(4,1)S(1)} %fusion.141, bf16[512,8,64]{0,2,1:T(8,128)(2,1)S(1)} %bitcast.87, bf16[1632,8,64]{0,2,1:T(8,128)(2,1)} %bitcast.86), kind=kOutput, calls=%fused_computation.7.clone.1 | convolution fusion | flops 875687936 | bytes 29786112 | tf_op jit(solution)/shard_map/while/body/eval_jaxpr/qhd,shd->hqs/dot_general | solution.py:97
  615.4 11.9 %fusion.143 = bf16[8,64,512]{2,1,0:T(8,128)(2,1)S(1)} fusion(bf16[1632,8,64]{0,2,1:T(8,128)(2,1)S(1)} %bitcast.85, f32[8,512,1632]{1,2,0:T(8,128)} %get-tuple-element.189, f32[8,512]{1,0:T(8,128)S(1)} %get-tuple-element.190, pred[512,1632]{0,1:T(8,128)(4,1)S(1)} %fusion.141), kind=kOutput, calls=%fused_computation.12.clone.1 | convolution fusion | flops 882638848 | bytes 29786112 | tf_op jit(solution)/shard_map/while/body/eval_jaxpr/hqs,shd->qhd/dot_general | solution.py:101
  632.9 11.7 %reduce-scatter.7.cloned.1.call-done = bf16[1024,512]{1,0:T(8,128)(2,1)} async-done(((bf16[1024,1024]{1,0:T(8,128)(2,1)}), bf16[1024,512]{1,0:T(8,128)(2,1)}) %reduce-scatter.7.cloned.1.call-update) | async-done | bytes 1048592 | tf_op jit(solution)/shard_map/reduce_scatter | solution.py:166
  647.3 11.7 %all-gather.9.cloned.1.call-done = bf16[1024,1024]{1,0:T(8,128)(2,1)} async-done(((bf16[1024,512]{1,0:T(8,128)(2,1)}), bf16[1024,1024]{1,0:T(8,128)(2,1)}) %all-gather.9.cloned.1.call-update) | async-done | bytes 2097168 | tf_op jit(solution)/shard_map/all_gather | solution.py:173
  663.2 14.5 %fusion.70 = bf16[1024,1024]{1,0:T(8,128)(2,1)} fusion(bf16[2048,1024]{1,0:T(8,128)(2,1)} %param.39, bf16[1024,2048]{1,0:T(8,128)(2,1)} %param.38, bf16[1024,1024]{1,0:T(8,128)(2,1)} %all-gather.9.cloned.1.call-done, f32[1024]{0:T(1024)S(1)} %add_rsqrt_fusion.1, f32[1024]{0:T(1024)S(1)} %broadcast_multiply_fusion.1), kind=kOutput, calls=%fused_computation.113 | convolution fusion | flops 8614051840 | bytes 12591104 | tf_op jit(solution)/shard_map/dot_general | solution.py:179
  677.9 10.9 %reduce-scatter.9.cloned.1.call-done = bf16[1024,512]{1,0:T(8,128)(2,1)} async-done(((bf16[1024,1024]{1,0:T(8,128)(2,1)}), bf16[1024,512]{1,0:T(8,128)(2,1)}) %reduce-scatter.9.cloned.1.call-update) | async-done | bytes 1048592 | tf_op jit(solution)/shard_map/reduce_scatter | solution.py:178
  691.4 11.8 %all-gather.11.cloned.1.call-done = bf16[1024,1024]{1,0:T(8,128)(2,1)} async-done(((bf16[1024,512]{1,0:T(8,128)(2,1)}), bf16[1024,1024]{1,0:T(8,128)(2,1)}) %all-gather.11.cloned.1.call-update) | async-done | bytes 2097168 | tf_op jit(solution)/shard_map/all_gather | solution.py:185
  710.8 84.7 %collective-permute-done.5 = bf16[1024,1024]{1,0:T(8,128)(2,1)S(1)} collective-permute-done((bf16[1024,1024]{1,0:T(8,128)(2,1)}, bf16[1024,1024]{1,0:T(8,128)(2,1)S(1)}, u32[]{:S(2)}, u32[]{:S(2)}) %collective-permute-start.5) | collective-permute-done | bytes 2097184 | tf_op jit(solution)/shard_map/ppermute | solution.py:24
  806.2 15.6 %fusion.30 = bf16[3072,1024]{1,0:T(8,128)(2,1)} fusion(f32[3072]{0:T(1024)S(1)} %add_rsqrt_fusion, f32[3072]{0:T(1024)S(1)} %broadcast_multiply_fusion, bf16[1024,512]{1,0:T(8,128)(2,1)S(1)} %copy-done.15, bf16[1024,512]{1,0:T(8,128)(2,1)S(1)} %copy-done.16, bf16[1024,1024]{1,0:T(8,128)(2,1)S(1)} %collective-permute-done.5, ...), kind=kOutput, calls=%fused_computation.67 | convolution fusion | flops 6478102528 | bytes 14704640 | tf_op jit(solution)/shard_map/dot_general | solution.py:39
  821.7 24.4 %gather_fusion.4 = bf16[4096,1024]{1,0:T(8,128)(2,1)} fusion(bf16[3072,1024]{1,0:T(8,128)(2,1)} %fusion.30, s32[4096]{0:T(1024)S(1)} %fusion.100), kind=kCustom, calls=%fused_computation.3.clone | custom fusion | bytes 16793600 | tf_op jit(solution)/shard_map/jit(_take)/gather | solution.py:71
  846.2 11.2 %copy.46 = bf16[4096,1024]{0,1:T(8,128)(2,1)} copy(bf16[4096,1024]{1,0:T(8,128)(2,1)} %gather_fusion.4) | data formatting | bytes 16777216 | tf_op jit(solution)/shard_map/jit(_take)/gather | solution.py:71
  857.4 24.5 %gather_fusion.3 = bf16[4096,1024]{1,0:T(8,128)(2,1)} fusion(bf16[3072,1024]{1,0:T(8,128)(2,1)} %fusion.30, s32[4096]{0:T(1024)S(1)} %fusion.99), kind=kCustom, calls=%fused_computation.2.clone | custom fusion | bytes 16793600 | tf_op jit(solution)/shard_map/jit(_take)/gather | solution.py:71
  881.9 11.7 %copy.45 = bf16[4096,1024]{0,1:T(8,128)(2,1)} copy(bf16[4096,1024]{1,0:T(8,128)(2,1)} %gather_fusion.3) | data formatting | bytes 16777216 | tf_op jit(solution)/shard_map/jit(_take)/gather | solution.py:71
  893.6 24.4 %gather_fusion.2 = bf16[4096,1024]{1,0:T(8,128)(2,1)} fusion(bf16[3072,1024]{1,0:T(8,128)(2,1)} %fusion.30, s32[4096]{0:T(1024)S(1)} %fusion.98), kind=kCustom, calls=%fused_computation.1.clone | custom fusion | bytes 16793600 | tf_op jit(solution)/shard_map/jit(_take)/gather | solution.py:71
  918.0 11.2 %copy.44 = bf16[4096,1024]{0,1:T(8,128)(2,1)} copy(bf16[4096,1024]{1,0:T(8,128)(2,1)} %gather_fusion.2) | data formatting | bytes 16777216 | tf_op jit(solution)/shard_map/jit(_take)/gather | solution.py:71
  929.2 24.4 %gather_fusion.1 = bf16[4096,1024]{1,0:T(8,128)(2,1)} fusion(bf16[3072,1024]{1,0:T(8,128)(2,1)} %fusion.30, s32[4096]{0:T(1024)S(1)} %fusion.97), kind=kCustom, calls=%fused_computation.clone | custom fusion | bytes 16793600 | tf_op jit(solution)/shard_map/jit(_take)/gather | solution.py:71
  953.6 12.0 %copy.43 = bf16[4096,1024]{0,1:T(8,128)(2,1)} copy(bf16[4096,1024]{1,0:T(8,128)(2,1)} %gather_fusion.1) | data formatting | bytes 16777216 | tf_op jit(solution)/shard_map/jit(_take)/gather | solution.py:71
  999.4 10.4 %reduce-scatter.11.cloned.1.call-done = bf16[2048,100]{0,1:T(8,128)(2,1)} async-done(((bf16[4096,100]{0,1:T(8,128)(2,1)}), bf16[2048,100]{0,1:T(8,128)(2,1)}) %reduce-scatter.11.cloned.1.call-update) | async-done | bytes 409616 | tf_op jit(solution)/shard_map/reduce_scatter | solution.py:200
  (151 shorter events, 154.4 us)
Async XLA Ops:
  7.2 435.1 %copy-start = (bf16[512,1024]{1,0:T(8,128)(2,1)S(1)}, bf16[512,1024]{1,0:T(8,128)(2,1)}, u32[]{:S(2)}) copy-start(bf16[512,1024]{1,0:T(8,128)(2,1)} %param.33) | copy-start | bytes 3145732
  7.2 401.7 %all-gather.5.cloned.1.call-start = ((), (), s32[]{:S(2)}) async-start(), calls=%async_computation.4 | async-start | bytes 3145728 | tf_op jit(solution)/shard_map/all_gather | solution.py:133
  7.2 38.5 %collective-permute-start.1 = (bf16[4096,100]{0,1:T(8,128)(2,1)}, bf16[4096,100]{0,1:T(8,128)(2,1)S(1)}, u32[]{:S(2)}, u32[]{:S(2)}) collective-permute-start(bf16[4096,100]{0,1:T(8,128)(2,1)} %param.24), channel_id=1, source_target_pairs={{2,0},{4,2},{6,4},{8,6},{10,8},{12,10},{14,12},{16,14},{18,16},{20... | collective-permute-start | bytes 2457608 | tf_op jit(solution)/shard_map/ppermute | solution.py:24
  9.5 37.9 %collective-permute-start = (bf16[4096,100]{0,1:T(8,128)(2,1)}, bf16[4096,100]{0,1:T(8,128)(2,1)S(1)}, u32[]{:S(2)}, u32[]{:S(2)}) collective-permute-start(bf16[4096,100]{0,1:T(8,128)(2,1)} %param.24), channel_id=1, source_target_pairs={{0,2},{2,4},{4,6},{6,8},{8,10},{10,12},{12,14},{14,16},{16,18},{18... | collective-permute-start | bytes 2457608 | tf_op jit(solution)/shard_map/ppermute | solution.py:22
  14.5 442.8 %reduce-scatter.5.cloned.1.call-start = ((), (), s32[]{:S(2)}) async-start(), calls=%async_computation.5 | async-start | bytes 3145728 | tf_op jit(solution)/shard_map/reduce_scatter | solution.py:138
  231.1 89.0 %copy-start.9 = (pred[1024,32]{0,1:T(8,128)(4,1)S(1)}, pred[1024,32]{0,1:T(8,128)(4,1)}, u32[]{:S(2)}) copy-start(pred[1024,32]{0,1:T(8,128)(4,1)} %compare_and_fusion) | copy-start | bytes 98308
  364.9 48.2 %copy-start.14 = (bf16[1024,512]{1,0:T(8,128)(2,1)S(1)}, bf16[1024,512]{1,0:T(8,128)(2,1)}, u32[]{:S(2)}) copy-start(bf16[1024,512]{1,0:T(8,128)(2,1)} %param.32) | copy-start | bytes 3145732
  416.3 11.8 %copy-start.12 = (pred[1024,32]{0,1:T(8,128)(4,1)S(1)}, pred[1024,32]{0,1:T(8,128)(4,1)}, u32[]{:S(2)}) copy-start(pred[1024,32]{0,1:T(8,128)(4,1)} %iota_compare_fusion) | copy-start | bytes 98308
  442.3 15.0 %copy-start.7 = (bf16[1024,512]{1,0:T(8,128)(2,1)S(1)}, bf16[1024,512]{1,0:T(8,128)(2,1)}, u32[]{:S(2)}) copy-start(bf16[1024,512]{1,0:T(8,128)(2,1)} %param.25) | copy-start | bytes 3145732
  445.0 26.8 %all-gather.7.cloned.1.call-start = ((), (), s32[]{:S(2)}) async-start(), calls=%async_computation.6 | async-start | bytes 3145728 | tf_op jit(solution)/shard_map/all_gather | solution.py:145
  459.9 184.7 %reduce-scatter.7.cloned.1.call-start = ((), (), s32[]{:S(2)}) async-start(), calls=%async_computation.7 | async-start | bytes 3145728 | tf_op jit(solution)/shard_map/reduce_scatter | solution.py:166
  482.2 51.5 %collective-permute-start.3 = (bf16[560,1024]{1,0:T(8,128)(2,1)}, bf16[560,1024]{1,0:T(8,128)(2,1)}, u32[]{:S(2)}, u32[]{:S(2)}) collective-permute-start(bf16[560,1024]{1,0:T(8,128)(2,1)} %get-tuple-element.126), channel_id=1, source_target_pairs={{2,0},{4,2},{6,4},{8,6},{10,8},{12,10},{14,12},{16,14},{18,16},{20... | collective-permute-start | bytes 3440648 | tf_op jit(solution)/shard_map/ppermute | solution.py:24
  484.4 51.2 %collective-permute-start.2 = (bf16[560,1024]{1,0:T(8,128)(2,1)}, bf16[560,1024]{1,0:T(8,128)(2,1)}, u32[]{:S(2)}, u32[]{:S(2)}) collective-permute-start(bf16[560,1024]{1,0:T(8,128)(2,1)} %get-tuple-element.125), channel_id=1, source_target_pairs={{0,2},{2,4},{4,6},{6,8},{8,10},{10,12},{12,14},{14,16},{16,18},{18... | collective-permute-start | bytes 3440648 | tf_op jit(solution)/shard_map/ppermute | solution.py:22
  557.3 13.6 %copy-start.2 = (bf16[1632,512]{0,1:T(8,128)(2,1)S(1)}, bf16[1632,512]{0,1:T(8,128)(2,1)}, u32[]{:S(2)}) copy-start(bf16[1632,512]{0,1:T(8,128)(2,1)} %copy.81) | copy-start | bytes 5013508 | tf_op jit(solution)/shard_map/while
  570.9 12.2 %copy-start.17 = (bf16[2,512,512]{2,1,0:T(8,128)(2,1)S(1)}, bf16[2,512,512]{2,1,0:T(8,128)(2,1)}, u32[]{:S(2)}) copy-start(bf16[2,512,512]{2,1,0:T(8,128)(2,1)} %get-tuple-element.204) | copy-start | bytes 3145732 | tf_op jit(solution)/shard_map/while
  601.8 13.6 %copy-start.2 = (bf16[1632,512]{0,1:T(8,128)(2,1)S(1)}, bf16[1632,512]{0,1:T(8,128)(2,1)}, u32[]{:S(2)}) copy-start(bf16[1632,512]{0,1:T(8,128)(2,1)} %copy.81) | copy-start | bytes 5013508 | tf_op jit(solution)/shard_map/while
  615.4 12.2 %copy-start.17 = (bf16[2,512,512]{2,1,0:T(8,128)(2,1)S(1)}, bf16[2,512,512]{2,1,0:T(8,128)(2,1)}, u32[]{:S(2)}) copy-start(bf16[2,512,512]{2,1,0:T(8,128)(2,1)} %get-tuple-element.204) | copy-start | bytes 3145732 | tf_op jit(solution)/shard_map/while
  628.6 16.0 %copy-start.4 = (bf16[1024,512]{1,0:T(8,128)(2,1)S(1)}, bf16[1024,512]{1,0:T(8,128)(2,1)}, u32[]{:S(2)}) copy-start(bf16[1024,512]{1,0:T(8,128)(2,1)} %add_convert_fusion.2) | copy-start | bytes 3145732
  632.8 26.2 %all-gather.9.cloned.1.call-start = ((), (), s32[]{:S(2)}) async-start(), calls=%async_computation.8 | async-start | bytes 3145728 | tf_op jit(solution)/shard_map/all_gather | solution.py:173
  647.1 41.7 %reduce-scatter.9.cloned.1.call-start = ((), (), s32[]{:S(2)}) async-start(), calls=%async_computation.9 | async-start | bytes 3145728 | tf_op jit(solution)/shard_map/reduce_scatter | solution.py:178
  663.2 25.5 %copy-start.5 = (bf16[1024,512]{1,0:T(8,128)(2,1)S(1)}, bf16[1024,512]{1,0:T(8,128)(2,1)}, u32[]{:S(2)}) copy-start(bf16[1024,512]{1,0:T(8,128)(2,1)} %add_convert_fusion.1) | copy-start | bytes 3145732
  677.8 13.5 %copy-start.11 = (s32[4096,4]{0,1:T(4,128)S(1)}, s32[4096,4]{0,1:T(4,128)}, u32[]{:S(2)}) copy-start(s32[4096,4]{0,1:T(4,128)} %param.28) | copy-start | bytes 196612
  677.8 33.0 %copy-start.13 = (s32[4096]{0:T(1024)S(1)}, s32[4096]{0:T(1024)}, u32[]{:S(2)}) copy-start(s32[4096]{0:T(1024)} %param.29) | copy-start | bytes 49156
  677.8 25.4 %all-gather.11.cloned.1.call-start = ((), (), s32[]{:S(2)}) async-start(), calls=%async_computation.10 | async-start | bytes 3145728 | tf_op jit(solution)/shard_map/all_gather | solution.py:185
  691.3 318.6 %reduce-scatter.11.cloned.1.call-start = ((), (), s32[]{:S(2)}) async-start(), calls=%async_computation.11 | async-start | bytes 1277952 | tf_op jit(solution)/shard_map/reduce_scatter | solution.py:200
  703.2 97.8 %copy-start.6 = (bf16[1024,1024]{1,0:T(8,128)(2,1)S(1)}, bf16[1024,1024]{1,0:T(8,128)(2,1)}, u32[]{:S(2)}) copy-start(bf16[1024,1024]{1,0:T(8,128)(2,1)} %all-gather.11.cloned.1.call-done) | copy-start | bytes 6291460
  703.2 92.4 %collective-permute-start.5 = (bf16[1024,1024]{1,0:T(8,128)(2,1)}, bf16[1024,1024]{1,0:T(8,128)(2,1)S(1)}, u32[]{:S(2)}, u32[]{:S(2)}) collective-permute-start(bf16[1024,1024]{1,0:T(8,128)(2,1)} %all-gather.11.cloned.1.call-done), channel_id=1, source_target_pairs={{2,0},{4,2},{6,4},{8,6},{10,8},{12,10},{14,12},{16,14},{18,16},{20... | collective-permute-start | bytes 6291464 | tf_op jit(solution)/shard_map/ppermute | solution.py:24
  705.5 91.9 %collective-permute-start.4 = (bf16[1024,1024]{1,0:T(8,128)(2,1)}, bf16[1024,1024]{1,0:T(8,128)(2,1)S(1)}, u32[]{:S(2)}, u32[]{:S(2)}) collective-permute-start(bf16[1024,1024]{1,0:T(8,128)(2,1)} %all-gather.11.cloned.1.call-done), channel_id=1, source_target_pairs={{0,2},{2,4},{4,6},{6,8},{8,10},{10,12},{12,14},{14,16},{16,18},{18... | collective-permute-start | bytes 6291464 | tf_op jit(solution)/shard_map/ppermute | solution.py:22
  965.6 8.3 copy-start.3
  973.9 9.8 copy-start.8
  973.9 9.8 copy-start.19
  991.0 20.7 %copy-start.1 = (bf16[512,1024]{1,0:T(8,128)(2,1)S(1)}, bf16[512,1024]{1,0:T(8,128)(2,1)}, u32[]{:S(2)}) copy-start(bf16[512,1024]{1,0:T(8,128)(2,1)} %param.33) | copy-start | bytes 3145732
  (5 other events, 19.1 us)
Sparse Core Ops, SparseCore 0:
  14.6 11.8 all-gather.4
  445.1 12.1 reduce-scatter.4
  460.0 11.7 all-gather.6
  633.0 11.5 reduce-scatter.6
  647.2 11.7 all-gather.8
  677.9 10.7 reduce-scatter.8
  691.4 11.7 all-gather.10
  999.5 10.2 reduce-scatter.10
where the time goes:
time: 1030 us; the launch traced here: 1020 us
  local copies, waits for them, and re-layouts  480 us (47%)
  waiting for transfers between devices  238 us (23%)
  other arithmetic  136 us (13%)
  matrix products  122 us (12%)
  starting transfers between devices  22.2 us (2%)
  between operations  15.1 us (1%)
    gather x2, local copies, waits for them, and re-layouts, local(): jnp.take(near_grid_pairs, encoder_sources, axis=0)  260 us
    ppermute x3, waiting for transfers between devices, with_halo(): lax.ppermute(head, axis, [((i + 1) % count, i) for i in range(ends)])  151 us
    gather x8, local copies, waits for them, and re-layouts, slot_attention(): picked = jnp.take(table, sources[:, slot], axis=0)  144 us
    dot_general x6, matrix products, project(): jnp.dot(matrix, weight, preferred_element_type=jnp.float32)  47.5 us
    select_n x2, other arithmetic, local(): jnp.take(near_grid_pairs, encoder_sources, axis=0)  45.6 us
    slice x1, local copies, waits for them, and re-layouts, edge_attention(): gathered[:, :, :full_width]  43.9 us
    dot_general x2, matrix products, window_attention(): jnp.einsum('qhd,shd->hqs', query_heads, key_heads, preferred_element_type...  27.2 us
    dot_general x2, matrix products, window_attention(): jnp.einsum('hqs,shd->qhd', weights, value_heads, preferred_element_type=j...  23.9 us
  transfers between devices with their start and end apart: 14, of which 13 were waited for; matrix products, arithmetic and copies ran while one was open for 36% of the time, Pallas kernels for 0%

commit v1 on v0

v1 whole, which is shorter than its diff:
```python
import functools
import math

import jax
import jax.numpy as jnp
from jax import lax
from jax.experimental import pallas as pl
from jax.experimental.pallas import tpu as pltpu
from jax.sharding import PartitionSpec as P

HALF_WIN = 560
HEAD_DIM = 64
LANES = 128
EPSILON = 1e-05
NEGATIVE = -1e30
SCALE = HEAD_DIM ** (-0.5) * math.log2(math.e)

bf16 = jnp.bfloat16
f32 = jnp.float32
ROWS_BY_ROWS = (((1,), (1,)), ((), ()))
VMEM = pl.BlockSpec(memory_space=pltpu.VMEM)
SMEM = pl.BlockSpec(memory_space=pltpu.SMEM)
BIG = pltpu.CompilerParams(vmem_limit_bytes=58 * 2**20)


def dot(a, b):
    return jnp.dot(a, b, preferred_element_type=f32)


def layer_norm(matrix):
    x = matrix.astype(f32)
    centred = x - jnp.mean(x, axis=-1, keepdims=True)
    variance = jnp.mean(centred * centred, axis=-1, keepdims=True)
    return (centred * lax.rsqrt(variance + EPSILON)).astype(bf16)


def low_lanes(shape):
    return lax.broadcasted_iota(jnp.int32, shape, len(shape) - 1) % LANES < HEAD_DIM


def query_kernel(state, wq_mine, wq_other, keys_mine, keys_other, out):
    normed = layer_norm(state[...])
    pairs = wq_mine.shape[1] // LANES
    for side, (wq, keys) in enumerate(((wq_mine, keys_mine), (wq_other, keys_other))):
        query = (dot(normed, wq[...])).astype(bf16)
        for pair in range(pairs):
            two = query[:, pair * LANES : (pair + 1) * LANES]
            low = low_lanes(two.shape)
            weight = keys[:, pair * LANES : (pair + 1) * LANES]
            for sub in range(2):
                one = jnp.where(low if sub == 0 else ~low, two, jnp.zeros_like(two))
                out[(side * pairs + pair) * 2 + sub] = (
                    lax.dot_general(one, weight, ROWS_BY_ROWS, preferred_element_type=f32) * SCALE
                )


GROUP = 8
CHAINS = 4


def encoder_kernel(
    info, sources, counts, query, own, prev_mine, prev_other, next_mine, next_other,
    values_mine, values_other, out_mine, out_other, state,
    result, table, *scratch,
):
    picked, mix = scratch[:-1], scratch[-1]
    core = info[0]
    grid_count, width = own.shape
    half = prev_mine.shape[0]
    heads, rows, _ = query.shape
    slots = sources.shape[0] // rows
    span = GROUP * slots
    table[...] = jnp.zeros_like(table)

    def fill(start, ref):
        table[pl.ds(pl.multiple_of(start, 8), ref.shape[0]), :width] = ref[...].astype(f32)

    fill(core * half, prev_mine)
    fill((1 - core) * half, prev_other)
    fill(grid_count, own)
    fill(2 * grid_count + core * half, next_mine)
    fill(2 * grid_count + (1 - core) * half, next_other)

    node = lax.broadcasted_iota(jnp.int32, (GROUP, span), 0)
    slot = lax.broadcasted_iota(jnp.int32, (GROUP, span), 1) - node * slots

    def step(index, carry):
        groups = [index * CHAINS + chain for chain in range(CHAINS)]
        starts = [pl.multiple_of(group * GROUP, GROUP) for group in groups]
        for group, rows_ref in zip(groups, picked):
            for s in range(span):
                rows_ref[s : s + 1, :] = table[pl.ds(sources[group * span + s], 1), :]
        grids = [ref[...].astype(bf16) for ref in picked]
        live = [(slot >= 0) & (slot < counts[pl.ds(start, GROUP), :]) for start in starts]
        queries = [
            query[:, pl.ds(start, GROUP), :].reshape(heads * GROUP, LANES).astype(bf16)
            for start in starts
        ]
        scores = [
            lax.dot_general(q, g, ROWS_BY_ROWS, preferred_element_type=f32)
            for q, g in zip(queries, grids)
        ]
        powers = [
            jnp.where(on[None], jnp.exp2(s.reshape(heads, GROUP, span)), 0.0).reshape(
                heads * GROUP, span
            )
            for s, on in zip(scores, live)
        ]
        weights = [(p * (1.0 / jnp.sum(p, -1, keepdims=True))).astype(bf16) for p in powers]
        mixed = [dot(w, g) for w, g in zip(weights, grids)]
        for start, m in zip(starts, mixed):
            mix[:, pl.ds(start, GROUP), :] = m.reshape(heads, GROUP, LANES)
        return carry

    lax.fori_loop(0, rows // (GROUP * CHAINS), step, 0)

    pairs = values_mine.shape[1] // LANES
    total = state[...].astype(f32)
    for side, (values, out) in enumerate(((values_mine, out_mine), (values_other, out_other))):
        parts = []
        for pair in range(pairs):
            weight = values[:, pair * LANES : (pair + 1) * LANES]
            low = low_lanes(weight.shape)
            both = jnp.concatenate(
                [jnp.where(low, weight, 0.0).astype(bf16), jnp.where(low, 0.0, weight).astype(bf16)], 0
            )
            head = (side * pairs + pair) * 2
            two = jnp.concatenate([mix[head].astype(bf16), mix[head + 1].astype(bf16)], 1)
            parts.append(dot(two, both).astype(bf16))
        total = total + dot(jnp.concatenate(parts, 1), out[...])
    result[...] = total.astype(bf16)


def window_kernel(
    info, own, partner, far, far_more, near,
    wq_mine, wq_other, wk_mine, wk_other, wv_mine, wv_other,
    result, query, key, value, bias,
):
    core, first, total = info[0], info[1], info[2]
    rows = own.shape[0]
    reach = HALF_WIN
    more = far_more.shape[0]
    lead = core == 0
    span_all = key.shape[1]
    pairs = wq_mine.shape[1] // LANES

    def put(target, start, block):
        for pair in range(pairs):
            target[0][target[1] * pairs + pair, pl.ds(pl.multiple_of(start, 16), block.shape[0]), :] = (
                block[:, pair * LANES : (pair + 1) * LANES]
            )

    segments = (
        (own, reach),
        (partner, jnp.where(lead, reach + rows, reach - rows)),
        (far, jnp.where(lead, more, reach + rows)),
        (far_more, jnp.where(lead, 0, reach + 2 * rows)),
        (near, jnp.where(lead, reach + 2 * rows, 0)),
    )
    for ref, start in segments:
        normed = layer_norm(ref[...])
        for side, (wk, wv) in enumerate(((wk_mine, wv_mine), (wk_other, wv_other))):
            put((key, side), start, dot(normed, wk[...]).astype(bf16))
            put((value, side), start, dot(normed, wv[...]).astype(bf16))
        if ref is own:
            for side, wq in enumerate((wq_mine, wq_other)):
                put((query, side), 0, (dot(normed, wq[...]).astype(bf16).astype(f32) * SCALE).astype(bf16))

    blocks, block, span = bias.shape
    for b in range(blocks):
        row = lax.broadcasted_iota(jnp.int32, (block, span), 0)
        col = lax.broadcasted_iota(jnp.int32, (block, span), 1)
        place = first - reach + b * block + col
        live = (col >= row) & (col <= row + 2 * reach) & (place >= 0) & (place < total)
        bias[b] = jnp.where(live, 0.0, NEGATIVE)

    def step(pair, carry):
        for b in range(blocks):
            k = key[pair, pl.ds(b * block, span), :]
            v = value[pair, pl.ds(b * block, span), :]
            q = query[pair, pl.ds(b * block, block), :]
            low = low_lanes(q.shape)
            mixes = []
            for sub in range(2):
                one = jnp.where(low if sub == 0 else ~low, q, jnp.zeros_like(q))
                s = lax.dot_general(one, k, ROWS_BY_ROWS, preferred_element_type=f32)
                p = jnp.exp2(s + bias[b])
                w = (p * (1.0 / jnp.sum(p, -1, keepdims=True))).astype(bf16)
                mixes.append(dot(w, v))
            result[pair, pl.ds(b * block, block), :] = jnp.where(low, mixes[0], mixes[1]).astype(bf16)
        return carry

    lax.fori_loop(0, 2 * pairs, step, 0)


def feed_kernel(mix, mid, wo_mine, wo_other, up_mine, up_other, down_mine, down_other, result, att, normed, total):
    index = pl.program_id(0)
    half = pl.num_programs(0) // 2

    @pl.when(index == 0)
    def _():
        pairs = wo_mine.shape[0] // LANES
        acc = mid[...].astype(f32)
        for side, wo in enumerate((wo_mine, wo_other)):
            block = jnp.concatenate([mix[side * pairs + pair] for pair in range(pairs)], 1)
            acc = acc + dot(block, wo[...])
        att[...] = acc.astype(bf16)
        normed[...] = layer_norm(att[...])
        total[...] = att[...].astype(f32)

    def part(up, down):
        inner = jax.nn.gelu(dot(normed[...], up[...]), approximate=True).astype(bf16)
        total[...] += dot(inner, down[...])

    @pl.when(index < half)
    def _():
        part(up_mine, down_mine)

    @pl.when(index >= half)
    def _():
        part(up_other, down_other)

    @pl.when(index == 2 * half - 1)
    def _():
        result[...] = total[...].astype(bf16)


POINTS = 32


def decoder_kernel(
    info, sources, counts, grid, own, partner, prev_mine, prev_other, next_mine, next_other,
    wq_mine, wq_other, wk_mine, wk_other, wv_mine, wv_other, wo_mine, wo_other,
    result, table, query, product,
):
    core = info[0]
    rows = own.shape[0]
    nodes = 2 * rows
    parts = wk_mine.shape[1] // LANES
    deep = 2 * parts
    points = grid.shape[0]
    slots = sources.shape[0] // points
    piece = rows // 2

    starts = (
        (prev_mine, core * rows),
        (prev_other, (1 - core) * rows),
        (own, nodes + core * rows),
        (partner, nodes + (1 - core) * rows),
        (next_mine, 2 * nodes + core * rows),
        (next_other, 2 * nodes + (1 - core) * rows),
    )
    for ref, start in starts:

        def fill(index, carry, ref=ref, start=start):
            normed = layer_norm(ref[pl.ds(pl.multiple_of(index * piece, piece), piece), :])
            base = (start + index * piece) * (2 * deep)
            for group, weight in enumerate((wk_mine, wk_other, wv_mine, wv_other)):
                block = dot(normed, weight[...])
                for part in range(parts):
                    table[pl.ds(base + group * parts + part, piece, stride=2 * deep), :] = block[
                        :, part * LANES : (part + 1) * LANES
                    ]
            return carry

        lax.fori_loop(0, rows // piece, fill, 0)

    def ask(index, carry):
        own_grid = grid[pl.ds(pl.multiple_of(index * piece, piece), piece), :]
        for group, weight in enumerate((wq_mine, wq_other)):
            block = dot(own_grid, weight[...]) * SCALE
            for part in range(parts):
                query[pl.ds(index * (piece * deep) + group * parts + part, piece, stride=deep), :] = block[
                    :, part * LANES : (part + 1) * LANES
                ]
        return carry

    lax.fori_loop(0, points // piece, ask, 0)

    ones_row = lax.broadcasted_iota(jnp.int32, (2 * LANES, 2 * LANES), 0) // HEAD_DIM
    ones_col = lax.broadcasted_iota(jnp.int32, (2 * LANES, 2 * LANES), 1) // HEAD_DIM
    same_head = jnp.where(ones_row == ones_col, 1.0, 0.0).astype(bf16)
    half = POINTS * deep // 2

    def step(index, carry):
        first = index * POINTS
        for point in range(0, POINTS, 2):
            q = [query[pl.ds(pl.multiple_of((first + point + t) * deep, deep), deep), :] for t in range(2)]
            for slot in range(slots):
                terms = []
                for t in range(2):
                    at = pl.multiple_of(sources[(first + point + t) * slots + slot], deep)
                    terms.append(table[pl.ds(at, deep), :] * q[t])
                product[slot, point * deep : (point + 2) * deep, :] = jnp.concatenate(terms, 0).astype(bf16)
        live = jnp.concatenate(
            [jnp.full((deep, LANES), counts[first + point], jnp.int32) for point in range(POINTS)], 0
        )
        powers = []
        for slot in range(slots):
            wide = jnp.concatenate([product[slot, :half, :], product[slot, half:, :]], 1)
            score = dot(wide, same_head)
            score = jnp.concatenate([score[:, :LANES], score[:, LANES:]], 0)
            powers.append(jnp.where(live > slot, jnp.exp2(score), 0.0))
        total = powers[0]
        for slot in range(1, slots):
            total = total + powers[slot]
        inverse = 1.0 / total
        weights = [p * inverse for p in powers]
        for point in range(POINTS):
            mixed = None
            for slot in range(slots):
                at = pl.multiple_of(sources[(first + point) * slots + slot], deep)
                term = weights[slot][point * deep : (point + 1) * deep, :] * table[pl.ds(at + deep, deep), :]
                mixed = term if mixed is None else mixed + term
            query[pl.ds(pl.multiple_of((first + point) * deep, deep), deep), :] = mixed
        return carry

    lax.fori_loop(0, points // POINTS, step, 0)

    width = result.shape[1]

    def finish(index, carry):
        at = pl.ds(pl.multiple_of(index * piece, piece), piece)
        acc = None
        for group, weight in enumerate((wo_mine, wo_other)):
            block = jnp.concatenate(
                [
                    query[pl.ds(index * (piece * deep) + group * parts + part, piece, stride=deep), :].astype(bf16)
                    for part in range(parts)
                ],
                1,
            )
            term = dot(block, weight[...])
            acc = term if acc is None else acc + term
        result[at, :] = (grid[at, :].astype(f32)[:, :width] + acc[:, :width]).astype(bf16)
        return carry

    lax.fori_loop(0, points // piece, finish, 0)


def local(
    grid_state,
    hidden_state,
    encoder_sources,
    encoder_counts,
    decoder_sources,
    decoder_counts,
    encoder_keys,
    encoder_values,
    encoder_query,
    encoder_output,
    window_query,
    window_keys,
    window_values,
    window_output,
    feed_up,
    feed_down,
    decoder_query,
    decoder_keys,
    decoder_values,
    decoder_output,
):
    bands, band, core = lax.axis_size("band"), lax.axis_index("band"), lax.axis_index("head")
    cores = lax.axis_size("head")
    grid_count, width = grid_state.shape
    nodes, channels = hidden_state.shape
    rows, points = nodes // cores, grid_count // cores
    full = channels * cores
    heads = full // HEAD_DIM

    def swap(x):
        return lax.ppermute(x, "head", [(0, 1), (1, 0)])

    def onward(x):
        return lax.ppermute(x, "band", [(i, i + 1) for i in range(bands - 1)])

    def backward(x):
        return lax.ppermute(x, "band", [(i + 1, i) for i in range(bands - 1)])

    def my_part(x, size):
        return lax.dynamic_slice_in_dim(x, core * size, size, 0)

    def wide(x):
        return jnp.pad(x, ((0, LANES - x.shape[0]), (0, 0)))

    info = jnp.stack([core, band * nodes + core * rows, bands * nodes]).astype(jnp.int32)

    my_grid = my_part(grid_state, points)
    prev_mine, next_mine = onward(my_grid), backward(my_grid)
    prev_other, next_other = swap(prev_mine), swap(next_mine)

    kept = my_part(hidden_state, rows)
    got = swap(lax.dynamic_slice_in_dim(hidden_state, (1 - core) * rows, rows, 0))
    state = jnp.where(
        core == 0, jnp.concatenate([kept, got], 1), jnp.concatenate([got, kept], 1)
    )

    ek_mine, ev_mine, dq_mine = wide(encoder_keys), wide(encoder_values), wide(decoder_query)
    do_mine = jnp.pad(decoder_output, ((0, 0), (0, LANES - width)))

    query = pl.pallas_call(
        query_kernel,
        out_shape=jax.ShapeDtypeStruct((heads, rows, LANES), f32),
        in_specs=[VMEM] * 5,
        out_specs=VMEM,
        compiler_params=BIG,
        name="queries",
    )(state, encoder_query, swap(encoder_query), ek_mine, swap(ek_mine))

    my_sources = my_part(encoder_sources, rows).reshape(-1)
    my_counts = my_part(encoder_counts, rows)[:, None]
    slots = encoder_sources.shape[1]
    mid = pl.pallas_call(
        encoder_kernel,
        out_shape=jax.ShapeDtypeStruct((rows, full), bf16),
        in_specs=[SMEM, SMEM] + [VMEM] * 12,
        out_specs=VMEM,
        scratch_shapes=[pltpu.VMEM((3 * grid_count, LANES), f32)]
        + [pltpu.VMEM((GROUP * slots, LANES), f32) for _ in range(CHAINS)]
        + [pltpu.VMEM((heads, rows, LANES), f32)],
        compiler_params=BIG,
        name="encoder",
    )(
        info, my_sources, my_counts, query, grid_state, prev_mine, prev_other, next_mine, next_other,
        ev_mine, swap(ev_mine), encoder_output, swap(encoder_output), state,
    )

    more = HALF_WIN - rows
    partner = swap(mid)
    facing = [(2 * i + 1, 2 * i + 2) for i in range(bands - 1)]
    far = lax.ppermute(mid, ("band", "head"), facing + [(b, a) for a, b in facing])
    edge = jnp.where(core == 0, mid[rows - more :], mid[:more])
    far_more = lax.ppermute(
        edge,
        ("band", "head"),
        [(2 * i, 2 * i + 2) for i in range(bands - 1)] + [(2 * i + 3, 2 * i + 1) for i in range(bands - 1)],
    )
    near = swap(jnp.where(core == 0, far[rows - more :], far[:more]))

    block = rows // 2
    span = block + 2 * HALF_WIN
    keys_all = rows + 2 * HALF_WIN
    pairs = full // LANES
    mix = pl.pallas_call(
        window_kernel,
        out_shape=jax.ShapeDtypeStruct((pairs, rows, LANES), bf16),
        in_specs=[SMEM] + [VMEM] * 11,
        out_specs=VMEM,
        scratch_shapes=[
            pltpu.VMEM((pairs, rows, LANES), bf16),
            pltpu.VMEM((pairs, keys_all, LANES), bf16),
            pltpu.VMEM((pairs, keys_all, LANES), bf16),
            pltpu.VMEM((rows // block, block, span), f32),
        ],
        compiler_params=BIG,
        name="window",
    )(
        info, mid, partner, far, far_more, near,
        window_query, swap(window_query), window_keys, swap(window_keys), window_values, swap(window_values),
    )

    units = feed_up.shape[1]
    chunk = min(512, units)
    steps = units // chunk
    whole = lambda shape: pl.BlockSpec(shape, lambda i: (0,) * len(shape))
    final = pl.pallas_call(
        feed_kernel,
        grid=(2 * steps,),
        out_shape=jax.ShapeDtypeStruct((rows, full), bf16),
        in_specs=[
            whole((pairs, rows, LANES)),
            whole((rows, full)),
            whole((channels, full)),
            whole((channels, full)),
            pl.BlockSpec((full, chunk), lambda i: (0, jnp.minimum(i, steps - 1))),
            pl.BlockSpec((full, chunk), lambda i: (0, jnp.maximum(i - steps, 0))),
            pl.BlockSpec((chunk, full), lambda i: (jnp.minimum(i, steps - 1), 0)),
            pl.BlockSpec((chunk, full), lambda i: (jnp.maximum(i - steps, 0), 0)),
        ],
        out_specs=whole((rows, full)),
        scratch_shapes=[
            pltpu.VMEM((rows, full), bf16),
            pltpu.VMEM((rows, full), bf16),
            pltpu.VMEM((rows, full), f32),
        ],
        compiler_params=BIG,
        name="feed",
    )(
        mix, mid, window_output, swap(window_output), feed_up, swap(feed_up), feed_down, swap(feed_down),
    )

    final_partner = swap(final)
    before, after = onward(final), backward(final)
    before_other, after_other = swap(before), swap(after)
    columns = lax.dynamic_slice_in_dim(final, core * channels, channels, 1)
    partner_columns = lax.dynamic_slice_in_dim(final_partner, core * channels, channels, 1)
    hidden_final = jnp.where(
        core == 0,
        jnp.concatenate([columns, partner_columns], 0),
        jnp.concatenate([partner_columns, columns], 0),
    )

    deep = full // LANES
    dec_sources = ((my_part(decoder_sources, points) - (band - 1) * nodes) * (2 * deep)).reshape(-1)
    dec_counts = my_part(decoder_counts, points)
    dec_slots = decoder_sources.shape[1]
    grid_wide = jnp.pad(my_grid, ((0, 0), (0, LANES - width)))
    grid_next = pl.pallas_call(
        decoder_kernel,
        out_shape=jax.ShapeDtypeStruct((points, width), bf16),
        in_specs=[SMEM] * 3 + [VMEM] * 15,
        out_specs=VMEM,
        scratch_shapes=[
            pltpu.VMEM((3 * nodes * 2 * deep, LANES), f32),
            pltpu.VMEM((points * deep, LANES), f32),
            pltpu.VMEM((dec_slots, POINTS * deep, LANES), bf16),
        ],
        compiler_params=BIG,
        name="decoder",
    )(
        info, dec_sources, dec_counts, grid_wide, final, final_partner,
        before, before_other, after, after_other,
        dq_mine, swap(dq_mine), decoder_keys, swap(decoder_keys), decoder_values, swap(decoder_values),
        do_mine, swap(do_mine),
    )
    return (grid_next, hidden_final)


def solution(mesh):
    in_specs = (
        P("band", None),
        P("band", "head"),
        P("band", None),
        P("band"),
        P("band", None),
        P("band"),
        P(None, "head"),
        P(None, "head"),
        P(None, "head"),
        P("head", None),
        P(None, "head"),
        P(None, "head"),
        P(None, "head"),
        P("head", None),
        P(None, "head"),
        P("head", None),
        P(None, "head"),
        P(None, "head"),
        P(None, "head"),
        P("head", None),
    )
    out_specs = (P(("band", "head"), None), P("band", "head"))
    return jax.shard_map(local, mesh=mesh, in_specs=in_specs, out_specs=out_specs, check_vma=False)
```

time: 1030 us -> 297 us (0.29)
  local copies, waits for them, and re-layouts: 480 us -> 16.7 us
  waiting for transfers between devices: 238 us -> 81.2 us
  Pallas kernels: 0 us -> 146 us
  other arithmetic: 136 us -> 6.3 us
  matrix products: 122 us -> 0 us
  starting transfers between devices: 22.2 us -> 41.6 us
  between operations: 15.1 us -> 1.05 us
    gather x10 -> x0, local copies, waits for them, and re-layouts: 403 us -> none  [the longest x2 260 us: local(): jnp.take(near_grid_pairs, encoder_sources, axis=0)]
    pallas_call x0 -> x5, Pallas kernels: none -> 146 us  [the longest x1 56.6 us: local(): pl.pallas_call(decoder_kernel, out_shape=jax.ShapeDtypeStruct((points, wi...]
    dot_general x14 -> x0, matrix products: 122 us -> none  [the longest x6 47.5 us: project(): jnp.dot(matrix, weight, preferred_element_type=jnp.float32)]
    ppermute x6 -> x28, waiting for transfers between devices: 157 us -> 81.2 us  [the longest x2 30.1 us: onward(): return lax.ppermute(x, 'band', [(i, i + 1) for i in range(bands - 1)])]
    select_n x4, other arithmetic: 62.3 us -> 4.89 us  [the longest x1 2.5 us: local(): jnp.where(core == 0, jnp.concatenate([kept, got], 1), jnp.concatenate([go...]
    slice x5 -> x0, local copies, waits for them, and re-layouts: 53.9 us -> none  [the longest x1 43.9 us: edge_attention(): gathered[:, :, :full_width]]
    reduce_scatter x4 -> x0, waiting for transfers between devices: 45.3 us -> none  [the longest x1 12.3 us: local(): lax.psum_scatter(jnp.dot(enc_mix, encoder_output, preferred_element_type=...]
    all_gather x4 -> x0, waiting for transfers between devices: 35.4 us -> none  [the longest x1 11.9 us: local(): whole_mid = lax.all_gather(hidden_mid, 'head', axis=1, tiled=True)]
  transfers between devices with their start and end apart: 14 -> 28, of which waited for: 13 -> 10; matrix products, arithmetic and copies ran while one was open for 36% -> 6% of each run, Pallas kernels for 0% -> 24%
where the time goes in v1:
time: 297 us; the launch traced here: 293 us
  Pallas kernels  146 us (49%)
  waiting for transfers between devices  81.2 us (27%)
  starting transfers between devices  41.6 us (14%)
  local copies, waits for them, and re-layouts  16.7 us (6%)
  other arithmetic  6.3 us (2%)
    pallas_call x1, Pallas kernels, local(): pl.pallas_call(decoder_kernel, out_shape=jax.ShapeDtypeStruct((points, wi...  56.6 us
    pallas_call x1, Pallas kernels, local(): pl.pallas_call(window_kernel, out_shape=jax.ShapeDtypeStruct((pairs, rows...  35.1 us
    ppermute x2, waiting for transfers between devices, onward(): return lax.ppermute(x, 'band', [(i, i + 1) for i in range(bands - 1)])  30.1 us
    pallas_call x1, Pallas kernels, local(): pl.pallas_call(encoder_kernel, out_shape=jax.ShapeDtypeStruct((rows, full...  29.9 us
    ppermute x2, waiting for transfers between devices, backward(): return lax.ppermute(x, 'band', [(i + 1, i) for i in range(bands - 1)])  29.1 us
    pallas_call x1, Pallas kernels, local(): pl.pallas_call(feed_kernel, grid=(2 * steps,), out_shape=jax.ShapeDtypeSt...  18.1 us
    ppermute x1, starting transfers between devices, local(): lax.ppermute(edge, ('band', 'head'), [(2 * i, 2 * i + 2) for i in range(b...  13.9 us
    ppermute x1, waiting for transfers between devices, local(): lax.ppermute(mid, ('band', 'head'), facing + [(b, a) for a, b in facing])  11.2 us
  transfers between devices with their start and end apart: 28, of which 10 were waited for; matrix products, arithmetic and copies ran while one was open for 6% of the time, Pallas kernels for 24%

profile of v1, /device:TPU:23, one launch (start us, length us, event | category | flops | bytes accessed | tf_op | source)
XLA Modules:
  0.0 292.8 jit_solution(1996432317621200425)
XLA Ops:
  1.5 2.1 constant_dynamic-slice_fusion.3
  4.7 1.6 copy.27.own
  6.3 2.4 collective-permute-done.2.keys_other
  8.7 3.1 %collective-permute-start.3 = (bf16[2048,100]{1,0:T(8,128)(2,1)S(1)}, bf16[2048,100]{1,0:T(8,128)(2,1)S(1)}, u32[]{:S(2)}, u32[]{:S(2)}) collective-permute-start(bf16[2048,100]{1,0:T(8,128)(2,1)S(1)} %constant_dynamic-slice_fusion.5), channel_id=1, source_target_pairs={{0,2},{2,4},{4,6},{6,8},{8,10},{10,12},{12,14},{14,16},{16,18},{18... | collective-permute-start | bytes 1228808 | tf_op jit(solution)/shard_map/ppermute | solution.py:375
  11.8 2.2 collective-permute-start.5
  14.0 9.7 %collective-permute-done.3.prev_mine = bf16[2048,100]{1,0:T(8,128)(2,1)S(1)} collective-permute-done((bf16[2048,100]{1,0:T(8,128)(2,1)S(1)}, bf16[2048,100]{1,0:T(8,128)(2,1)S(1)}, u32[]{:S(2)}, u32[]{:S(2)}) %collective-permute-start.3) | collective-permute-done | bytes 409632 | tf_op jit(solution)/shard_map/ppermute | solution.py:375
  23.7 2.0 collective-permute-start.4
  25.7 8.8 %collective-permute-done.5.next_mine = bf16[2048,100]{1,0:T(8,128)(2,1)S(1)} collective-permute-done((bf16[2048,100]{1,0:T(8,128)(2,1)S(1)}, bf16[2048,100]{1,0:T(8,128)(2,1)S(1)}, u32[]{:S(2)}, u32[]{:S(2)}) %collective-permute-start.5) | collective-permute-done | bytes 409632 | tf_op jit(solution)/shard_map/ppermute | solution.py:378
  35.6 4.0 %collective-permute-done.6.next_other = bf16[2048,100]{1,0:T(8,128)(2,1)S(1)} collective-permute-done((bf16[2048,100]{1,0:T(8,128)(2,1)S(1)}, bf16[2048,100]{1,0:T(8,128)(2,1)S(1)}, u32[]{:S(2)}, u32[]{:S(2)}) %collective-permute-start.6) | collective-permute-done | bytes 409632 | tf_op jit(solution)/shard_map/ppermute | solution.py:372
  41.0 1.0 copy-done.6
  42.9 1.0 copy.28
  46.1 2.5 maximum_select_fusion.state
  48.7 6.3 %queries.1.query = f32[16,512,128]{2,1,0:T(8,128)} custom-call(bf16[512,1024]{1,0:T(8,128)(2,1)} %maximum_select_fusion.state, bf16[1024,512]{1,0:T(8,128)(2,1)} %wq_mine.2, bf16[1024,512]{1,0:T(8,128)(2,1)} %copy-done.8, bf16[128,512]{1,0:T(8,128)(2,1)} %copy-done.19, bf16[128,512]{1,0:T(8,128)(2,1)} %collective-permute-done.2.keys_other), custom_call_target="tpu_custom_call" | custom-call | tf_op jit(solution)/shard_map/queries/pallas_call | solution.py:401
  55.0 29.9 %encoder.1.own.mid = bf16[512,1024]{1,0:T(8,128)(2,1)} custom-call(s32[3]{0:T(128)} %pad_add_fusion.info, s32[16384]{0:T(1024)} %reshape.11.sources, s32[512,1]{1,0:T(8,128)} %copy.29.counts, f32[16,512,128]{2,1,0:T(8,128)} %queries.1.query, bf16[4096,100]{1,0:T(8,128)(2,1)} %copy-done.1, bf16[2048,100]{1,0:T(8,128)(2,1)} %copy-done.15, ...), custom_call_target="tpu_custom_call" | custom-call | tf_op jit(solution)/shard_map/encoder/pallas_call | solution.py:413
  84.9 5.4 %collective-permute-start.10 = (bf16[512,1024]{1,0:T(8,128)(2,1)}, bf16[512,1024]{1,0:T(8,128)(2,1)S(1)}, u32[]{:S(2)}, u32[]{:S(2)}) collective-permute-start(bf16[512,1024]{1,0:T(8,128)(2,1)} %encoder.1.own.mid), channel_id=1, source_target_pairs={{1,2},{3,4},{5,6},{7,8},{9,10},{11,12},{13,14},{15,16},{17,18},{19... | collective-permute-start | bytes 3145736 | tf_op jit(solution)/shard_map/ppermute | solution.py:431
  91.9 11.2 %collective-permute-done.10.far = bf16[512,1024]{1,0:T(8,128)(2,1)S(1)} collective-permute-done((bf16[512,1024]{1,0:T(8,128)(2,1)}, bf16[512,1024]{1,0:T(8,128)(2,1)S(1)}, u32[]{:S(2)}, u32[]{:S(2)}) %collective-permute-start.10) | collective-permute-done | bytes 1048608 | tf_op jit(solution)/shard_map/ppermute | solution.py:431
  103.1 13.9 %collective-permute-start.11 = (bf16[48,1024]{1,0:T(8,128)(2,1)S(1)}, bf16[48,1024]{1,0:T(8,128)(2,1)S(1)}, u32[]{:S(2)}, u32[]{:S(2)}) collective-permute-start(bf16[48,1024]{1,0:T(8,128)(2,1)S(1)} %slice_select_fusion.1), channel_id=1, source_target_pairs={{0,2},{2,4},{4,6},{6,8},{8,10},{10,12},{12,14},{14,16},{16,18},{18... | collective-permute-start | bytes 294920 | tf_op jit(solution)/shard_map/ppermute | solution.py:433
  117.0 2.2 collective-permute-done.11.far_more
  119.2 1.4 collective-permute-start.12
  122.2 35.1 %window.1.mix = bf16[8,512,128]{2,1,0:T(8,128)(2,1)} custom-call(s32[3]{0:T(128)} %pad_add_fusion.info, bf16[512,1024]{1,0:T(8,128)(2,1)} %encoder.1.own.mid, bf16[512,1024]{1,0:T(8,128)(2,1)} %copy-done.9, bf16[512,1024]{1,0:T(8,128)(2,1)} %copy-done.4, bf16[48,1024]{1,0:T(8,128)(2,1)} %copy-done.26, bf16[48,1024]{1,0:T(8,128)(2,1)} %copy-done.27, ...), custom_call_target="tpu_custom_call" | custom-call | tf_op jit(solution)/shard_map/window/pallas_call | solution.py:444
  158.4 18.1 %feed.1.own = bf16[512,1024]{1,0:T(8,128)(2,1)} custom-call(bf16[8,512,128]{2,1,0:T(8,128)(2,1)} %window.1.mix, bf16[512,1024]{1,0:T(8,128)(2,1)} %encoder.1.own.mid, bf16[512,1024]{1,0:T(8,128)(2,1)} %wo_mine.1, bf16[512,1024]{1,0:T(8,128)(2,1)} %copy-done.11, bf16[1024,2048]{1,0:T(8,128)(2,1)} %up_mine.1, ...), custom_call_target="tpu_custom_call" | custom-call | tf_op jit(solution)/shard_map/feed/pallas_call | solution.py:466
  176.4 2.7 collective-permute-start.20
  179.1 3.4 %collective-permute-start.22 = (bf16[512,1024]{1,0:T(8,128)(2,1)}, bf16[512,1024]{1,0:T(8,128)(2,1)}, u32[]{:S(2)}, u32[]{:S(2)}) collective-permute-start(bf16[512,1024]{1,0:T(8,128)(2,1)} %feed.1.own), channel_id=1, source_target_pairs={{2,0},{4,2},{6,4},{8,6},{10,8},{12,10},{14,12},{16,14},{18,16},{20... | collective-permute-start | bytes 3145736 | tf_op jit(solution)/shard_map/ppermute | solution.py:378
  183.8 20.4 %collective-permute-done.20.prev_mine = bf16[512,1024]{1,0:T(8,128)(2,1)} collective-permute-done((bf16[512,1024]{1,0:T(8,128)(2,1)}, bf16[512,1024]{1,0:T(8,128)(2,1)}, u32[]{:S(2)}, u32[]{:S(2)}) %collective-permute-start.20) | collective-permute-done | bytes 1048608 | tf_op jit(solution)/shard_map/ppermute | solution.py:375
  204.2 1.3 collective-permute-start.21
  205.5 20.3 %collective-permute-done.22.next_mine = bf16[512,1024]{1,0:T(8,128)(2,1)} collective-permute-done((bf16[512,1024]{1,0:T(8,128)(2,1)}, bf16[512,1024]{1,0:T(8,128)(2,1)}, u32[]{:S(2)}, u32[]{:S(2)}) %collective-permute-start.22) | collective-permute-done | bytes 1048608 | tf_op jit(solution)/shard_map/ppermute | solution.py:378
  226.3 1.0 pad.18.grid
  228.4 1.3 reshape.10.sources
  230.7 1.2 collective-permute-done.27.wo_other
  232.1 1.4 maximum_select_fusion.1
  234.1 56.6 %decoder.1 = bf16[2048,100]{1,0:T(8,128)(2,1)} custom-call(s32[3]{0:T(128)} %pad_add_fusion.info, s32[8192]{0:T(1024)} %reshape.10.sources, s32[2048]{0:T(1024)} %dynamic_slice.28.counts, bf16[2048,128]{1,0:T(8,128)(2,1)} %pad.18.grid, bf16[512,1024]{1,0:T(8,128)(2,1)} %feed.1.own, bf16[512,1024]{1,0:T(8,128)(2,1)} %copy-done.3, ...), custom_call_target="tpu_custom_call" | custom-call | tf_op jit(solution)/shard_map/decoder/pallas_call | solution.py:508
  290.7 2.1 copy.32
  (115 shorter events, 16.2 us)
Async XLA Ops:
  0.7 156.7 %collective-permute-start.17 = (bf16[1024,2048]{1,0:T(8,128)(2,1)}, bf16[1024,2048]{1,0:T(8,128)(2,1)}, u32[]{:S(2)}, u32[]{:S(2)}) collective-permute-start(bf16[1024,2048]{1,0:T(8,128)(2,1)} %up_mine.1), channel_id=1, source_target_pairs={{0,1},{1,0},{2,3},{3,2},{4,5},{5,4},{6,7},{7,6},{8,9},{9,8},{10,11... | collective-permute-start | bytes 12582920 | tf_op jit(solution)/shard_map/ppermute | solution.py:372
  1.4 156.0 %collective-permute-start.18 = (bf16[2048,1024]{1,0:T(8,128)(2,1)}, bf16[2048,1024]{1,0:T(8,128)(2,1)}, u32[]{:S(2)}, u32[]{:S(2)}) collective-permute-start(bf16[2048,1024]{1,0:T(8,128)(2,1)} %down_mine.1), channel_id=1, source_target_pairs={{0,1},{1,0},{2,3},{3,2},{4,5},{5,4},{6,7},{7,6},{8,9},{9,8},{10,11... | collective-permute-start | bytes 12582920 | tf_op jit(solution)/shard_map/ppermute | solution.py:372
  3.6 31.5 %collective-permute-start = (bf16[512,512]{1,0:T(8,128)(2,1)}, bf16[512,512]{1,0:T(8,128)(2,1)}, u32[]{:S(2)}, u32[]{:S(2)}) collective-permute-start(bf16[512,512]{1,0:T(8,128)(2,1)} %get-tuple-element.7), channel_id=1, source_target_pairs={{0,1},{1,0},{2,3},{3,2},{4,5},{5,4},{6,7},{7,6},{8,9},{9,8},{10,11... | collective-permute-start | bytes 1572872 | tf_op jit(solution)/shard_map/ppermute | solution.py:372
  4.0 4.7 %collective-permute-start.2 = (bf16[128,512]{1,0:T(8,128)(2,1)S(1)}, bf16[128,512]{1,0:T(8,128)(2,1)}, u32[]{:S(2)}, u32[]{:S(2)}) collective-permute-start(bf16[128,512]{1,0:T(8,128)(2,1)S(1)} %pad.19.keys_mine), channel_id=1, source_target_pairs={{0,1},{1,0},{2,3},{3,2},{4,5},{5,4},{6,7},{7,6},{8,9},{9,8},{10,11... | collective-permute-start | bytes 393224 | tf_op jit(solution)/shard_map/ppermute | solution.py:372
  4.2 7.6 %collective-permute-start.7 = (bf16[128,512]{1,0:T(8,128)(2,1)S(1)}, bf16[128,512]{1,0:T(8,128)(2,1)}, u32[]{:S(2)}, u32[]{:S(2)}) collective-permute-start(bf16[128,512]{1,0:T(8,128)(2,1)S(1)} %pad.20.values_mine), channel_id=1, source_target_pairs={{0,1},{1,0},{2,3},{3,2},{4,5},{5,4},{6,7},{7,6},{8,9},{9,8},{10,11... | collective-permute-start | bytes 393224 | tf_op jit(solution)/shard_map/ppermute | solution.py:372
  8.7 15.0 %collective-permute-start.3 = (bf16[2048,100]{1,0:T(8,128)(2,1)S(1)}, bf16[2048,100]{1,0:T(8,128)(2,1)S(1)}, u32[]{:S(2)}, u32[]{:S(2)}) collective-permute-start(bf16[2048,100]{1,0:T(8,128)(2,1)S(1)} %constant_dynamic-slice_fusion.5), channel_id=1, source_target_pairs={{0,2},{2,4},{4,6},{6,8},{8,10},{10,12},{12,14},{14,16},{16,18},{18... | collective-permute-start | bytes 1228808 | tf_op jit(solution)/shard_map/ppermute | solution.py:375
  11.8 22.7 %collective-permute-start.5 = (bf16[2048,100]{1,0:T(8,128)(2,1)S(1)}, bf16[2048,100]{1,0:T(8,128)(2,1)S(1)}, u32[]{:S(2)}, u32[]{:S(2)}) collective-permute-start(bf16[2048,100]{1,0:T(8,128)(2,1)S(1)} %constant_dynamic-slice_fusion.5), channel_id=1, source_target_pairs={{2,0},{4,2},{6,4},{8,6},{10,8},{12,10},{14,12},{16,14},{18,16},{20... | collective-permute-start | bytes 1228808 | tf_op jit(solution)/shard_map/ppermute | solution.py:378
  23.7 11.4 %collective-permute-start.4 = (bf16[2048,100]{1,0:T(8,128)(2,1)S(1)}, bf16[2048,100]{1,0:T(8,128)(2,1)S(1)}, u32[]{:S(2)}, u32[]{:S(2)}) collective-permute-start(bf16[2048,100]{1,0:T(8,128)(2,1)S(1)} %collective-permute-done.3.prev_mine), channel_id=1, source_target_pairs={{0,1},{1,0},{2,3},{3,2},{4,5},{5,4},{6,7},{7,6},{8,9},{9,8},{10,11... | collective-permute-start | bytes 1228808 | tf_op jit(solution)/shard_map/ppermute | solution.py:372
  34.6 5.4 %collective-permute-start.1 = (bf16[1024,512]{1,0:T(8,128)(2,1)}, bf16[1024,512]{1,0:T(8,128)(2,1)S(1)}, u32[]{:S(2)}, u32[]{:S(2)}) collective-permute-start(bf16[1024,512]{1,0:T(8,128)(2,1)} %wq_mine.2), channel_id=1, source_target_pairs={{0,1},{1,0},{2,3},{3,2},{4,5},{5,4},{6,7},{7,6},{8,9},{9,8},{10,11... | collective-permute-start | bytes 3145736 | tf_op jit(solution)/shard_map/ppermute | solution.py:372
  35.1 5.1 %collective-permute-start.8 = (bf16[512,1024]{1,0:T(8,128)(2,1)S(1)}, bf16[512,1024]{1,0:T(8,128)(2,1)S(1)}, u32[]{:S(2)}, u32[]{:S(2)}) collective-permute-start(bf16[512,1024]{1,0:T(8,128)(2,1)S(1)} %copy-done.5), channel_id=1, source_target_pairs={{0,1},{1,0},{2,3},{3,2},{4,5},{5,4},{6,7},{7,6},{8,9},{9,8},{10,11... | collective-permute-start | bytes 3145736 | tf_op jit(solution)/shard_map/ppermute | solution.py:372
  35.1 4.5 %collective-permute-start.6 = (bf16[2048,100]{1,0:T(8,128)(2,1)S(1)}, bf16[2048,100]{1,0:T(8,128)(2,1)S(1)}, u32[]{:S(2)}, u32[]{:S(2)}) collective-permute-start(bf16[2048,100]{1,0:T(8,128)(2,1)S(1)} %collective-permute-done.5.next_mine), channel_id=1, source_target_pairs={{0,1},{1,0},{2,3},{3,2},{4,5},{5,4},{6,7},{7,6},{8,9},{9,8},{10,11... | collective-permute-start | bytes 1228808 | tf_op jit(solution)/shard_map/ppermute | solution.py:372
  39.6 45.3 %collective-permute-start.13 = (bf16[1024,512]{1,0:T(8,128)(2,1)}, bf16[1024,512]{1,0:T(8,128)(2,1)}, u32[]{:S(2)}, u32[]{:S(2)}) collective-permute-start(bf16[1024,512]{1,0:T(8,128)(2,1)} %wq_mine.3), channel_id=1, source_target_pairs={{0,1},{1,0},{2,3},{3,2},{4,5},{5,4},{6,7},{7,6},{8,9},{9,8},{10,11... | collective-permute-start | bytes 3145736 | tf_op jit(solution)/shard_map/ppermute | solution.py:372
  40.0 50.3 %collective-permute-start.14 = (bf16[1024,512]{1,0:T(8,128)(2,1)}, bf16[1024,512]{1,0:T(8,128)(2,1)}, u32[]{:S(2)}, u32[]{:S(2)}) collective-permute-start(bf16[1024,512]{1,0:T(8,128)(2,1)} %wk_mine.2), channel_id=1, source_target_pairs={{0,1},{1,0},{2,3},{3,2},{4,5},{5,4},{6,7},{7,6},{8,9},{9,8},{10,11... | collective-permute-start | bytes 3145736 | tf_op jit(solution)/shard_map/ppermute | solution.py:372
  42.0 48.3 %collective-permute-start.15 = (bf16[1024,512]{1,0:T(8,128)(2,1)}, bf16[1024,512]{1,0:T(8,128)(2,1)S(1)}, u32[]{:S(2)}, u32[]{:S(2)}) collective-permute-start(bf16[1024,512]{1,0:T(8,128)(2,1)} %wv_mine.2), channel_id=1, source_target_pairs={{0,1},{1,0},{2,3},{3,2},{4,5},{5,4},{6,7},{7,6},{8,9},{9,8},{10,11... | collective-permute-start | bytes 3145736 | tf_op jit(solution)/shard_map/ppermute | solution.py:372
  84.9 18.2 %collective-permute-start.10 = (bf16[512,1024]{1,0:T(8,128)(2,1)}, bf16[512,1024]{1,0:T(8,128)(2,1)S(1)}, u32[]{:S(2)}, u32[]{:S(2)}) collective-permute-start(bf16[512,1024]{1,0:T(8,128)(2,1)} %encoder.1.own.mid), channel_id=1, source_target_pairs={{1,2},{3,4},{5,6},{7,8},{9,10},{11,12},{13,14},{15,16},{17,18},{19... | collective-permute-start | bytes 3145736 | tf_op jit(solution)/shard_map/ppermute | solution.py:431
  90.3 30.3 %collective-permute-start.9 = (bf16[512,1024]{1,0:T(8,128)(2,1)}, bf16[512,1024]{1,0:T(8,128)(2,1)S(1)}, u32[]{:S(2)}, u32[]{:S(2)}) collective-permute-start(bf16[512,1024]{1,0:T(8,128)(2,1)} %encoder.1.own.mid), channel_id=1, source_target_pairs={{0,1},{1,0},{2,3},{3,2},{4,5},{5,4},{6,7},{7,6},{8,9},{9,8},{10,11... | collective-permute-start | bytes 3145736 | tf_op jit(solution)/shard_map/ppermute | solution.py:372
  90.4 67.0 %collective-permute-start.16 = (bf16[512,1024]{1,0:T(8,128)(2,1)S(1)}, bf16[512,1024]{1,0:T(8,128)(2,1)S(1)}, u32[]{:S(2)}, u32[]{:S(2)}) collective-permute-start(bf16[512,1024]{1,0:T(8,128)(2,1)S(1)} %copy-done.10), channel_id=1, source_target_pairs={{0,1},{1,0},{2,3},{3,2},{4,5},{5,4},{6,7},{7,6},{8,9},{9,8},{10,11... | collective-permute-start | bytes 3145736 | tf_op jit(solution)/shard_map/ppermute | solution.py:372
  103.1 16.1 %collective-permute-start.11 = (bf16[48,1024]{1,0:T(8,128)(2,1)S(1)}, bf16[48,1024]{1,0:T(8,128)(2,1)S(1)}, u32[]{:S(2)}, u32[]{:S(2)}) collective-permute-start(bf16[48,1024]{1,0:T(8,128)(2,1)S(1)} %slice_select_fusion.1), channel_id=1, source_target_pairs={{0,2},{2,4},{4,6},{6,8},{8,10},{10,12},{12,14},{14,16},{16,18},{18... | collective-permute-start | bytes 294920 | tf_op jit(solution)/shard_map/ppermute | solution.py:433
  119.2 2.3 collective-permute-start.12
  176.4 53.2 %copy-start.28 = (s32[4096]{0:T(1024)S(1)}, s32[4096]{0:T(1024)}, u32[]{:S(2)}) copy-start(s32[4096]{0:T(1024)} %param.25) | copy-start | bytes 49156
  176.4 53.8 %copy-start.24 = (bf16[512,100]{0,1:T(8,128)(2,1)S(1)}, bf16[512,100]{0,1:T(8,128)(2,1)}, u32[]{:S(2)}) copy-start(bf16[512,100]{0,1:T(8,128)(2,1)} %param.39) | copy-start | bytes 307204
  176.4 54.0 %copy-start.25 = (bf16[100,512]{1,0:T(8,128)(2,1)S(1)}, bf16[100,512]{1,0:T(8,128)(2,1)}, u32[]{:S(2)}) copy-start(bf16[100,512]{1,0:T(8,128)(2,1)} %param.36) | copy-start | bytes 307204
  176.4 54.2 %copy-start.2 = (bf16[512,1024]{1,0:T(8,128)(2,1)S(1)}, bf16[512,1024]{1,0:T(8,128)(2,1)}, u32[]{:S(2)}) copy-start(bf16[512,1024]{1,0:T(8,128)(2,1)} %feed.1.own) | copy-start | bytes 3145732
  176.4 27.8 %collective-permute-start.20 = (bf16[512,1024]{1,0:T(8,128)(2,1)}, bf16[512,1024]{1,0:T(8,128)(2,1)}, u32[]{:S(2)}, u32[]{:S(2)}) collective-permute-start(bf16[512,1024]{1,0:T(8,128)(2,1)} %feed.1.own), channel_id=1, source_target_pairs={{0,2},{2,4},{4,6},{6,8},{8,10},{10,12},{12,14},{14,16},{16,18},{18... | collective-permute-start | bytes 3145736 | tf_op jit(solution)/shard_map/ppermute | solution.py:375
  179.1 46.7 %collective-permute-start.22 = (bf16[512,1024]{1,0:T(8,128)(2,1)}, bf16[512,1024]{1,0:T(8,128)(2,1)}, u32[]{:S(2)}, u32[]{:S(2)}) collective-permute-start(bf16[512,1024]{1,0:T(8,128)(2,1)} %feed.1.own), channel_id=1, source_target_pairs={{2,0},{4,2},{6,4},{8,6},{10,8},{12,10},{14,12},{16,14},{18,16},{20... | collective-permute-start | bytes 3145736 | tf_op jit(solution)/shard_map/ppermute | solution.py:378
  182.6 47.9 %collective-permute-start.19 = (bf16[512,1024]{1,0:T(8,128)(2,1)}, bf16[512,1024]{1,0:T(8,128)(2,1)S(1)}, u32[]{:S(2)}, u32[]{:S(2)}) collective-permute-start(bf16[512,1024]{1,0:T(8,128)(2,1)} %feed.1.own), channel_id=1, source_target_pairs={{0,1},{1,0},{2,3},{3,2},{4,5},{5,4},{6,7},{7,6},{8,9},{9,8},{10,11... | collective-permute-start | bytes 3145736 | tf_op jit(solution)/shard_map/ppermute | solution.py:372
  183.3 50.2 %collective-permute-start.25 = (bf16[1024,512]{1,0:T(8,128)(2,1)}, bf16[1024,512]{1,0:T(8,128)(2,1)}, u32[]{:S(2)}, u32[]{:S(2)}) collective-permute-start(bf16[1024,512]{1,0:T(8,128)(2,1)} %wk_mine.3), channel_id=1, source_target_pairs={{0,1},{1,0},{2,3},{3,2},{4,5},{5,4},{6,7},{7,6},{8,9},{9,8},{10,11... | collective-permute-start | bytes 3145736 | tf_op jit(solution)/shard_map/ppermute | solution.py:372
  183.4 50.2 %collective-permute-start.26 = (bf16[1024,512]{1,0:T(8,128)(2,1)}, bf16[1024,512]{1,0:T(8,128)(2,1)}, u32[]{:S(2)}, u32[]{:S(2)}) collective-permute-start(bf16[1024,512]{1,0:T(8,128)(2,1)} %wv_mine.3), channel_id=1, source_target_pairs={{0,1},{1,0},{2,3},{3,2},{4,5},{5,4},{6,7},{7,6},{8,9},{9,8},{10,11... | collective-permute-start | bytes 3145736 | tf_op jit(solution)/shard_map/ppermute | solution.py:372
  204.2 29.3 %collective-permute-start.21 = (bf16[512,1024]{1,0:T(8,128)(2,1)}, bf16[512,1024]{1,0:T(8,128)(2,1)}, u32[]{:S(2)}, u32[]{:S(2)}) collective-permute-start(bf16[512,1024]{1,0:T(8,128)(2,1)} %collective-permute-done.20.prev_mine), channel_id=1, source_target_pairs={{0,1},{1,0},{2,3},{3,2},{4,5},{5,4},{6,7},{7,6},{8,9},{9,8},{10,11... | collective-permute-start | bytes 3145736 | tf_op jit(solution)/shard_map/ppermute | solution.py:372
  225.8 7.7 %collective-permute-start.23 = (bf16[512,1024]{1,0:T(8,128)(2,1)}, bf16[512,1024]{1,0:T(8,128)(2,1)}, u32[]{:S(2)}, u32[]{:S(2)}) collective-permute-start(bf16[512,1024]{1,0:T(8,128)(2,1)} %collective-permute-done.22.next_mine), channel_id=1, source_target_pairs={{0,1},{1,0},{2,3},{3,2},{4,5},{5,4},{6,7},{7,6},{8,9},{9,8},{10,11... | collective-permute-start | bytes 3145736 | tf_op jit(solution)/shard_map/ppermute | solution.py:372
  230.5 1.4 collective-permute-start.27
  231.9 1.6 collective-permute-start.24
  (26 other events, 366.6 us)

commit v2 on v1

v2 whole, which is shorter than its diff:
```python
import functools
import math

import jax
import jax.numpy as jnp
from jax import lax
from jax.experimental import pallas as pl
from jax.experimental.pallas import tpu as pltpu
from jax.sharding import PartitionSpec as P

HALF_WIN = 560
HEAD_DIM = 64
LANES = 128
EPSILON = 1e-05
NEGATIVE = -1e30
SCALE = HEAD_DIM ** (-0.5) * math.log2(math.e)

bf16 = jnp.bfloat16
f32 = jnp.float32
ROWS_BY_ROWS = (((1,), (1,)), ((), ()))
VMEM = pl.BlockSpec(memory_space=pltpu.VMEM)
SMEM = pl.BlockSpec(memory_space=pltpu.SMEM)
ANY = pl.BlockSpec(memory_space=pl.ANY)
BIG = pltpu.CompilerParams(vmem_limit_bytes=58 * 2**20)


def cost(flops):
    return pl.CostEstimate(flops=flops, bytes_accessed=flops // 256, transcendentals=0)


def dot(a, b):
    return jnp.dot(a, b, preferred_element_type=f32)


def layer_norm(matrix):
    x = matrix.astype(f32)
    centred = x - jnp.mean(x, axis=-1, keepdims=True)
    variance = jnp.mean(centred * centred, axis=-1, keepdims=True)
    return (centred * lax.rsqrt(variance + EPSILON)).astype(bf16)


def low_lanes(shape):
    return lax.broadcasted_iota(jnp.int32, shape, len(shape) - 1) % LANES < HEAD_DIM


def query_kernel(state, wq_mine, wq_other, keys_mine, keys_other, passing, *refs):
    out, passed = refs[-2:]
    del passing, passed
    normed = layer_norm(state[...])
    pairs = wq_mine.shape[1] // LANES
    for side, (wq, keys) in enumerate(((wq_mine, keys_mine), (wq_other, keys_other))):
        query = (dot(normed, wq[...])).astype(bf16)
        for pair in range(pairs):
            two = query[:, pair * LANES : (pair + 1) * LANES]
            low = low_lanes(two.shape)
            weight = keys[:, pair * LANES : (pair + 1) * LANES]
            for sub in range(2):
                one = jnp.where(low if sub == 0 else ~low, two, jnp.zeros_like(two))
                out[(side * pairs + pair) * 2 + sub] = (
                    lax.dot_general(one, weight, ROWS_BY_ROWS, preferred_element_type=f32) * SCALE
                )


GRID_CHUNKS = 2
ENCODER_CHUNKS = 1
GROUP = 8
CHAINS = 4


def encoder_kernel(
    info, sources, counts, query, own, *refs, spots, skip,
):
    near, refs = refs[: len(spots)], refs[len(spots) :]
    values_mine, values_other, out_mine, out_other, state, result, table = refs[:7]
    picked, mix = refs[7:-1], refs[-1]
    grid_count, width = own.shape
    heads = query.shape[0]
    rows = result.shape[0]
    slots = sources.shape[0] // query.shape[1]
    span = GROUP * slots
    table[...] = jnp.zeros_like(table)

    def fill(start, ref):
        table[pl.ds(pl.multiple_of(start, 8), ref.shape[0]), :width] = ref[...].astype(f32)

    fill(grid_count, own)
    for ref, (place, offset) in zip(near, spots):
        fill(info[place] + offset, ref)

    node = lax.broadcasted_iota(jnp.int32, (GROUP, span), 0)
    slot = lax.broadcasted_iota(jnp.int32, (GROUP, span), 1) - node * slots

    def step(index, carry):
        groups = [index * CHAINS + chain for chain in range(CHAINS)]
        starts = [pl.multiple_of(group * GROUP, GROUP) for group in groups]
        for group, rows_ref in zip(groups, picked):
            base = group * span + skip * slots
            for s in range(span):
                rows_ref[s : s + 1, :] = table[pl.ds(sources[base + s], 1), :]
        grids = [ref[...].astype(bf16) for ref in picked]
        live = [(slot >= 0) & (slot < counts[pl.ds(start + skip, GROUP), :]) for start in starts]
        queries = [
            query[:, pl.ds(start + skip, GROUP), :].reshape(heads * GROUP, LANES).astype(bf16)
            for start in starts
        ]
        scores = [
            lax.dot_general(q, g, ROWS_BY_ROWS, preferred_element_type=f32)
            for q, g in zip(queries, grids)
        ]
        powers = [
            jnp.where(on[None], jnp.exp2(s.reshape(heads, GROUP, span)), 0.0).reshape(
                heads * GROUP, span
            )
            for s, on in zip(scores, live)
        ]
        weights = [(p * (1.0 / jnp.sum(p, -1, keepdims=True))).astype(bf16) for p in powers]
        mixed = [dot(w, g) for w, g in zip(weights, grids)]
        for start, m in zip(starts, mixed):
            mix[:, pl.ds(start, GROUP), :] = m.reshape(heads, GROUP, LANES)
        return carry

    lax.fori_loop(0, rows // (GROUP * CHAINS), step, 0)

    pairs = values_mine.shape[1] // LANES
    total = state[skip : skip + rows, :].astype(f32)
    for side, (values, out) in enumerate(((values_mine, out_mine), (values_other, out_other))):
        parts = []
        for pair in range(pairs):
            weight = values[:, pair * LANES : (pair + 1) * LANES]
            low = low_lanes(weight.shape)
            both = jnp.concatenate(
                [jnp.where(low, weight, 0.0).astype(bf16), jnp.where(low, 0.0, weight).astype(bf16)], 0
            )
            head = (side * pairs + pair) * 2
            two = jnp.concatenate([mix[head].astype(bf16), mix[head + 1].astype(bf16)], 1)
            parts.append(dot(two, both).astype(bf16))
        total = total + dot(jnp.concatenate(parts, 1), out[...])
    result[...] = total.astype(bf16)


def lay(start, block, refs):
    for ref in refs:
        block[start : start + ref.shape[0], :] = layer_norm(ref[...])
        start += ref.shape[0]
    return start


def project_pairs(target, rows, weights, scale=None):
    for side, weight in enumerate(weights):
        block = dot(rows, weight[...]).astype(bf16)
        if scale is not None:
            block = (block.astype(f32) * scale).astype(bf16)
        pairs = weight.shape[1] // LANES
        for pair in range(pairs):
            target[side * pairs + pair] = block[:, pair * LANES : (pair + 1) * LANES]


def score_bound(query, key):
    row = lax.broadcasted_iota(jnp.int32, (LANES, LANES), 0) // HEAD_DIM
    col = lax.broadcasted_iota(jnp.int32, (LANES, LANES), 1) // HEAD_DIM
    same_head = jnp.where(row == col, 1.0, 0.0).astype(bf16)

    def longest(ref):
        most = None
        for pair in range(ref.shape[0]):
            x = ref[pair].astype(f32)
            found = jnp.max(dot((x * x).astype(bf16), same_head), axis=0, keepdims=True)
            most = found if most is None else jnp.maximum(most, found)
        return jnp.max(most)

    return longest(query) * longest(key) * 1.05


SAFE = 100.0


def attend(query, key, value, bias, block, finish, free=0):
    pairs, rows, _ = query.shape
    heads_at = lambda q, low, sub: jnp.where(low if sub == 0 else ~low, q, jnp.zeros_like(q))
    safe = score_bound(query, key) <= SAFE * SAFE

    def plain(pair, carry):
        k, v = key[pair], value[pair]
        low_v = low_lanes(v.shape)
        ones = jnp.ones_like(v)
        sides = [jnp.where(low_v, v, ones), jnp.where(low_v, ones, v)]
        for start in range(0, rows, block):
            at = slice(start, start + block)
            q = query[pair, at, :]
            low = low_lanes(q.shape)
            found = []
            for sub in range(2):
                s = lax.dot_general(heads_at(q, low, sub), k, ROWS_BY_ROWS, preferred_element_type=f32)
                p = jnp.exp2(s[:, free:] + bias[at, free:]).astype(bf16)
                if free:
                    p = jnp.concatenate([jnp.exp2(s[:, :free]).astype(bf16), p], 1)
                found.append(dot(p, sides[sub]))
            sums = pltpu.roll(jnp.where(low, found[1], found[0]), HEAD_DIM, 1)
            mixed = jnp.where(low, found[0], found[1]) * (1.0 / jnp.where(sums == 0.0, 1.0, sums))
            finish(pair, at, mixed, sums)
        return carry

    def careful(pair, carry):
        for start in range(0, rows, block):
            at = slice(start, start + block)
            q = query[pair, at, :]
            low = low_lanes(q.shape)
            mixes, sums = [], []
            for sub in range(2):
                s = lax.dot_general(
                    heads_at(q, low, sub), key[pair], ROWS_BY_ROWS, preferred_element_type=f32
                )
                p = jnp.exp2(s + bias[at, :])
                total = jnp.sum(p, -1, keepdims=True)
                w = (p * (1.0 / jnp.where(total == 0.0, 1.0, total))).astype(bf16)
                mixes.append(dot(w, value[pair]))
                sums.append(total)
            finish(pair, at, jnp.where(low, mixes[0], mixes[1]), jnp.where(low, sums[0], sums[1]))
        return carry

    @pl.when(safe)
    def _():
        lax.fori_loop(0, pairs, plain, 0)

    @pl.when(jnp.logical_not(safe))
    def _():
        lax.fori_loop(0, pairs, careful, 0)


def near_window_kernel(info, *refs):
    count = (len(refs) - 14) // 2
    nodes, weights = refs[: 2 * count], refs[2 * count : 2 * count + 6]
    query, mix, total, token, normed, key, value, bias = refs[2 * count + 6 :]
    lay(0, normed, nodes)
    rows = query.shape[1]
    project_pairs(query, normed[:rows, :], weights[:2], SCALE)
    project_pairs(key, normed[...], weights[2:4])
    project_pairs(value, normed[...], weights[4:])
    row = lax.broadcasted_iota(jnp.int32, bias.shape, 0)
    col = lax.broadcasted_iota(jnp.int32, bias.shape, 1)
    place = jnp.where(col < rows, col, col - rows + jnp.where(info[0] == 0, rows, -rows))
    bias[...] = jnp.where(jnp.abs(row - place) <= HALF_WIN, 0.0, NEGATIVE)
    token[...] = jnp.zeros_like(token)

    def finish(pair, at, mixed, sums):
        mix[pair, at, :] = mixed
        total[pair, at, :] = sums

    attend(query, key, value, bias, rows // 2, finish, free=rows)


def far_window_kernel(info, query, near_mix, near_total, *refs):
    count = len(refs) - 9
    nodes, weights = refs[:count], refs[count : count + 4]
    result, normed, key, value, bias = refs[count + 4 :]
    rows = query.shape[1]
    more = nodes[-1].shape[0]
    used = lay(0, normed, nodes)
    normed[used:, :] = jnp.zeros_like(normed[used:, :])
    project_pairs(key, normed[...], weights[:2])
    project_pairs(value, normed[...], weights[2:])
    first, whole, lead = info[1], info[2], info[0] == 0
    row = lax.broadcasted_iota(jnp.int32, bias.shape, 0)
    col = lax.broadcasted_iota(jnp.int32, bias.shape, 1)
    place = jnp.where(
        col < rows,
        col + jnp.where(lead, -rows, rows),
        jnp.where(
            col < rows + more,
            col - rows + jnp.where(lead, -rows - more, 2 * rows),
            col - rows - more + jnp.where(lead, 2 * rows, -rows - more),
        ),
    )
    live = (jnp.abs(row - place) <= HALF_WIN) & (first + place >= 0) & (first + place < whole) & (col < used)
    bias[...] = jnp.where(live, 0.0, NEGATIVE)

    def finish(pair, at, mixed, sums):
        near_sums = near_total[pair, at, :]
        inverse = 1.0 / (near_sums + sums)
        result[pair, at, :] = (near_mix[pair, at, :] * (near_sums * inverse) + mixed * (sums * inverse)).astype(bf16)

    attend(query, key, value, bias, rows, finish)


def feed_kernel(mix, mid, wo_mine, wo_other, up_mine, up_other, down_mine, down_other, result, att, normed, total):
    index = pl.program_id(0)
    half = pl.num_programs(0) // 2

    @pl.when(index == 0)
    def _():
        pairs = wo_mine.shape[0] // LANES
        acc = mid[...].astype(f32)
        for side, wo in enumerate((wo_mine, wo_other)):
            block = jnp.concatenate([mix[side * pairs + pair] for pair in range(pairs)], 1)
            acc = acc + dot(block, wo[...])
        att[...] = acc.astype(bf16)
        normed[...] = layer_norm(att[...])
        total[...] = att[...].astype(f32)

    def part(up, down):
        inner = jax.nn.gelu(dot(normed[...], up[...]), approximate=True).astype(bf16)
        total[...] += dot(inner, down[...])

    @pl.when(index < half)
    def _():
        part(up_mine, down_mine)

    @pl.when(index >= half)
    def _():
        part(up_other, down_other)

    @pl.when(index == 2 * half - 1)
    def _():
        result[...] = total[...].astype(bf16)


POINTS = 32
FEED_CHUNKS = 2


def decoder_kernel(info, sources, counts, grid, *refs, spots):
    nodes_in, refs = refs[: len(spots)], refs[len(spots) :]
    wq_mine, wq_other, wk_mine, wk_other, wv_mine, wv_other, wo_mine, wo_other = refs[:8]
    result, table, query, product, gathered = refs[8:]
    deep = query.shape[1]
    points = grid.shape[0]
    slots = sources.shape[0] // points
    piece = 256

    for ref, (place, offset) in zip(nodes_in, spots):
        gathered[pl.ds(pl.multiple_of(info[place] + offset, 16), ref.shape[0]), :] = ref[...]
    count = gathered.shape[0] // 6

    def fill(index, carry):
        at = pl.ds(pl.multiple_of(index * count, 16), count)
        normed = layer_norm(gathered[at, :])
        for side, pair in enumerate(((wk_mine, wk_other), (wv_mine, wv_other))):
            block = jnp.concatenate([dot(normed, weight[...]) for weight in pair], 1)
            table[at, side * deep : (side + 1) * deep, :] = block.reshape(count, deep, LANES)
        return carry

    lax.fori_loop(0, 6, fill, 0)

    def ask(index, carry):
        at = pl.ds(pl.multiple_of(index * piece, piece), piece)
        own_grid = grid[at, :]
        block = jnp.concatenate([dot(own_grid, weight[...]) for weight in (wq_mine, wq_other)], 1) * SCALE
        query[at] = block.reshape(piece, deep, LANES)
        return carry

    lax.fori_loop(0, points // piece, ask, 0)

    ones_row = lax.broadcasted_iota(jnp.int32, (2 * LANES, 2 * LANES), 0) // HEAD_DIM
    ones_col = lax.broadcasted_iota(jnp.int32, (2 * LANES, 2 * LANES), 1) // HEAD_DIM
    same_head = jnp.where(ones_row == ones_col, 1.0, 0.0).astype(bf16)
    half = POINTS * deep // 2

    def step(index, carry):
        first = index * POINTS
        for point in range(0, POINTS, 2):
            q = [query[first + point + t] for t in range(2)]
            for slot in range(slots):
                terms = []
                for t in range(2):
                    at = sources[(first + point + t) * slots + slot]
                    terms.append(table[at, :deep, :] * q[t])
                product[slot, point * deep : (point + 2) * deep, :] = jnp.concatenate(terms, 0).astype(bf16)
        live = jnp.concatenate(
            [jnp.full((deep, LANES), counts[first + point], jnp.int32) for point in range(POINTS)], 0
        )
        powers = []
        for slot in range(slots):
            pair = jnp.concatenate([product[slot, :half, :], product[slot, half:, :]], 1)
            score = dot(pair, same_head)
            score = jnp.concatenate([score[:, :LANES], score[:, LANES:]], 0)
            powers.append(jnp.where(live > slot, jnp.exp2(score), 0.0))
        total = powers[0]
        for slot in range(1, slots):
            total = total + powers[slot]
        inverse = 1.0 / total
        weights = [p * inverse for p in powers]
        for point in range(POINTS):
            mixed = None
            for slot in range(slots):
                at = sources[(first + point) * slots + slot]
                term = weights[slot][point * deep : (point + 1) * deep, :] * table[at, deep:, :]
                mixed = term if mixed is None else mixed + term
            query[first + point] = mixed
        return carry

    lax.fori_loop(0, points // POINTS, step, 0)

    width = result.shape[1]
    inner = deep * LANES // 2

    def finish(index, carry):
        at = pl.ds(pl.multiple_of(index * piece, piece), piece)
        block = query[at].reshape(piece, deep * LANES).astype(bf16)
        acc = dot(block[:, :inner], wo_mine[...]) + dot(block[:, inner:], wo_other[...])
        result[at, :] = (grid[at, :].astype(f32)[:, :width] + acc[:, :width]).astype(bf16)
        return carry

    lax.fori_loop(0, points // piece, finish, 0)


def local(
    grid_state,
    hidden_state,
    encoder_sources,
    encoder_counts,
    decoder_sources,
    decoder_counts,
    encoder_keys,
    encoder_values,
    encoder_query,
    encoder_output,
    window_query,
    window_keys,
    window_values,
    window_output,
    feed_up,
    feed_down,
    decoder_query,
    decoder_keys,
    decoder_values,
    decoder_output,
):
    bands, band, core = lax.axis_size("band"), lax.axis_index("band"), lax.axis_index("head")
    cores = lax.axis_size("head")
    grid_count, width = grid_state.shape
    nodes, channels = hidden_state.shape
    rows, points = nodes // cores, grid_count // cores
    full = channels * cores
    heads = full // HEAD_DIM

    def swap(x):
        return lax.ppermute(x, "head", [(0, 1), (1, 0)])

    def pair_swap(x):
        return lax.ppermute(x, "band", [(i, i ^ 1) for i in range(bands)])

    def pass_on(x):
        jumps = [(i, i + 2) for i in range(0, bands - 2, 2)] + [(i, i - 2) for i in range(3, bands, 2)]
        return lax.ppermute(x, "band", jumps)

    def my_part(x, size):
        return lax.dynamic_slice_in_dim(x, core * size, size, 0)

    def wide(x):
        return jnp.pad(x, ((0, LANES - x.shape[0]), (0, 0)))

    even = band % 2 == 0
    near_side = jnp.where(even, 2, 0)
    far_side = 2 - near_side
    info = jnp.stack(
        [
            core,
            band * nodes + core * rows,
            bands * nodes,
            near_side * grid_count + core * points,
            near_side * grid_count + (1 - core) * points,
            far_side * grid_count + core * points,
            far_side * grid_count + (1 - core) * points,
            nodes + core * rows,
            nodes + (1 - core) * rows,
            near_side * nodes + core * rows,
            near_side * nodes + (1 - core) * rows,
            far_side * nodes + core * rows,
            far_side * nodes + (1 - core) * rows,
        ]
    ).astype(jnp.int32)

    my_grid = my_part(grid_state, points)
    grid_cut = points // GRID_CHUNKS
    firsts = [pair_swap(my_grid[chunk * grid_cut : (chunk + 1) * grid_cut]) for chunk in range(GRID_CHUNKS)]

    kept = my_part(hidden_state, rows)
    got = swap(lax.dynamic_slice_in_dim(hidden_state, (1 - core) * rows, rows, 0))
    state = jnp.where(
        core == 0, jnp.concatenate([kept, got], 1), jnp.concatenate([got, kept], 1)
    )

    ek_mine, ev_mine, dq_mine = wide(encoder_keys), wide(encoder_values), wide(decoder_query)
    do_mine = jnp.pad(decoder_output, ((0, 0), (0, LANES - width)))

    my_sources = my_part(encoder_sources, rows).reshape(-1)
    my_counts = my_part(encoder_counts, rows)[:, None]
    dec_sources = (my_part(decoder_sources, points) - (band - 1) * nodes).reshape(-1)
    dec_counts = my_part(decoder_counts, points)
    grid_wide = jnp.pad(my_grid, ((0, 0), (0, LANES - width)))
    early = (info, my_sources, my_counts, dec_sources, dec_counts, grid_wide)

    query, last = pl.pallas_call(
        query_kernel,
        out_shape=(
            jax.ShapeDtypeStruct((heads, rows, LANES), f32),
            jax.ShapeDtypeStruct(firsts[-1].shape, bf16),
        ),
        in_specs=[VMEM] * 5 + [ANY] * (1 + len(early)),
        out_specs=(VMEM, ANY),
        input_output_aliases={5: 1},
        compiler_params=BIG,
        cost_estimate=cost(6 * rows * full * full),
        name="queries",
    )(state, encoder_query, swap(encoder_query), ek_mine, swap(ek_mine), firsts[-1], *early)

    grid_parts, grid_spots = [], []
    for chunk, first in enumerate(firsts[:-1] + [last]):
        second = pass_on(first)
        grid_parts += [first, swap(first), second, swap(second)]
        grid_spots += [(3 + side, chunk * grid_cut) for side in range(4)]

    slots = encoder_sources.shape[1]
    encoder_rows = rows // ENCODER_CHUNKS
    encoder_inputs = (ev_mine, swap(ev_mine), encoder_output, swap(encoder_output))

    def encode(index):
        at = slice(index * encoder_rows, (index + 1) * encoder_rows)
        return pl.pallas_call(
            functools.partial(encoder_kernel, spots=tuple(grid_spots), skip=index * encoder_rows),
            out_shape=jax.ShapeDtypeStruct((encoder_rows, full), bf16),
            in_specs=[SMEM, SMEM] + [VMEM] * (8 + len(grid_spots)),
            out_specs=VMEM,
            scratch_shapes=[pltpu.VMEM((3 * grid_count, LANES), f32)]
            + [pltpu.VMEM((GROUP * slots, LANES), f32) for _ in range(CHAINS)]
            + [pltpu.VMEM((heads, encoder_rows, LANES), f32)],
            compiler_params=BIG,
            cost_estimate=cost(16 * rows * full * full),
            name="encoder",
        )(info, my_sources, my_counts, query, grid_state, *grid_parts, *encoder_inputs, state)

    more = HALF_WIN - rows
    facing = [(2 * i + 1, 2 * i + 2) for i in range(bands - 1)]
    facing = facing + [(b, a) for a, b in facing]
    mids, partners, fars = [], [], []
    for index in range(ENCODER_CHUNKS):
        mids.append(encode(index))
        sent = mids[-1]
        if index == ENCODER_CHUNKS - 1:
            edge = swap(jnp.where(core == 0, mids[-1][encoder_rows - more :], mids[0][:more]))
            sent = jnp.concatenate([sent, edge], 0)
        fars.append(lax.ppermute(sent, ("band", "head"), facing))
        partners.append(swap(mids[-1]))

    pairs = full // LANES
    window_weights = (window_keys, swap(window_keys), window_values, swap(window_values))
    near_count = 2 * rows
    win_query, near_mix, near_sum, token = pl.pallas_call(
        near_window_kernel,
        out_shape=(
            jax.ShapeDtypeStruct((pairs, rows, LANES), bf16),
            jax.ShapeDtypeStruct((pairs, rows, LANES), f32),
            jax.ShapeDtypeStruct((pairs, rows, LANES), f32),
            jax.ShapeDtypeStruct((8, LANES), jnp.int32),
        ),
        in_specs=[SMEM] + [VMEM] * (2 * ENCODER_CHUNKS + 6),
        out_specs=(VMEM,) * 4,
        scratch_shapes=[
            pltpu.VMEM((near_count, full), bf16),
            pltpu.VMEM((pairs, near_count, LANES), bf16),
            pltpu.VMEM((pairs, near_count, LANES), bf16),
            pltpu.VMEM((rows, near_count), f32),
        ],
        compiler_params=BIG,
        cost_estimate=cost(1024),
        name="near_window",
    )(info, *mids, *partners, window_query, swap(window_query), *window_weights)

    near = swap(
        jnp.where(core + token[0, 0] == 0, fars[-1][encoder_rows - more : encoder_rows], fars[0][:more])
    )
    far_count = -(-(rows + 2 * more) // LANES) * LANES
    mix = pl.pallas_call(
        far_window_kernel,
        out_shape=jax.ShapeDtypeStruct((pairs, rows, LANES), bf16),
        in_specs=[SMEM] + [VMEM] * (3 + ENCODER_CHUNKS + 1 + 4),
        out_specs=VMEM,
        scratch_shapes=[
            pltpu.VMEM((far_count, full), bf16),
            pltpu.VMEM((pairs, far_count, LANES), bf16),
            pltpu.VMEM((pairs, far_count, LANES), bf16),
            pltpu.VMEM((rows, far_count), f32),
        ],
        compiler_params=BIG,
        cost_estimate=cost(20 * rows * full * full),
        name="far_window",
    )(info, win_query, near_mix, near_sum, *fars, near, *window_weights)

    units = feed_up.shape[1]
    chunk = min(512, units)
    steps = units // chunk
    whole = lambda shape: pl.BlockSpec(shape, lambda i: (0,) * len(shape))
    cut = rows // FEED_CHUNKS
    weights = (
        window_output, swap(window_output), feed_up, swap(feed_up), feed_down, swap(feed_down),
    )

    def feed(index):
        return pl.pallas_call(
            feed_kernel,
            grid=(2 * steps,),
            out_shape=jax.ShapeDtypeStruct((cut, full), bf16),
            in_specs=[
                pl.BlockSpec((pairs, cut, LANES), lambda i: (0, index, 0)),
                pl.BlockSpec((cut, full), lambda i: (index, 0)),
                whole((channels, full)),
                whole((channels, full)),
                pl.BlockSpec((full, chunk), lambda i: (0, jnp.minimum(i, steps - 1))),
                pl.BlockSpec((full, chunk), lambda i: (0, jnp.maximum(i - steps, 0))),
                pl.BlockSpec((chunk, full), lambda i: (jnp.minimum(i, steps - 1), 0)),
                pl.BlockSpec((chunk, full), lambda i: (jnp.maximum(i - steps, 0), 0)),
            ],
            out_specs=whole((cut, full)),
            scratch_shapes=[
                pltpu.VMEM((cut, full), bf16),
                pltpu.VMEM((cut, full), bf16),
                pltpu.VMEM((cut, full), f32),
            ],
            compiler_params=BIG,
            cost_estimate=cost(2 * cut * full * (full + 4 * units)),
            name="feed",
        )(mix, mids[0], *weights)

    node_parts, node_spots, own_parts, partner_parts = [], [], [], []
    for index in range(FEED_CHUNKS):
        final = feed(index)
        first = pair_swap(final)
        other = swap(final)
        second = pass_on(first)
        own_parts.append(final)
        partner_parts.append(other)
        node_parts += [final, other, first, swap(first), second, swap(second)]
        node_spots += [(7 + side, index * cut) for side in range(6)]

    deep = full // LANES
    decoder_weights = (decoder_keys, swap(decoder_keys), decoder_values, swap(decoder_values))

    def columns(parts):
        return jnp.concatenate(
            [lax.dynamic_slice_in_dim(part, core * channels, channels, 1) for part in parts], 0
        )

    own_columns, partner_columns = columns(own_parts), columns(partner_parts)
    hidden_final = jnp.where(
        core == 0,
        jnp.concatenate([own_columns, partner_columns], 0),
        jnp.concatenate([partner_columns, own_columns], 0),
    )

    dec_slots = decoder_sources.shape[1]
    grid_next = pl.pallas_call(
        functools.partial(decoder_kernel, spots=tuple(node_spots)),
        out_shape=jax.ShapeDtypeStruct((points, width), bf16),
        in_specs=[SMEM] * 3 + [VMEM] * (9 + len(node_spots)),
        out_specs=VMEM,
        scratch_shapes=[
            pltpu.VMEM((3 * nodes, 2 * deep, LANES), f32),
            pltpu.VMEM((points, deep, LANES), f32),
            pltpu.VMEM((dec_slots, POINTS * deep, LANES), bf16),
            pltpu.VMEM((3 * nodes, full), bf16),
        ],
        compiler_params=BIG,
        name="decoder",
    )(
        info, dec_sources, dec_counts, grid_wide, *node_parts,
        dq_mine, swap(dq_mine), *decoder_weights,
        do_mine, swap(do_mine),
    )
    return (grid_next, hidden_final)


def solution(mesh):
    in_specs = (
        P("band", None),
        P("band", "head"),
        P("band", None),
        P("band"),
        P("band", None),
        P("band"),
        P(None, "head"),
        P(None, "head"),
        P(None, "head"),
        P("head", None),
        P(None, "head"),
        P(None, "head"),
        P(None, "head"),
        P("head", None),
        P(None, "head"),
        P("head", None),
        P(None, "head"),
        P(None, "head"),
        P(None, "head"),
        P("head", None),
    )
    out_specs = (P(("band", "head"), None), P("band", "head"))
    return jax.shard_map(local, mesh=mesh, in_specs=in_specs, out_specs=out_specs, check_vma=False)
```

time: 297 us -> 258 us (0.87); the launches traced: 293 us -> 257 us
  waiting for transfers between devices: 81.2 us -> 36.1 us
  Pallas kernels: 146 us -> 162 us
  starting transfers between devices: 41.6 us -> 29.1 us
  local copies, waits for them, and re-layouts: 16.7 us -> 19.9 us
    ppermute x6 -> x9, waiting for transfers between devices: 72.6 us -> 29.1 us  [the longest x4 21 us: pass_on(): return lax.ppermute(x, 'band', jumps)]
    pallas_call x5 -> x7, Pallas kernels: 146 us -> 162 us  [the longest x1 54.8 us: local(): pl.pallas_call(functools.partial(decoder_kernel, spots=tuple(node_spots))...]
    ppermute x6 -> x9, starting transfers between devices: 30.7 us -> 14.8 us  [the longest x4 8.31 us: pass_on(): return lax.ppermute(x, 'band', jumps)]
    ppermute x22 -> x28, starting transfers between devices: 10.9 us -> 14.2 us  [swap(): return lax.ppermute(x, 'head', [(0, 1), (1, 0)])]
    ppermute x22 -> x28, waiting for transfers between devices: 8.56 us -> 7.01 us  [swap(): return lax.ppermute(x, 'head', [(0, 1), (1, 0)])]
    unnamed x63 -> x87, local copies, waits for them, and re-layouts: 7.96 us -> 7.04 us
  transfers between devices with their start and end apart: 28 -> 37, of which waited for: 10 -> 12; matrix products, arithmetic and copies ran while one was open for 6% -> 8% of each run, Pallas kernels for 24% -> 42%
where the time goes in v2:
time: 258 us; the launch traced here: 257 us
  Pallas kernels  162 us (63%)
  waiting for transfers between devices  36.1 us (14%)
  starting transfers between devices  29.1 us (11%)
  local copies, waits for them, and re-layouts  19.9 us (8%)
  other arithmetic  7.91 us (3%)
    pallas_call x1, Pallas kernels, local(): pl.pallas_call(functools.partial(decoder_kernel, spots=tuple(node_spots))...  54.8 us
    pallas_call x1, Pallas kernels, encode(): pl.pallas_call(functools.partial(encoder_kernel, spots=tuple(grid_spots),...  29.8 us
    pallas_call x2, Pallas kernels, feed(): pl.pallas_call(feed_kernel, grid=(2 * steps,), out_shape=jax.ShapeDtypeSt...  28.9 us
    pallas_call x1, Pallas kernels, local(): pl.pallas_call(near_window_kernel, out_shape=(jax.ShapeDtypeStruct((pairs...  24.3 us
    ppermute x4, waiting for transfers between devices, pass_on(): return lax.ppermute(x, 'band', jumps)  21 us
    pallas_call x1, Pallas kernels, local(): pl.pallas_call(far_window_kernel, out_shape=jax.ShapeDtypeStruct((pairs,...  17.9 us
    ppermute x28, starting transfers between devices, swap(): return lax.ppermute(x, 'head', [(0, 1), (1, 0)])  14.2 us
    ppermute x4, starting transfers between devices, pass_on(): return lax.ppermute(x, 'band', jumps)  8.31 us
  transfers between devices with their start and end apart: 37, of which 12 were waited for; matrix products, arithmetic and copies ran while one was open for 8% of the time, Pallas kernels for 42%

profile of v2, /device:TPU:23, one launch (start us, length us, event | category | flops | bytes accessed | tf_op | source)
XLA Modules:
  0.0 256.8 jit_solution(6586681209994223076)
XLA Ops:
  1.4 2.1 constant_dynamic-slice_fusion.7
  7.4 1.1 copy.27
  8.5 1.2 reshape.10.refs_3_.sources
  9.8 1.3 collective-permute-start.4
  16.5 2.5 maximum_select_fusion.state.refs_12_
  19.6 2.1 collective-permute-start.6
  22.1 6.3 %queries.1 = (f32[16,512,128]{2,1,0:T(8,128)}, bf16[1024,100]{1,0:T(8,128)(2,1)}) custom-call(bf16[512,1024]{1,0:T(8,128)(2,1)} %maximum_select_fusion.state.refs_12_, bf16[1024,512]{1,0:T(8,128)(2,1)} %wq_mine.1, bf16[1024,512]{1,0:T(8,128)(2,1)} %collective-permute-done.1.wq_other, ...), custom_call_target="tpu_custom_call", output_to_operand_aliasing={{1}: (5, {})} | custom-call | flops 3221225472 | bytes 12582912 | tf_op jit(solution)/shard_map/queries/pallas_call | solution.py:493
  28.5 1.7 collective-permute-done.6.refs_2_
  31.1 1.9 collective-permute-start.9
  33.1 8.9 %collective-permute-done.9.refs_6_ = bf16[1024,100]{1,0:T(8,128)(2,1)S(1)} collective-permute-done((bf16[1024,100]{1,0:T(8,128)(2,1)}, bf16[1024,100]{1,0:T(8,128)(2,1)S(1)}, u32[]{:S(2)}, u32[]{:S(2)}) %collective-permute-start.9) | collective-permute-done | bytes 204832 | tf_op jit(solution)/shard_map/ppermute | solution.py:444
  44.7 29.8 %encoder.1.refs_0_.mid = bf16[512,1024]{1,0:T(8,128)(2,1)} custom-call(s32[13]{0:T(128)} %stack.51.refs_0_.info, s32[16384]{0:T(1024)} %reshape.11.refs_1_.sources, s32[512,1]{1,0:T(8,128)} %copy.31.refs_2_.counts, f32[16,512,128]{2,1,0:T(8,128)} %get-tuple-element.8.query, bf16[4096,100]{1,0:T(8,128)(2,1)} %copy-done.3, bf16[1024,100]{1,0:T(8,128)(2,1)} %copy-done.33, ...), custom_call_target="tpu_custom_call" | custom-call | flops 8589934592 | bytes 33554432 | tf_op jit(solution)/shard_map/encoder/pallas_call | solution.py:519
  74.5 1.1 slice_select_fusion.1
  77.0 1.3 pad_maximum_fusion
  78.3 3.7 %collective-permute-start.18 = (bf16[560,1024]{1,0:T(8,128)(2,1)S(1)}, bf16[560,1024]{1,0:T(8,128)(2,1)}, u32[]{:S(2)}, u32[]{:S(2)}) collective-permute-start(bf16[560,1024]{1,0:T(8,128)(2,1)S(1)} %pad_maximum_fusion), channel_id=1, source_target_pairs={{1,2},{3,4},{5,6},{7,8},{9,10},{11,12},{13,14},{15,16},{17,18},{19... | collective-permute-start | bytes 3440648 | tf_op jit(solution)/shard_map/ppermute | solution.py:542
  82.6 2.6 %collective-permute-done.14.refs_3_ = bf16[1024,512]{1,0:T(8,128)(2,1)S(1)} collective-permute-done((bf16[1024,512]{1,0:T(8,128)(2,1)S(1)}, bf16[1024,512]{1,0:T(8,128)(2,1)S(1)}, u32[]{:S(2)}, u32[]{:S(2)}) %collective-permute-start.14) | collective-permute-done | bytes 1048608 | tf_op jit(solution)/shard_map/ppermute | solution.py:437
  85.2 1.1 collective-permute-done.13.refs_1_
  86.3 24.3 %near_window.1 = (bf16[8,512,128]{2,1,0:T(8,128)(2,1)}, f32[8,512,128]{2,1,0:T(8,128)}, f32[8,512,128]{2,1,0:T(8,128)}, s32[8,128]{1,0:T(8,128)}) custom-call(s32[13]{0:T(128)} %stack.51.refs_0_.info, bf16[512,1024]{1,0:T(8,128)(2,1)} %encoder.1.refs_0_.mid, bf16[512,1024]{1,0:T(8,128)(2,1)} %collective-permute-done.13.refs_1_, bf16[1024,512]{1,0:T(8,128)(2,1)} %refs_2_.2, ...), custom_call_target="tpu_custom_call" | custom-call | flops 1024 | bytes 4 | tf_op jit(solution)/shard_map/near_window/pallas_call | solution.py:548
  110.7 1.2 slice.25
  115.5 17.9 %far_window.1.mix = bf16[8,512,128]{2,1,0:T(8,128)(2,1)} custom-call(s32[13]{0:T(128)} %stack.51.refs_0_.info, bf16[8,512,128]{2,1,0:T(8,128)(2,1)} %get-tuple-element.10.query, f32[8,512,128]{2,1,0:T(8,128)} %get-tuple-element.11.near_mix, f32[8,512,128]{2,1,0:T(8,128)} %get-tuple-element.12.near_total, bf16[560,1024]{1,0:T(8,128)(2,1)} %collective-permute-done.18.refs_0_, ...), custom_call_target="tpu_custom_call" | custom-call | flops 10737418240 | bytes 41943040 | tf_op jit(solution)/shard_map/far_window/pallas_call | solution.py:573
  134.3 14.4 %feed.3.refs_6_ = bf16[256,1024]{1,0:T(8,128)(2,1)} custom-call(bf16[8,512,128]{2,1,0:T(8,128)(2,1)} %far_window.1.mix, bf16[512,1024]{1,0:T(8,128)(2,1)} %encoder.1.refs_0_.mid, bf16[512,1024]{1,0:T(8,128)(2,1)} %wo_mine.3, bf16[512,1024]{1,0:T(8,128)(2,1)} %copy-done.5, bf16[1024,2048]{1,0:T(8,128)(2,1)} %up_mine.3, ...), custom_call_target="tpu_custom_call" | custom-call | flops 4831838208 | bytes 18874368 | tf_op jit(solution)/shard_map/feed/pallas_call | solution.py:599
  149.0 14.6 %feed.2.refs_0_ = bf16[256,1024]{1,0:T(8,128)(2,1)} custom-call(bf16[8,512,128]{2,1,0:T(8,128)(2,1)} %far_window.1.mix, bf16[512,1024]{1,0:T(8,128)(2,1)} %encoder.1.refs_0_.mid, bf16[512,1024]{1,0:T(8,128)(2,1)} %wo_mine.3, bf16[512,1024]{1,0:T(8,128)(2,1)} %copy-done.5, bf16[1024,2048]{1,0:T(8,128)(2,1)} %up_mine.3, ...), custom_call_target="tpu_custom_call" | custom-call | flops 4831838208 | bytes 18874368 | tf_op jit(solution)/shard_map/feed/pallas_call | solution.py:599
  167.2 1.9 collective-permute-start.31
  169.1 8.1 %collective-permute-done.24.refs_2_ = bf16[256,1024]{1,0:T(8,128)(2,1)} collective-permute-done((bf16[256,1024]{1,0:T(8,128)(2,1)}, bf16[256,1024]{1,0:T(8,128)(2,1)}, u32[]{:S(2)}, u32[]{:S(2)}) %collective-permute-start.24) | collective-permute-done | bytes 524320 | tf_op jit(solution)/shard_map/ppermute | solution.py:440
  177.2 2.4 collective-permute-start.26
  179.6 1.9 collective-permute-start.35
  182.0 1.1 collective-permute-done.31.refs_10_
  183.1 2.0 collective-permute-start.32
  185.1 9.3 %collective-permute-done.26.refs_4_ = bf16[256,1024]{1,0:T(8,128)(2,1)S(1)} collective-permute-done((bf16[256,1024]{1,0:T(8,128)(2,1)}, bf16[256,1024]{1,0:T(8,128)(2,1)S(1)}, u32[]{:S(2)}, u32[]{:S(2)}) %collective-permute-start.26) | collective-permute-done | bytes 524320 | tf_op jit(solution)/shard_map/ppermute | solution.py:444
  194.3 1.2 collective-permute-start.27
  196.6 1.4 maximum_select_fusion.1
  200.0 54.8 %decoder.1 = bf16[2048,100]{1,0:T(8,128)(2,1)} custom-call(s32[13]{0:T(128)} %stack.51.refs_0_.info, s32[8192]{0:T(1024)} %reshape.10.refs_3_.sources, s32[2048]{0:T(1024)} %dynamic_slice.34.refs_4_.counts, bf16[2048,128]{1,0:T(8,128)(2,1)} %pad.18.refs_5_.grid, bf16[256,1024]{1,0:T(8,128)(2,1)} %feed.2.refs_0_, bf16[256,1024]{1,0:T(8,128)(2,1)} %copy-done.8, ...), custom_call_target="tpu_custom_call" | custom-call | tf_op jit(solution)/shard_map/decoder/pallas_call | solution.py:651
  254.8 2.1 copy.34
  (163 shorter events, 27.8 us)
Async XLA Ops:
  0.7 21.1 %collective-permute-start.1 = (bf16[1024,512]{1,0:T(8,128)(2,1)}, bf16[1024,512]{1,0:T(8,128)(2,1)}, u32[]{:S(2)}, u32[]{:S(2)}) collective-permute-start(bf16[1024,512]{1,0:T(8,128)(2,1)} %wq_mine.1), channel_id=1, source_target_pairs={{0,1},{1,0},{2,3},{3,2},{4,5},{5,4},{6,7},{7,6},{8,9},{9,8},{10,11... | collective-permute-start | bytes 3145736 | tf_op jit(solution)/shard_map/ppermute | solution.py:437
  3.5 12.2 %collective-permute-start = (bf16[512,512]{1,0:T(8,128)(2,1)}, bf16[512,512]{1,0:T(8,128)(2,1)}, u32[]{:S(2)}, u32[]{:S(2)}) collective-permute-start(bf16[512,512]{1,0:T(8,128)(2,1)} %get-tuple-element.21), channel_id=1, source_target_pairs={{0,1},{1,0},{2,3},{3,2},{4,5},{5,4},{6,7},{7,6},{8,9},{9,8},{10,11... | collective-permute-start | bytes 1572872 | tf_op jit(solution)/shard_map/ppermute | solution.py:437
  5.1 14.0 %collective-permute-start.3 = (bf16[1024,100]{1,0:T(8,128)(2,1)}, bf16[1024,100]{1,0:T(8,128)(2,1)}, u32[]{:S(2)}, u32[]{:S(2)}) collective-permute-start(bf16[1024,100]{1,0:T(8,128)(2,1)} %get-tuple-element.19), channel_id=1, source_target_pairs={{0,2},{2,0},{4,6},{6,4},{8,10},{10,8},{12,14},{14,12},{16,18},{18,... | collective-permute-start | bytes 614408 | tf_op jit(solution)/shard_map/ppermute | solution.py:440
  6.0 3.8 %collective-permute-start.2 = (bf16[128,512]{1,0:T(8,128)(2,1)}, bf16[128,512]{1,0:T(8,128)(2,1)}, u32[]{:S(2)}, u32[]{:S(2)}) collective-permute-start(bf16[128,512]{1,0:T(8,128)(2,1)} %pad.19.keys_mine), channel_id=1, source_target_pairs={{0,1},{1,0},{2,3},{3,2},{4,5},{5,4},{6,7},{7,6},{8,9},{9,8},{10,11... | collective-permute-start | bytes 393224 | tf_op jit(solution)/shard_map/ppermute | solution.py:437
  6.7 36.1 %collective-permute-start.12 = (bf16[512,1024]{1,0:T(8,128)(2,1)}, bf16[512,1024]{1,0:T(8,128)(2,1)}, u32[]{:S(2)}, u32[]{:S(2)}) collective-permute-start(bf16[512,1024]{1,0:T(8,128)(2,1)} %refs_10_.1), channel_id=1, source_target_pairs={{0,1},{1,0},{2,3},{3,2},{4,5},{5,4},{6,7},{7,6},{8,9},{9,8},{10,11... | collective-permute-start | bytes 3145736 | tf_op jit(solution)/shard_map/ppermute | solution.py:437
  9.8 9.8 %collective-permute-start.4 = (bf16[1024,100]{1,0:T(8,128)(2,1)S(1)}, bf16[1024,100]{1,0:T(8,128)(2,1)S(1)}, u32[]{:S(2)}, u32[]{:S(2)}) collective-permute-start(bf16[1024,100]{1,0:T(8,128)(2,1)S(1)} %get-tuple-element.18), channel_id=1, source_target_pairs={{0,2},{2,0},{4,6},{6,4},{8,10},{10,8},{12,14},{14,12},{16,18},{18,... | collective-permute-start | bytes 614408 | tf_op jit(solution)/shard_map/ppermute | solution.py:440
  15.7 3.3 %collective-permute-start.11 = (bf16[128,512]{1,0:T(8,128)(2,1)S(1)}, bf16[128,512]{1,0:T(8,128)(2,1)S(1)}, u32[]{:S(2)}, u32[]{:S(2)}) collective-permute-start(bf16[128,512]{1,0:T(8,128)(2,1)S(1)} %pad.20.refs_8_), channel_id=1, source_target_pairs={{0,1},{1,0},{2,3},{3,2},{4,5},{5,4},{6,7},{7,6},{8,9},{9,8},{10,11... | collective-permute-start | bytes 393224 | tf_op jit(solution)/shard_map/ppermute | solution.py:437
  19.0 114.4 %collective-permute-start.21 = (bf16[1024,2048]{1,0:T(8,128)(2,1)}, bf16[1024,2048]{1,0:T(8,128)(2,1)}, u32[]{:S(2)}, u32[]{:S(2)}) collective-permute-start(bf16[1024,2048]{1,0:T(8,128)(2,1)} %up_mine.3), channel_id=1, source_target_pairs={{0,1},{1,0},{2,3},{3,2},{4,5},{5,4},{6,7},{7,6},{8,9},{9,8},{10,11... | collective-permute-start | bytes 12582920 | tf_op jit(solution)/shard_map/ppermute | solution.py:437
  19.1 114.3 %collective-permute-start.22 = (bf16[2048,1024]{1,0:T(8,128)(2,1)}, bf16[2048,1024]{1,0:T(8,128)(2,1)}, u32[]{:S(2)}, u32[]{:S(2)}) collective-permute-start(bf16[2048,1024]{1,0:T(8,128)(2,1)} %down_mine.3), channel_id=1, source_target_pairs={{0,1},{1,0},{2,3},{3,2},{4,5},{5,4},{6,7},{7,6},{8,9},{9,8},{10,11... | collective-permute-start | bytes 12582920 | tf_op jit(solution)/shard_map/ppermute | solution.py:437
  19.6 10.7 %collective-permute-start.6 = (bf16[1024,100]{1,0:T(8,128)(2,1)S(1)}, bf16[1024,100]{1,0:T(8,128)(2,1)S(1)}, u32[]{:S(2)}, u32[]{:S(2)}) collective-permute-start(bf16[1024,100]{1,0:T(8,128)(2,1)S(1)} %collective-permute-done.4.refs_0_), channel_id=1, source_target_pairs={{0,4},{4,8},{8,12},{12,16},{16,20},{20,24},{24,28},{6,2},{10,6},{1... | collective-permute-start | bytes 614408 | tf_op jit(solution)/shard_map/ppermute | solution.py:444
  21.7 9.4 %collective-permute-start.5 = (bf16[1024,100]{1,0:T(8,128)(2,1)S(1)}, bf16[1024,100]{1,0:T(8,128)(2,1)S(1)}, u32[]{:S(2)}, u32[]{:S(2)}) collective-permute-start(bf16[1024,100]{1,0:T(8,128)(2,1)S(1)} %collective-permute-done.4.refs_0_), channel_id=1, source_target_pairs={{0,1},{1,0},{2,3},{3,2},{4,5},{5,4},{6,7},{7,6},{8,9},{9,8},{10,11... | collective-permute-start | bytes 614408 | tf_op jit(solution)/shard_map/ppermute | solution.py:437
  30.2 2.8 %collective-permute-start.7 = (bf16[1024,100]{1,0:T(8,128)(2,1)S(1)}, bf16[1024,100]{1,0:T(8,128)(2,1)S(1)}, u32[]{:S(2)}, u32[]{:S(2)}) collective-permute-start(bf16[1024,100]{1,0:T(8,128)(2,1)S(1)} %collective-permute-done.6.refs_2_), channel_id=1, source_target_pairs={{0,1},{1,0},{2,3},{3,2},{4,5},{5,4},{6,7},{7,6},{8,9},{9,8},{10,11... | collective-permute-start | bytes 614408 | tf_op jit(solution)/shard_map/ppermute | solution.py:437
  31.1 10.9 %collective-permute-start.9 = (bf16[1024,100]{1,0:T(8,128)(2,1)}, bf16[1024,100]{1,0:T(8,128)(2,1)S(1)}, u32[]{:S(2)}, u32[]{:S(2)}) collective-permute-start(bf16[1024,100]{1,0:T(8,128)(2,1)} %get-tuple-element.9.refs_4_), channel_id=1, source_target_pairs={{0,4},{4,8},{8,12},{12,16},{16,20},{20,24},{24,28},{6,2},{10,6},{1... | collective-permute-start | bytes 614408 | tf_op jit(solution)/shard_map/ppermute | solution.py:444
  33.0 9.9 %collective-permute-start.8 = (bf16[1024,100]{1,0:T(8,128)(2,1)}, bf16[1024,100]{1,0:T(8,128)(2,1)S(1)}, u32[]{:S(2)}, u32[]{:S(2)}) collective-permute-start(bf16[1024,100]{1,0:T(8,128)(2,1)} %get-tuple-element.9.refs_4_), channel_id=1, source_target_pairs={{0,1},{1,0},{2,3},{3,2},{4,5},{5,4},{6,7},{7,6},{8,9},{9,8},{10,11... | collective-permute-start | bytes 614408 | tf_op jit(solution)/shard_map/ppermute | solution.py:437
  42.8 39.2 %collective-permute-start.15 = (bf16[1024,512]{1,0:T(8,128)(2,1)S(1)}, bf16[1024,512]{1,0:T(8,128)(2,1)}, u32[]{:S(2)}, u32[]{:S(2)}) collective-permute-start(bf16[1024,512]{1,0:T(8,128)(2,1)S(1)} %copy-done.10), channel_id=1, source_target_pairs={{0,1},{1,0},{2,3},{3,2},{4,5},{5,4},{6,7},{7,6},{8,9},{9,8},{10,11... | collective-permute-start | bytes 3145736 | tf_op jit(solution)/shard_map/ppermute | solution.py:437
  42.9 39.2 %collective-permute-start.16 = (bf16[1024,512]{1,0:T(8,128)(2,1)}, bf16[1024,512]{1,0:T(8,128)(2,1)}, u32[]{:S(2)}, u32[]{:S(2)}) collective-permute-start(bf16[1024,512]{1,0:T(8,128)(2,1)} %refs_4_.3), channel_id=1, source_target_pairs={{0,1},{1,0},{2,3},{3,2},{4,5},{5,4},{6,7},{7,6},{8,9},{9,8},{10,11... | collective-permute-start | bytes 3145736 | tf_op jit(solution)/shard_map/ppermute | solution.py:437
  78.3 34.2 %collective-permute-start.18 = (bf16[560,1024]{1,0:T(8,128)(2,1)S(1)}, bf16[560,1024]{1,0:T(8,128)(2,1)}, u32[]{:S(2)}, u32[]{:S(2)}) collective-permute-start(bf16[560,1024]{1,0:T(8,128)(2,1)S(1)} %pad_maximum_fusion), channel_id=1, source_target_pairs={{1,2},{3,4},{5,6},{7,8},{9,10},{11,12},{13,14},{15,16},{17,18},{19... | collective-permute-start | bytes 3440648 | tf_op jit(solution)/shard_map/ppermute | solution.py:542
  82.0 3.2 %collective-permute-start.14 = (bf16[1024,512]{1,0:T(8,128)(2,1)S(1)}, bf16[1024,512]{1,0:T(8,128)(2,1)S(1)}, u32[]{:S(2)}, u32[]{:S(2)}) collective-permute-start(bf16[1024,512]{1,0:T(8,128)(2,1)S(1)} %copy-done.9), channel_id=1, source_target_pairs={{0,1},{1,0},{2,3},{3,2},{4,5},{5,4},{6,7},{7,6},{8,9},{9,8},{10,11... | collective-permute-start | bytes 3145736 | tf_op jit(solution)/shard_map/ppermute | solution.py:437
  82.1 4.3 %collective-permute-start.13 = (bf16[512,1024]{1,0:T(8,128)(2,1)S(1)}, bf16[512,1024]{1,0:T(8,128)(2,1)}, u32[]{:S(2)}, u32[]{:S(2)}) collective-permute-start(bf16[512,1024]{1,0:T(8,128)(2,1)S(1)} %copy-done.2), channel_id=1, source_target_pairs={{0,1},{1,0},{2,3},{3,2},{4,5},{5,4},{6,7},{7,6},{8,9},{9,8},{10,11... | collective-permute-start | bytes 3145736 | tf_op jit(solution)/shard_map/ppermute | solution.py:437
  113.7 19.7 %collective-permute-start.20 = (bf16[512,1024]{1,0:T(8,128)(2,1)S(1)}, bf16[512,1024]{1,0:T(8,128)(2,1)S(1)}, u32[]{:S(2)}, u32[]{:S(2)}) collective-permute-start(bf16[512,1024]{1,0:T(8,128)(2,1)S(1)} %copy-done.4), channel_id=1, source_target_pairs={{0,1},{1,0},{2,3},{3,2},{4,5},{5,4},{6,7},{7,6},{8,9},{9,8},{10,11... | collective-permute-start | bytes 3145736 | tf_op jit(solution)/shard_map/ppermute | solution.py:437
  114.1 65.5 %collective-permute-start.34 = (bf16[1024,512]{1,0:T(8,128)(2,1)}, bf16[1024,512]{1,0:T(8,128)(2,1)S(1)}, u32[]{:S(2)}, u32[]{:S(2)}) collective-permute-start(bf16[1024,512]{1,0:T(8,128)(2,1)} %refs_14_.1), channel_id=1, source_target_pairs={{0,1},{1,0},{2,3},{3,2},{4,5},{5,4},{6,7},{7,6},{8,9},{9,8},{10,11... | collective-permute-start | bytes 3145736 | tf_op jit(solution)/shard_map/ppermute | solution.py:437
  148.7 18.5 %collective-permute-start.29 = (bf16[256,1024]{1,0:T(8,128)(2,1)}, bf16[256,1024]{1,0:T(8,128)(2,1)S(1)}, u32[]{:S(2)}, u32[]{:S(2)}) collective-permute-start(bf16[256,1024]{1,0:T(8,128)(2,1)} %feed.3.refs_6_), channel_id=1, source_target_pairs={{0,2},{2,0},{4,6},{6,4},{8,10},{10,8},{12,14},{14,12},{16,18},{18,... | collective-permute-start | bytes 1572872 | tf_op jit(solution)/shard_map/ppermute | solution.py:440
  163.6 13.6 %collective-permute-start.24 = (bf16[256,1024]{1,0:T(8,128)(2,1)}, bf16[256,1024]{1,0:T(8,128)(2,1)}, u32[]{:S(2)}, u32[]{:S(2)}) collective-permute-start(bf16[256,1024]{1,0:T(8,128)(2,1)} %feed.2.refs_0_), channel_id=1, source_target_pairs={{0,2},{2,0},{4,6},{6,4},{8,10},{10,8},{12,14},{14,12},{16,18},{18,... | collective-permute-start | bytes 1572872 | tf_op jit(solution)/shard_map/ppermute | solution.py:440
  166.6 14.9 %collective-permute-start.28 = (bf16[256,1024]{1,0:T(8,128)(2,1)S(1)}, bf16[256,1024]{1,0:T(8,128)(2,1)S(1)}, u32[]{:S(2)}, u32[]{:S(2)}) collective-permute-start(bf16[256,1024]{1,0:T(8,128)(2,1)S(1)} %copy-done.6), channel_id=1, source_target_pairs={{0,1},{1,0},{2,3},{3,2},{4,5},{5,4},{6,7},{7,6},{8,9},{9,8},{10,11... | collective-permute-start | bytes 1572872 | tf_op jit(solution)/shard_map/ppermute | solution.py:437
  167.0 14.5 %collective-permute-start.23 = (bf16[256,1024]{1,0:T(8,128)(2,1)}, bf16[256,1024]{1,0:T(8,128)(2,1)S(1)}, u32[]{:S(2)}, u32[]{:S(2)}) collective-permute-start(bf16[256,1024]{1,0:T(8,128)(2,1)} %feed.2.refs_0_), channel_id=1, source_target_pairs={{0,1},{1,0},{2,3},{3,2},{4,5},{5,4},{6,7},{7,6},{8,9},{9,8},{10,11... | collective-permute-start | bytes 1572872 | tf_op jit(solution)/shard_map/ppermute | solution.py:437
  167.2 15.9 %collective-permute-start.31 = (bf16[256,1024]{1,0:T(8,128)(2,1)S(1)}, bf16[256,1024]{1,0:T(8,128)(2,1)S(1)}, u32[]{:S(2)}, u32[]{:S(2)}) collective-permute-start(bf16[256,1024]{1,0:T(8,128)(2,1)S(1)} %collective-permute-done.29.refs_8_), channel_id=1, source_target_pairs={{0,4},{4,8},{8,12},{12,16},{16,20},{20,24},{24,28},{6,2},{10,6},{1... | collective-permute-start | bytes 1572872 | tf_op jit(solution)/shard_map/ppermute | solution.py:444
  177.2 17.1 %collective-permute-start.26 = (bf16[256,1024]{1,0:T(8,128)(2,1)}, bf16[256,1024]{1,0:T(8,128)(2,1)S(1)}, u32[]{:S(2)}, u32[]{:S(2)}) collective-permute-start(bf16[256,1024]{1,0:T(8,128)(2,1)} %collective-permute-done.24.refs_2_), channel_id=1, source_target_pairs={{0,4},{4,8},{8,12},{12,16},{16,20},{20,24},{24,28},{6,2},{10,6},{1... | collective-permute-start | bytes 1572872 | tf_op jit(solution)/shard_map/ppermute | solution.py:444
  179.6 18.5 %collective-permute-start.35 = (bf16[1024,512]{1,0:T(8,128)(2,1)S(1)}, bf16[1024,512]{1,0:T(8,128)(2,1)S(1)}, u32[]{:S(2)}, u32[]{:S(2)}) collective-permute-start(bf16[1024,512]{1,0:T(8,128)(2,1)S(1)} %copy-done.12), channel_id=1, source_target_pairs={{0,1},{1,0},{2,3},{3,2},{4,5},{5,4},{6,7},{7,6},{8,9},{9,8},{10,11... | collective-permute-start | bytes 3145736 | tf_op jit(solution)/shard_map/ppermute | solution.py:437
  181.5 16.7 %collective-permute-start.30 = (bf16[256,1024]{1,0:T(8,128)(2,1)S(1)}, bf16[256,1024]{1,0:T(8,128)(2,1)S(1)}, u32[]{:S(2)}, u32[]{:S(2)}) collective-permute-start(bf16[256,1024]{1,0:T(8,128)(2,1)S(1)} %collective-permute-done.29.refs_8_), channel_id=1, source_target_pairs={{0,1},{1,0},{2,3},{3,2},{4,5},{5,4},{6,7},{7,6},{8,9},{9,8},{10,11... | collective-permute-start | bytes 1572872 | tf_op jit(solution)/shard_map/ppermute | solution.py:437
  181.6 16.6 %collective-permute-start.25 = (bf16[256,1024]{1,0:T(8,128)(2,1)}, bf16[256,1024]{1,0:T(8,128)(2,1)S(1)}, u32[]{:S(2)}, u32[]{:S(2)}) collective-permute-start(bf16[256,1024]{1,0:T(8,128)(2,1)} %collective-permute-done.24.refs_2_), channel_id=1, source_target_pairs={{0,1},{1,0},{2,3},{3,2},{4,5},{5,4},{6,7},{7,6},{8,9},{9,8},{10,11... | collective-permute-start | bytes 1572872 | tf_op jit(solution)/shard_map/ppermute | solution.py:437
  183.1 15.1 %collective-permute-start.32 = (bf16[256,1024]{1,0:T(8,128)(2,1)S(1)}, bf16[256,1024]{1,0:T(8,128)(2,1)S(1)}, u32[]{:S(2)}, u32[]{:S(2)}) collective-permute-start(bf16[256,1024]{1,0:T(8,128)(2,1)S(1)} %collective-permute-done.31.refs_10_), channel_id=1, source_target_pairs={{0,1},{1,0},{2,3},{3,2},{4,5},{5,4},{6,7},{7,6},{8,9},{9,8},{10,11... | collective-permute-start | bytes 1572872 | tf_op jit(solution)/shard_map/ppermute | solution.py:437
  194.3 5.6 %collective-permute-start.27 = (bf16[256,1024]{1,0:T(8,128)(2,1)S(1)}, bf16[256,1024]{1,0:T(8,128)(2,1)}, u32[]{:S(2)}, u32[]{:S(2)}) collective-permute-start(bf16[256,1024]{1,0:T(8,128)(2,1)S(1)} %collective-permute-done.26.refs_4_), channel_id=1, source_target_pairs={{0,1},{1,0},{2,3},{3,2},{4,5},{5,4},{6,7},{7,6},{8,9},{9,8},{10,11... | collective-permute-start | bytes 1572872 | tf_op jit(solution)/shard_map/ppermute | solution.py:437
  (47 other events, 568.9 us)

commit v3 on v2

--- a/solution.py
+++ b/solution.py
@@ -58,21 +58,20 @@
                 one = jnp.where(low if sub == 0 else ~low, two, jnp.zeros_like(two))
                 out[(side * pairs + pair) * 2 + sub] = (
                     lax.dot_general(one, weight, ROWS_BY_ROWS, preferred_element_type=f32) * SCALE
-                )
+                ).astype(bf16)
 
 
 GRID_CHUNKS = 2
-ENCODER_CHUNKS = 1
 GROUP = 8
 CHAINS = 4
 
 
 def encoder_kernel(
-    info, sources, counts, query, own, *refs, spots, skip,
+    info, sources, counts, query, own, *refs, spots,
 ):
     near, refs = refs[: len(spots)], refs[len(spots) :]
-    values_mine, values_other, out_mine, out_other, state, result, table = refs[:7]
-    picked, mix = refs[7:-1], refs[-1]
+    values_mine, values_other, out_mine, out_other, state, result, normed, table = refs[:8]
+    picked, mix = refs[8:-1], refs[-1]
     grid_count, width = own.shape
     heads = query.shape[0]
     rows = result.shape[0]
@@ -94,14 +93,15 @@
         groups = [index * CHAINS + chain for chain in range(CHAINS)]
         starts = [pl.multiple_of(group * GROUP, GROUP) for group in groups]
         for group, rows_ref in zip(groups, picked):
-            base = group * span + skip * slots
+            base = group * span
             for s in range(span):
                 rows_ref[s : s + 1, :] = table[pl.ds(sources[base + s], 1), :]
         grids = [ref[...].astype(bf16) for ref in picked]
-        live = [(slot >= 0) & (slot < counts[pl.ds(start + skip, GROUP), :]) for start in starts]
+        live = [(slot >= 0) & (slot < counts[pl.ds(start, GROUP), :]) for start in starts]
+        asked = query[:, pl.ds(pl.multiple_of(index * (CHAINS * GROUP), 16), CHAINS * GROUP), :].astype(f32)
         queries = [
-            query[:, pl.ds(start + skip, GROUP), :].reshape(heads * GROUP, LANES).astype(bf16)
-            for start in starts
+            asked[:, chain * GROUP : (chain + 1) * GROUP, :].reshape(heads * GROUP, LANES).astype(bf16)
+            for chain in range(CHAINS)
         ]
         scores = [
             lax.dot_general(q, g, ROWS_BY_ROWS, preferred_element_type=f32)
@@ -122,7 +122,7 @@
     lax.fori_loop(0, rows // (GROUP * CHAINS), step, 0)
 
     pairs = values_mine.shape[1] // LANES
-    total = state[skip : skip + rows, :].astype(f32)
+    total = state[...].astype(f32)
     for side, (values, out) in enumerate(((values_mine, out_mine), (values_other, out_other))):
         parts = []
         for pair in range(pairs):
@@ -136,11 +136,12 @@
             parts.append(dot(two, both).astype(bf16))
         total = total + dot(jnp.concatenate(parts, 1), out[...])
     result[...] = total.astype(bf16)
+    normed[...] = layer_norm(result[...])
 
 
 def lay(start, block, refs):
     for ref in refs:
-        block[start : start + ref.shape[0], :] = layer_norm(ref[...])
+        block[start : start + ref.shape[0], :] = ref[...]
         start += ref.shape[0]
     return start
 
@@ -282,16 +283,17 @@
     attend(query, key, value, bias, rows, finish)
 
 
-def feed_kernel(mix, mid, wo_mine, wo_other, up_mine, up_other, down_mine, down_other, result, att, normed, total):
+def feed_kernel(mix, mid, wo_mine, wo_other, up_mine, up_other, down_mine, down_other, result, passed, att, normed, total, *, start):
     index = pl.program_id(0)
     half = pl.num_programs(0) // 2
 
     @pl.when(index == 0)
     def _():
         pairs = wo_mine.shape[0] // LANES
-        acc = mid[...].astype(f32)
+        at = slice(start, start + result.shape[0])
+        acc = mid[at, :].astype(f32)
         for side, wo in enumerate((wo_mine, wo_other)):
-            block = jnp.concatenate([mix[side * pairs + pair] for pair in range(pairs)], 1)
+            block = jnp.concatenate([mix[side * pairs + pair, at, :] for pair in range(pairs)], 1)
             acc = acc + dot(block, wo[...])
         att[...] = acc.astype(bf16)
         normed[...] = layer_norm(att[...])
@@ -312,34 +314,42 @@
     @pl.when(index == 2 * half - 1)
     def _():
         result[...] = total[...].astype(bf16)
+        passed[...] = layer_norm(result[...])
+
+
+def hold_kernel(*refs):
+    del refs
 
 
 POINTS = 32
-FEED_CHUNKS = 2
 
 
 def decoder_kernel(info, sources, counts, grid, *refs, spots):
     nodes_in, refs = refs[: len(spots)], refs[len(spots) :]
-    wq_mine, wq_other, wk_mine, wk_other, wv_mine, wv_other, wo_mine, wo_other = refs[:8]
-    result, table, query, product, gathered = refs[8:]
+    wq_mine, wq_other, wo_mine, wo_other = refs[0], refs[1], refs[6], refs[7]
+    result, table, query, product, gathered, weights, arrived, loaded = refs[8:]
     deep = query.shape[1]
     points = grid.shape[0]
     slots = sources.shape[0] // points
     piece = 256
 
-    for ref, (place, offset) in zip(nodes_in, spots):
-        gathered[pl.ds(pl.multiple_of(info[place] + offset, 16), ref.shape[0]), :] = ref[...]
+    copies = [
+        pltpu.make_async_copy(
+            ref, gathered.at[pl.ds(pl.multiple_of(info[place] + offset, 16), ref.shape[0])], arrived.at[index]
+        )
+        for index, (ref, (place, offset)) in enumerate(zip(nodes_in, spots))
+    ] + [pltpu.make_async_copy(ref, weights.at[index], loaded.at[index]) for index, ref in enumerate(refs[2:6])]
+    for copy in copies:
+        copy.start()
     count = gathered.shape[0] // 6
 
     def fill(index, carry):
         at = pl.ds(pl.multiple_of(index * count, 16), count)
-        normed = layer_norm(gathered[at, :])
-        for side, pair in enumerate(((wk_mine, wk_other), (wv_mine, wv_other))):
-            block = jnp.concatenate([dot(normed, weight[...]) for weight in pair], 1)
+        normed = gathered[at, :]
+        for side in range(2):
+            block = jnp.concatenate([dot(normed, weights[2 * side + half]) for half in range(2)], 1)
             table[at, side * deep : (side + 1) * deep, :] = block.reshape(count, deep, LANES)
         return carry
-
-    lax.fori_loop(0, 6, fill, 0)
 
     def ask(index, carry):
         at = pl.ds(pl.multiple_of(index * piece, piece), piece)
@@ -349,11 +359,15 @@
         return carry
 
     lax.fori_loop(0, points // piece, ask, 0)
+    for copy in copies:
+        copy.wait()
+    lax.fori_loop(0, 6, fill, 0)
 
     ones_row = lax.broadcasted_iota(jnp.int32, (2 * LANES, 2 * LANES), 0) // HEAD_DIM
     ones_col = lax.broadcasted_iota(jnp.int32, (2 * LANES, 2 * LANES), 1) // HEAD_DIM
     same_head = jnp.where(ones_row == ones_col, 1.0, 0.0).astype(bf16)
     half = POINTS * deep // 2
+    vectors = table.reshape(table.shape[0] * 2 * deep, LANES)
 
     def step(index, carry):
         first = index * POINTS
@@ -362,8 +376,8 @@
             for slot in range(slots):
                 terms = []
                 for t in range(2):
-                    at = sources[(first + point + t) * slots + slot]
-                    terms.append(table[at, :deep, :] * q[t])
+                    at = pl.multiple_of(sources[(first + point + t) * slots + slot], deep)
+                    terms.append(vectors[pl.ds(at, deep), :] * q[t])
                 product[slot, point * deep : (point + 2) * deep, :] = jnp.concatenate(terms, 0).astype(bf16)
         live = jnp.concatenate(
             [jnp.full((deep, LANES), counts[first + point], jnp.int32) for point in range(POINTS)], 0
@@ -382,22 +396,22 @@
         for point in range(POINTS):
             mixed = None
             for slot in range(slots):
-                at = sources[(first + point) * slots + slot]
-                term = weights[slot][point * deep : (point + 1) * deep, :] * table[at, deep:, :]
+                at = pl.multiple_of(sources[(first + point) * slots + slot], deep)
+                term = weights[slot][point * deep : (point + 1) * deep, :] * vectors[pl.ds(at + deep, deep), :]
                 mixed = term if mixed is None else mixed + term
             query[first + point] = mixed
         return carry
 
     lax.fori_loop(0, points // POINTS, step, 0)
 
-    width = result.shape[1]
+    width = result.shape[0]
     inner = deep * LANES // 2
 
     def finish(index, carry):
         at = pl.ds(pl.multiple_of(index * piece, piece), piece)
         block = query[at].reshape(piece, deep * LANES).astype(bf16)
         acc = dot(block[:, :inner], wo_mine[...]) + dot(block[:, inner:], wo_other[...])
-        result[at, :] = (grid[at, :].astype(f32)[:, :width] + acc[:, :width]).astype(bf16)
+        result[:, at] = (grid[at, :].astype(f32) + acc).T[:width, :].astype(bf16)
         return carry
 
     lax.fori_loop(0, points // piece, finish, 0)
@@ -485,15 +499,15 @@
 
     my_sources = my_part(encoder_sources, rows).reshape(-1)
     my_counts = my_part(encoder_counts, rows)[:, None]
-    dec_sources = (my_part(decoder_sources, points) - (band - 1) * nodes).reshape(-1)
+    dec_sources = ((my_part(decoder_sources, points) - (band - 1) * nodes) * (2 * full // LANES)).reshape(-1)
     dec_counts = my_part(decoder_counts, points)
     grid_wide = jnp.pad(my_grid, ((0, 0), (0, LANES - width)))
-    early = (info, my_sources, my_counts, dec_sources, dec_counts, grid_wide)
+    early = (info, my_sources, my_counts)
 
     query, last = pl.pallas_call(
         query_kernel,
         out_shape=(
-            jax.ShapeDtypeStruct((heads, rows, LANES), f32),
+            jax.ShapeDtypeStruct((heads, rows, LANES), bf16),
             jax.ShapeDtypeStruct(firsts[-1].shape, bf16),
         ),
         in_specs=[VMEM] * 5 + [ANY] * (1 + len(early)),
@@ -511,36 +525,28 @@
         grid_spots += [(3 + side, chunk * grid_cut) for side in range(4)]
 
     slots = encoder_sources.shape[1]
-    encoder_rows = rows // ENCODER_CHUNKS
-    encoder_inputs = (ev_mine, swap(ev_mine), encoder_output, swap(encoder_output))
-
-    def encode(index):
-        at = slice(index * encoder_rows, (index + 1) * encoder_rows)
-        return pl.pallas_call(
-            functools.partial(encoder_kernel, spots=tuple(grid_spots), skip=index * encoder_rows),
-            out_shape=jax.ShapeDtypeStruct((encoder_rows, full), bf16),
-            in_specs=[SMEM, SMEM] + [VMEM] * (8 + len(grid_spots)),
-            out_specs=VMEM,
-            scratch_shapes=[pltpu.VMEM((3 * grid_count, LANES), f32)]
-            + [pltpu.VMEM((GROUP * slots, LANES), f32) for _ in range(CHAINS)]
-            + [pltpu.VMEM((heads, encoder_rows, LANES), f32)],
-            compiler_params=BIG,
-            cost_estimate=cost(16 * rows * full * full),
-            name="encoder",
-        )(info, my_sources, my_counts, query, grid_state, *grid_parts, *encoder_inputs, state)
+    mid, normed_mid = pl.pallas_call(
+        functools.partial(encoder_kernel, spots=tuple(grid_spots)),
+        out_shape=(jax.ShapeDtypeStruct((rows, full), bf16),) * 2,
+        in_specs=[SMEM, SMEM] + [VMEM] * (8 + len(grid_spots)),
+        out_specs=(VMEM, VMEM),
+        scratch_shapes=[pltpu.VMEM((3 * grid_count, LANES), f32)]
+        + [pltpu.VMEM((GROUP * slots, LANES), f32) for _ in range(CHAINS)]
+        + [pltpu.VMEM((heads, rows, LANES), f32)],
+        compiler_params=BIG,
+        cost_estimate=cost(16 * rows * full * full),
+        name="encoder",
+    )(
+        info, my_sources, my_counts, query, grid_state, *grid_parts,
+        ev_mine, swap(ev_mine), encoder_output, swap(encoder_output), state,
+    )
 
     more = HALF_WIN - rows
     facing = [(2 * i + 1, 2 * i + 2) for i in range(bands - 1)]
     facing = facing + [(b, a) for a, b in facing]
-    mids, partners, fars = [], [], []
-    for index in range(ENCODER_CHUNKS):
-        mids.append(encode(index))
-        sent = mids[-1]
-        if index == ENCODER_CHUNKS - 1:
-            edge = swap(jnp.where(core == 0, mids[-1][encoder_rows - more :], mids[0][:more]))
-            sent = jnp.concatenate([sent, edge], 0)
-        fars.append(lax.ppermute(sent, ("band", "head"), facing))
-        partners.append(swap(mids[-1]))
+    partner = swap(normed_mid)
+    edge = jnp.where(core == 0, partner[:more], partner[rows - more :])
+    far = lax.ppermute(jnp.concatenate([normed_mid, edge], 0), ("band", "head"), facing)
 
     pairs = full // LANES
     window_weights = (window_keys, swap(window_keys), window_values, swap(window_values))
@@ -553,7 +559,7 @@
             jax.ShapeDtypeStruct((pairs, rows, LANES), f32),
             jax.ShapeDtypeStruct((8, LANES), jnp.int32),
         ),
-        in_specs=[SMEM] + [VMEM] * (2 * ENCODER_CHUNKS + 6),
+        in_specs=[SMEM] + [VMEM] * 8,
         out_specs=(VMEM,) * 4,
         scratch_shapes=[
             pltpu.VMEM((near_count, full), bf16),
@@ -564,16 +570,16 @@
         compiler_params=BIG,
         cost_estimate=cost(1024),
         name="near_window",
-    )(info, *mids, *partners, window_query, swap(window_query), *window_weights)
+    )(info, normed_mid, partner, window_query, swap(window_query), *window_weights)
 
     near = swap(
-        jnp.where(core + token[0, 0] == 0, fars[-1][encoder_rows - more : encoder_rows], fars[0][:more])
+        jnp.where(core + token[0, 0] == 0, far[rows - more : rows], far[:more])
     )
     far_count = -(-(rows + 2 * more) // LANES) * LANES
     mix = pl.pallas_call(
         far_window_kernel,
         out_shape=jax.ShapeDtypeStruct((pairs, rows, LANES), bf16),
-        in_specs=[SMEM] + [VMEM] * (3 + ENCODER_CHUNKS + 1 + 4),
+        in_specs=[SMEM] + [VMEM] * 9,
         out_specs=VMEM,
         scratch_shapes=[
             pltpu.VMEM((far_count, full), bf16),
@@ -584,25 +590,25 @@
         compiler_params=BIG,
         cost_estimate=cost(20 * rows * full * full),
         name="far_window",
-    )(info, win_query, near_mix, near_sum, *fars, near, *window_weights)
+    )(info, win_query, near_mix, near_sum, far, near, *window_weights)
 
     units = feed_up.shape[1]
     chunk = min(512, units)
     steps = units // chunk
     whole = lambda shape: pl.BlockSpec(shape, lambda i: (0,) * len(shape))
-    cut = rows // FEED_CHUNKS
+    cuts = (rows * 5 // 8, rows - rows * 5 // 8)
     weights = (
         window_output, swap(window_output), feed_up, swap(feed_up), feed_down, swap(feed_down),
     )
 
-    def feed(index):
+    def feed(start, cut):
         return pl.pallas_call(
-            feed_kernel,
+            functools.partial(feed_kernel, start=start),
             grid=(2 * steps,),
-            out_shape=jax.ShapeDtypeStruct((cut, full), bf16),
+            out_shape=(jax.ShapeDtypeStruct((cut, full), bf16),) * 2,
             in_specs=[
-                pl.BlockSpec((pairs, cut, LANES), lambda i: (0, index, 0)),
-                pl.BlockSpec((cut, full), lambda i: (index, 0)),
+                whole((pairs, rows, LANES)),
+                whole((rows, full)),
                 whole((channels, full)),
                 whole((channels, full)),
                 pl.BlockSpec((full, chunk), lambda i: (0, jnp.minimum(i, steps - 1))),
@@ -610,7 +616,7 @@
                 pl.BlockSpec((chunk, full), lambda i: (jnp.minimum(i, steps - 1), 0)),
                 pl.BlockSpec((chunk, full), lambda i: (jnp.maximum(i - steps, 0), 0)),
             ],
-            out_specs=whole((cut, full)),
+            out_specs=(whole((cut, full)),) * 2,
             scratch_shapes=[
                 pltpu.VMEM((cut, full), bf16),
                 pltpu.VMEM((cut, full), bf16),
@@ -619,28 +625,26 @@
             compiler_params=BIG,
             cost_estimate=cost(2 * cut * full * (full + 4 * units)),
             name="feed",
-        )(mix, mids[0], *weights)
+        )(mix, mid, *weights)
 
     node_parts, node_spots, own_parts, partner_parts = [], [], [], []
-    for index in range(FEED_CHUNKS):
-        final = feed(index)
-        first = pair_swap(final)
-        other = swap(final)
-        second = pass_on(first)
-        own_parts.append(final)
-        partner_parts.append(other)
-        node_parts += [final, other, first, swap(first), second, swap(second)]
-        node_spots += [(7 + side, index * cut) for side in range(6)]
+    firsts, seconds = [], []
+    for index, cut in enumerate(cuts):
+        start = sum(cuts[:index])
+        final, normed = feed(start, cut)
+        first = pair_swap(normed)
+        firsts.append(first)
+        if index < len(cuts) - 1:
+            seconds.append(pass_on(first))
+        own_parts.append(lax.dynamic_slice_in_dim(final, core * channels, channels, 1))
+        partner_parts.append(swap(lax.dynamic_slice_in_dim(final, (1 - core) * channels, channels, 1)))
+        node_parts += [normed, swap(normed)]
+        node_spots += [(7 + side, start) for side in range(2)]
 
     deep = full // LANES
     decoder_weights = (decoder_keys, swap(decoder_keys), decoder_values, swap(decoder_values))
 
-    def columns(parts):
-        return jnp.concatenate(
-            [lax.dynamic_slice_in_dim(part, core * channels, channels, 1) for part in parts], 0
-        )
-
-    own_columns, partner_columns = columns(own_parts), columns(partner_parts)
+    own_columns, partner_columns = jnp.concatenate(own_parts, 0), jnp.concatenate(partner_parts, 0)
     hidden_final = jnp.where(
         core == 0,
         jnp.concatenate([own_columns, partner_columns], 0),
@@ -648,16 +652,32 @@
     )
 
     dec_slots = decoder_sources.shape[1]
+    firsts[-1] = pl.pallas_call(
+        hold_kernel,
+        out_shape=jax.ShapeDtypeStruct(firsts[-1].shape, bf16),
+        in_specs=[ANY] * 4,
+        out_specs=ANY,
+        input_output_aliases={0: 0},
+        name="hold",
+    )(firsts[-1], dec_sources, dec_counts, grid_wide)
+    for index, first in enumerate(firsts):
+        second = pass_on(first) if index == len(cuts) - 1 else seconds[index]
+        node_parts += [first, swap(first), second, swap(second)]
+        node_spots += [(9 + side, sum(cuts[:index])) for side in range(4)]
+
     grid_next = pl.pallas_call(
         functools.partial(decoder_kernel, spots=tuple(node_spots)),
-        out_shape=jax.ShapeDtypeStruct((points, width), bf16),
-        in_specs=[SMEM] * 3 + [VMEM] * (9 + len(node_spots)),
+        out_shape=jax.ShapeDtypeStruct((width, points), bf16),
+        in_specs=[SMEM] * 3 + [VMEM] + [ANY] * len(node_spots) + [VMEM] * 2 + [ANY] * 4 + [VMEM] * 2,
         out_specs=VMEM,
         scratch_shapes=[
             pltpu.VMEM((3 * nodes, 2 * deep, LANES), f32),
             pltpu.VMEM((points, deep, LANES), f32),
             pltpu.VMEM((dec_slots, POINTS * deep, LANES), bf16),
             pltpu.VMEM((3 * nodes, full), bf16),
+            pltpu.VMEM((4,) + decoder_keys.shape, bf16),
+            pltpu.SemaphoreType.DMA((len(node_spots),)),
+            pltpu.SemaphoreType.DMA((4,)),
         ],
         compiler_params=BIG,
         name="decoder",
@@ -666,7 +686,7 @@
         dq_mine, swap(dq_mine), *decoder_weights,
         do_mine, swap(do_mine),
     )
-    return (grid_next, hidden_final)
+    return (grid_next.T, hidden_final)
 
 
 def solution(mesh):

time: 258 us -> 244 us (0.946)
  waiting for transfers between devices: 36.1 us -> 28.4 us
  Pallas kernels: 162 us -> 155 us
  starting transfers between devices: 29.1 us -> 32.5 us
    ppermute x4, waiting for transfers between devices: 21 us -> 13.9 us  [pass_on(): return lax.ppermute(x, 'band', jumps)]
    pallas_call x1, Pallas kernels: 54.8 us -> 48.3 us  [local(): pl.pallas_call(functools.partial(decoder_kernel, spots=tuple(node_spots))...]
    pallas_call x3 -> x4, Pallas kernels: 58.7 us -> 60.1 us  [the longest x2 30.3 us: feed(): pl.pallas_call(functools.partial(feed_kernel, start=start), grid=(2 * ste...]
    ppermute x28 -> x29, starting transfers between devices: 14.2 us -> 15 us  [swap(): return lax.ppermute(x, 'head', [(0, 1), (1, 0)])]
    unnamed x87 -> x100, local copies, waits for them, and re-layouts: 7.04 us -> 7.74 us
    ppermute x28 -> x29, waiting for transfers between devices: 7.01 us -> 7.05 us  [swap(): return lax.ppermute(x, 'head', [(0, 1), (1, 0)])]
  transfers between devices with their start and end apart: 37 -> 38, of which waited for: 12 -> 12; matrix products, arithmetic and copies ran while one was open for 8% -> 8% of each run, Pallas kernels for 42% -> 37%
where the time goes in v3:
time: 244 us
  Pallas kernels  155 us (64%)
  starting transfers between devices  32.5 us (13%)
  waiting for transfers between devices  28.4 us (12%)
  local copies, waits for them, and re-layouts  19.3 us (8%)
  other arithmetic  6.59 us (3%)
    pallas_call x1, Pallas kernels, local(): pl.pallas_call(functools.partial(decoder_kernel, spots=tuple(node_spots))...  48.3 us
    pallas_call x2, Pallas kernels, feed(): pl.pallas_call(functools.partial(feed_kernel, start=start), grid=(2 * ste...  30.3 us
    pallas_call x1, Pallas kernels, local(): pl.pallas_call(functools.partial(encoder_kernel, spots=tuple(grid_spots))...  29.8 us
    pallas_call x1, Pallas kernels, local(): pl.pallas_call(near_window_kernel, out_shape=(jax.ShapeDtypeStruct((pairs...  23.4 us
    pallas_call x1, Pallas kernels, local(): pl.pallas_call(far_window_kernel, out_shape=jax.ShapeDtypeStruct((pairs,...  17.6 us
    ppermute x29, starting transfers between devices, swap(): return lax.ppermute(x, 'head', [(0, 1), (1, 0)])  15 us
    ppermute x4, waiting for transfers between devices, pass_on(): return lax.ppermute(x, 'band', jumps)  13.9 us
    ppermute x4, starting transfers between devices, pass_on(): return lax.ppermute(x, 'band', jumps)  9.41 us
  transfers between devices with their start and end apart: 38, of which 12 were waited for; matrix products, arithmetic and copies ran while one was open for 8% of the time, Pallas kernels for 37%

profile of v3, /device:TPU:23, one launch (start us, length us, event | category | flops | bytes accessed | tf_op | source)
XLA Modules:
  0.0 243.7 jit_solution(13751041792015330241)
XLA Ops:
  1.4 2.1 constant_dynamic-slice_fusion.7
  5.3 1.2 collective-permute-start.3
  9.0 2.9 %collective-permute-done.4.refs_0_ = bf16[1024,100]{1,0:T(8,128)(2,1)S(1)} collective-permute-done((bf16[1024,100]{1,0:T(8,128)(2,1)S(1)}, bf16[1024,100]{1,0:T(8,128)(2,1)S(1)}, u32[]{:S(2)}, u32[]{:S(2)}) %collective-permute-start.4) | collective-permute-done | bytes 204832 | tf_op jit(solution)/shard_map/ppermute | solution.py:454
  11.9 2.0 collective-permute-start.2
  14.0 2.1 collective-permute-start.6
  16.1 1.3 maximum_select_fusion.state.refs_12_
  18.0 5.5 %queries.1 = (bf16[16,512,128]{2,1,0:T(8,128)(2,1)}, bf16[1024,100]{1,0:T(8,128)(2,1)}) custom-call(bf16[512,1024]{1,0:T(8,128)(2,1)} %maximum_select_fusion.state.refs_12_, bf16[1024,512]{1,0:T(8,128)(2,1)} %wq_mine.1, bf16[1024,512]{1,0:T(8,128)(2,1)} %collective-permute-done.1.wq_other, ...), custom_call_target="tpu_custom_call", output_to_operand_aliasing={{1}: (5, {})} | custom-call | flops 3221225472 | bytes 12582912 | tf_op jit(solution)/shard_map/queries/pallas_call | solution.py:507
  23.6 3.0 %collective-permute-start.9 = (bf16[1024,100]{1,0:T(8,128)(2,1)}, bf16[1024,100]{1,0:T(8,128)(2,1)S(1)}, u32[]{:S(2)}, u32[]{:S(2)}) collective-permute-start(bf16[1024,100]{1,0:T(8,128)(2,1)} %get-tuple-element.15.refs_4_), channel_id=1, source_target_pairs={{0,4},{4,8},{8,12},{12,16},{16,20},{20,24},{24,28},{6,2},{10,6},{1... | collective-permute-start | bytes 614408 | tf_op jit(solution)/shard_map/ppermute | solution.py:458
  28.6 4.9 %collective-permute-done.9.refs_6_ = bf16[1024,100]{1,0:T(8,128)(2,1)S(1)} collective-permute-done((bf16[1024,100]{1,0:T(8,128)(2,1)}, bf16[1024,100]{1,0:T(8,128)(2,1)S(1)}, u32[]{:S(2)}, u32[]{:S(2)}) %collective-permute-start.9) | collective-permute-done | bytes 204832 | tf_op jit(solution)/shard_map/ppermute | solution.py:458
  33.6 1.7 collective-permute-start.10
  37.2 29.8 %encoder.1 = (bf16[512,1024]{1,0:T(8,128)(2,1)}, bf16[512,1024]{1,0:T(8,128)(2,1)}) custom-call(s32[13]{0:T(128)} %stack.51.refs_0_.info, s32[16384]{0:T(1024)} %reshape.11.refs_1_.sources, s32[512,1]{1,0:T(8,128)} %copy.31.refs_2_.counts, bf16[16,512,128]{2,1,0:T(8,128)(2,1)} %get-tuple-element.14.query, bf16[4096,100]{1,0:T(8,128)(2,1)} %copy-done.2, ...), custom_call_target="tpu_custom_call" | custom-call | flops 8589934592 | bytes 33554432 | tf_op jit(solution)/shard_map/encoder/pallas_call | solution.py:528
  67.6 2.5 %collective-permute-done.13.refs_1_ = bf16[512,1024]{1,0:T(8,128)(2,1)S(1)} collective-permute-done((bf16[512,1024]{1,0:T(8,128)(2,1)}, bf16[512,1024]{1,0:T(8,128)(2,1)S(1)}, u32[]{:S(2)}, u32[]{:S(2)}) %collective-permute-start.13) | collective-permute-done | bytes 1048608 | tf_op jit(solution)/shard_map/ppermute | solution.py:451
  70.1 1.7 pad_maximum_fusion
  71.8 4.7 %collective-permute-start.17 = (bf16[560,1024]{1,0:T(8,128)(2,1)S(1)}, bf16[560,1024]{1,0:T(8,128)(2,1)}, u32[]{:S(2)}, u32[]{:S(2)}) collective-permute-start(bf16[560,1024]{1,0:T(8,128)(2,1)S(1)} %pad_maximum_fusion), channel_id=1, source_target_pairs={{1,2},{3,4},{5,6},{7,8},{9,10},{11,12},{13,14},{15,16},{17,18},{19... | collective-permute-start | bytes 3440648 | tf_op jit(solution)/shard_map/ppermute | solution.py:549
  77.2 2.1 collective-permute-done.16.refs_7_.refs_5_
  80.8 1.0 copy-done.13
  81.8 23.4 %near_window.1 = (bf16[8,512,128]{2,1,0:T(8,128)(2,1)}, f32[8,512,128]{2,1,0:T(8,128)}, f32[8,512,128]{2,1,0:T(8,128)}, s32[8,128]{1,0:T(8,128)}) custom-call(s32[13]{0:T(128)} %stack.51.refs_0_.info, bf16[512,1024]{1,0:T(8,128)(2,1)} %get-tuple-element.16.refs_0_, bf16[512,1024]{1,0:T(8,128)(2,1)} %copy-done.5, bf16[1024,512]{1,0:T(8,128)(2,1)} %refs_2_.2, ...), custom_call_target="tpu_custom_call" | custom-call | flops 1024 | bytes 4 | tf_op jit(solution)/shard_map/near_window/pallas_call | solution.py:554
  105.2 1.2 slice.25
  110.0 17.6 %far_window.1.mix = bf16[8,512,128]{2,1,0:T(8,128)(2,1)} custom-call(s32[13]{0:T(128)} %stack.51.refs_0_.info, bf16[8,512,128]{2,1,0:T(8,128)(2,1)} %get-tuple-element.17.query, f32[8,512,128]{2,1,0:T(8,128)} %get-tuple-element.18.near_mix, f32[8,512,128]{2,1,0:T(8,128)} %get-tuple-element.19.near_total, bf16[560,1024]{1,0:T(8,128)(2,1)} %collective-permute-done.17.refs_0_, ...), custom_call_target="tpu_custom_call" | custom-call | flops 10737418240 | bytes 41943040 | tf_op jit(solution)/shard_map/far_window/pallas_call | solution.py:579
  128.6 16.2 %feed.2 = (bf16[320,1024]{1,0:T(8,128)(2,1)}, bf16[320,1024]{1,0:T(8,128)(2,1)}) custom-call(bf16[8,512,128]{2,1,0:T(8,128)(2,1)} %far_window.1.mix, bf16[512,1024]{1,0:T(8,128)(2,1)} %get-tuple-element.21.mid, bf16[512,1024]{1,0:T(8,128)(2,1)} %wo_mine.3, bf16[512,1024]{1,0:T(8,128)(2,1)} %copy-done.12, bf16[1024,2048]{1,0:T(8,128)(2,1)} %up_mine.3, ...), custom_call_target="tpu_custom_call" | custom-call | flops 6039797760 | bytes 23592960 | tf_op jit(solution)/shard_map/feed/pallas_call | solution.py:605
  145.8 14.1 %feed.3 = (bf16[192,1024]{1,0:T(8,128)(2,1)}, bf16[192,1024]{1,0:T(8,128)(2,1)}) custom-call(bf16[8,512,128]{2,1,0:T(8,128)(2,1)} %far_window.1.mix, bf16[512,1024]{1,0:T(8,128)(2,1)} %get-tuple-element.21.mid, bf16[512,1024]{1,0:T(8,128)(2,1)} %wo_mine.3, bf16[512,1024]{1,0:T(8,128)(2,1)} %copy-done.12, bf16[1024,2048]{1,0:T(8,128)(2,1)} %up_mine.3, ...), custom_call_target="tpu_custom_call" | custom-call | flops 3623878656 | bytes 14155776 | tf_op jit(solution)/shard_map/feed/pallas_call | solution.py:605
  159.9 1.8 collective-permute-start.28
  161.8 1.9 collective-permute-start.26
  164.4 1.8 constant_dynamic-slice_fusion.4
  167.0 4.3 %collective-permute-done.28.refs_0_ = bf16[192,1024]{1,0:T(8,128)(2,1)S(1)} collective-permute-done((bf16[192,1024]{1,0:T(8,128)(2,1)}, bf16[192,1024]{1,0:T(8,128)(2,1)S(1)}, u32[]{:S(2)}, u32[]{:S(2)}) %collective-permute-start.28) | collective-permute-done | bytes 393248 | tf_op jit(solution)/shard_map/ppermute | solution.py:454
  172.4 1.2 reshape.10.refs_1_.sources
  175.2 2.4 collective-permute-start.30
  178.5 2.1 collective-permute-done.26.refs_6_
  180.6 1.8 collective-permute-start.27
  182.5 6.9 %collective-permute-done.30.refs_10_ = bf16[192,1024]{1,0:T(8,128)(2,1)S(1)} collective-permute-done((bf16[192,1024]{1,0:T(8,128)(2,1)}, bf16[192,1024]{1,0:T(8,128)(2,1)S(1)}, u32[]{:S(2)}, u32[]{:S(2)}) %collective-permute-start.30) | collective-permute-done | bytes 393248 | tf_op jit(solution)/shard_map/ppermute | solution.py:458
  190.3 2.6 %maximum_select_fusion.1 = bf16[1024,512]{1,0:T(8,128)(2,1)} fusion(bf16[192,512]{1,0:T(8,128)(2,1)} %collective-permute-done.37, bf16[320,512]{1,0:T(8,128)(2,1)} %collective-permute-done.36, bf16[192,512]{1,0:T(8,128)(2,1)} %get-tuple-element.32, bf16[320,512]{1,0:T(8,128)(2,1)S(1)} %get-tuple-element.30, pred[]{:T(512)S(6)} %eq.14), kind=kLoop, calls=%fused_computation.2 | loop fusion | flops 8912896 | bytes 2097153 | tf_op jit(solution)/shard_map/jit(_where)/select_n | solution.py:648
  195.2 48.3 %decoder.1 = bf16[100,2048]{1,0:T(8,128)(2,1)} custom-call(s32[13]{0:T(128)} %stack.51.refs_0_.info, s32[8192]{0:T(1024)} %reshape.10.refs_1_.sources, s32[2048]{0:T(1024)} %dynamic_slice.34.refs_2_.counts, bf16[2048,128]{1,0:T(8,128)(2,1)} %pad.18.refs_3_.grid, bf16[320,1024]{1,0:T(8,128)(2,1)} %get-tuple-element.22.refs_0_, bf16[320,1024]{1,0:T(8,128)(2,1)} %copy-done.18, ...), custom_call_target="tpu_custom_call" | custom-call | tf_op jit(solution)/shard_map/decoder/pallas_call | solution.py:668
  (178 shorter events, 25.2 us)
Async XLA Ops:
  0.7 17.0 %collective-permute-start.1 = (bf16[1024,512]{1,0:T(8,128)(2,1)}, bf16[1024,512]{1,0:T(8,128)(2,1)}, u32[]{:S(2)}, u32[]{:S(2)}) collective-permute-start(bf16[1024,512]{1,0:T(8,128)(2,1)} %wq_mine.1), channel_id=1, source_target_pairs={{0,1},{1,0},{2,3},{3,2},{4,5},{5,4},{6,7},{7,6},{8,9},{9,8},{10,11... | collective-permute-start | bytes 3145736 | tf_op jit(solution)/shard_map/ppermute | solution.py:451
  3.5 10.5 %collective-permute-start = (bf16[512,512]{1,0:T(8,128)(2,1)}, bf16[512,512]{1,0:T(8,128)(2,1)S(1)}, u32[]{:S(2)}, u32[]{:S(2)}) collective-permute-start(bf16[512,512]{1,0:T(8,128)(2,1)} %get-tuple-element.29), channel_id=1, source_target_pairs={{0,1},{1,0},{2,3},{3,2},{4,5},{5,4},{6,7},{7,6},{8,9},{9,8},{10,11... | collective-permute-start | bytes 1572872 | tf_op jit(solution)/shard_map/ppermute | solution.py:451
  4.4 7.6 %collective-permute-start.4 = (bf16[1024,100]{1,0:T(8,128)(2,1)S(1)}, bf16[1024,100]{1,0:T(8,128)(2,1)S(1)}, u32[]{:S(2)}, u32[]{:S(2)}) collective-permute-start(bf16[1024,100]{1,0:T(8,128)(2,1)S(1)} %get-tuple-element.26), channel_id=1, source_target_pairs={{0,2},{2,0},{4,6},{6,4},{8,10},{10,8},{12,14},{14,12},{16,18},{18,... | collective-permute-start | bytes 614408 | tf_op jit(solution)/shard_map/ppermute | solution.py:454
  4.7 31.1 %collective-permute-start.12 = (bf16[512,1024]{1,0:T(8,128)(2,1)}, bf16[512,1024]{1,0:T(8,128)(2,1)}, u32[]{:S(2)}, u32[]{:S(2)}) collective-permute-start(bf16[512,1024]{1,0:T(8,128)(2,1)} %refs_10_.1), channel_id=1, source_target_pairs={{0,1},{1,0},{2,3},{3,2},{4,5},{5,4},{6,7},{7,6},{8,9},{9,8},{10,11... | collective-permute-start | bytes 3145736 | tf_op jit(solution)/shard_map/ppermute | solution.py:451
  5.3 12.3 %collective-permute-start.3 = (bf16[1024,100]{1,0:T(8,128)(2,1)S(1)}, bf16[1024,100]{1,0:T(8,128)(2,1)}, u32[]{:S(2)}, u32[]{:S(2)}) collective-permute-start(bf16[1024,100]{1,0:T(8,128)(2,1)S(1)} %get-tuple-element.27), channel_id=1, source_target_pairs={{0,2},{2,0},{4,6},{6,4},{8,10},{10,8},{12,14},{14,12},{16,18},{18,... | collective-permute-start | bytes 614408 | tf_op jit(solution)/shard_map/ppermute | solution.py:454
  11.9 5.5 %collective-permute-start.2 = (bf16[128,512]{1,0:T(8,128)(2,1)S(1)}, bf16[128,512]{1,0:T(8,128)(2,1)S(1)}, u32[]{:S(2)}, u32[]{:S(2)}) collective-permute-start(bf16[128,512]{1,0:T(8,128)(2,1)S(1)} %pad.19.keys_mine), channel_id=1, source_target_pairs={{0,1},{1,0},{2,3},{3,2},{4,5},{5,4},{6,7},{7,6},{8,9},{9,8},{10,11... | collective-permute-start | bytes 393224 | tf_op jit(solution)/shard_map/ppermute | solution.py:451
  14.0 13.4 %collective-permute-start.6 = (bf16[1024,100]{1,0:T(8,128)(2,1)S(1)}, bf16[1024,100]{1,0:T(8,128)(2,1)S(1)}, u32[]{:S(2)}, u32[]{:S(2)}) collective-permute-start(bf16[1024,100]{1,0:T(8,128)(2,1)S(1)} %collective-permute-done.4.refs_0_), channel_id=1, source_target_pairs={{0,4},{4,8},{8,12},{12,16},{16,20},{20,24},{24,28},{6,2},{10,6},{1... | collective-permute-start | bytes 614408 | tf_op jit(solution)/shard_map/ppermute | solution.py:458
  23.6 10.0 %collective-permute-start.9 = (bf16[1024,100]{1,0:T(8,128)(2,1)}, bf16[1024,100]{1,0:T(8,128)(2,1)S(1)}, u32[]{:S(2)}, u32[]{:S(2)}) collective-permute-start(bf16[1024,100]{1,0:T(8,128)(2,1)} %get-tuple-element.15.refs_4_), channel_id=1, source_target_pairs={{0,4},{4,8},{8,12},{12,16},{16,20},{20,24},{24,28},{6,2},{10,6},{1... | collective-permute-start | bytes 614408 | tf_op jit(solution)/shard_map/ppermute | solution.py:458
  27.3 8.0 %collective-permute-start.5 = (bf16[1024,100]{1,0:T(8,128)(2,1)S(1)}, bf16[1024,100]{1,0:T(8,128)(2,1)S(1)}, u32[]{:S(2)}, u32[]{:S(2)}) collective-permute-start(bf16[1024,100]{1,0:T(8,128)(2,1)S(1)} %collective-permute-done.4.refs_0_), channel_id=1, source_target_pairs={{0,1},{1,0},{2,3},{3,2},{4,5},{5,4},{6,7},{7,6},{8,9},{9,8},{10,11... | collective-permute-start | bytes 614408 | tf_op jit(solution)/shard_map/ppermute | solution.py:451
  27.4 8.0 %collective-permute-start.7 = (bf16[1024,100]{1,0:T(8,128)(2,1)S(1)}, bf16[1024,100]{1,0:T(8,128)(2,1)S(1)}, u32[]{:S(2)}, u32[]{:S(2)}) collective-permute-start(bf16[1024,100]{1,0:T(8,128)(2,1)S(1)} %collective-permute-done.6.refs_2_), channel_id=1, source_target_pairs={{0,1},{1,0},{2,3},{3,2},{4,5},{5,4},{6,7},{7,6},{8,9},{9,8},{10,11... | collective-permute-start | bytes 614408 | tf_op jit(solution)/shard_map/ppermute | solution.py:451
  28.3 7.5 %collective-permute-start.8 = (bf16[1024,100]{1,0:T(8,128)(2,1)}, bf16[1024,100]{1,0:T(8,128)(2,1)S(1)}, u32[]{:S(2)}, u32[]{:S(2)}) collective-permute-start(bf16[1024,100]{1,0:T(8,128)(2,1)} %get-tuple-element.15.refs_4_), channel_id=1, source_target_pairs={{0,1},{1,0},{2,3},{3,2},{4,5},{5,4},{6,7},{7,6},{8,9},{9,8},{10,11... | collective-permute-start | bytes 614408 | tf_op jit(solution)/shard_map/ppermute | solution.py:451
  35.3 92.3 %collective-permute-start.20 = (bf16[1024,2048]{1,0:T(8,128)(2,1)}, bf16[1024,2048]{1,0:T(8,128)(2,1)}, u32[]{:S(2)}, u32[]{:S(2)}) collective-permute-start(bf16[1024,2048]{1,0:T(8,128)(2,1)} %up_mine.3), channel_id=1, source_target_pairs={{0,1},{1,0},{2,3},{3,2},{4,5},{5,4},{6,7},{7,6},{8,9},{9,8},{10,11... | collective-permute-start | bytes 12582920 | tf_op jit(solution)/shard_map/ppermute | solution.py:451
  35.4 92.3 %collective-permute-start.21 = (bf16[2048,1024]{1,0:T(8,128)(2,1)}, bf16[2048,1024]{1,0:T(8,128)(2,1)}, u32[]{:S(2)}, u32[]{:S(2)}) collective-permute-start(bf16[2048,1024]{1,0:T(8,128)(2,1)} %down_mine.3), channel_id=1, source_target_pairs={{0,1},{1,0},{2,3},{3,2},{4,5},{5,4},{6,7},{7,6},{8,9},{9,8},{10,11... | collective-permute-start | bytes 12582920 | tf_op jit(solution)/shard_map/ppermute | solution.py:451
  67.5 9.2 %collective-permute-start.15 = (bf16[1024,512]{1,0:T(8,128)(2,1)S(1)}, bf16[1024,512]{1,0:T(8,128)(2,1)S(1)}, u32[]{:S(2)}, u32[]{:S(2)}) collective-permute-start(bf16[1024,512]{1,0:T(8,128)(2,1)S(1)} %copy-done.7), channel_id=1, source_target_pairs={{0,1},{1,0},{2,3},{3,2},{4,5},{5,4},{6,7},{7,6},{8,9},{9,8},{10,11... | collective-permute-start | bytes 3145736 | tf_op jit(solution)/shard_map/ppermute | solution.py:451
  71.8 35.3 %collective-permute-start.17 = (bf16[560,1024]{1,0:T(8,128)(2,1)S(1)}, bf16[560,1024]{1,0:T(8,128)(2,1)}, u32[]{:S(2)}, u32[]{:S(2)}) collective-permute-start(bf16[560,1024]{1,0:T(8,128)(2,1)S(1)} %pad_maximum_fusion), channel_id=1, source_target_pairs={{1,2},{3,4},{5,6},{7,8},{9,10},{11,12},{13,14},{15,16},{17,18},{19... | collective-permute-start | bytes 3440648 | tf_op jit(solution)/shard_map/ppermute | solution.py:549
  76.7 4.1 %collective-permute-start.14 = (bf16[1024,512]{1,0:T(8,128)(2,1)S(1)}, bf16[1024,512]{1,0:T(8,128)(2,1)S(1)}, u32[]{:S(2)}, u32[]{:S(2)}) collective-permute-start(bf16[1024,512]{1,0:T(8,128)(2,1)S(1)} %copy-done.6), channel_id=1, source_target_pairs={{0,1},{1,0},{2,3},{3,2},{4,5},{5,4},{6,7},{7,6},{8,9},{9,8},{10,11... | collective-permute-start | bytes 3145736 | tf_op jit(solution)/shard_map/ppermute | solution.py:451
  108.2 19.4 %collective-permute-start.19 = (bf16[512,1024]{1,0:T(8,128)(2,1)S(1)}, bf16[512,1024]{1,0:T(8,128)(2,1)S(1)}, u32[]{:S(2)}, u32[]{:S(2)}) collective-permute-start(bf16[512,1024]{1,0:T(8,128)(2,1)S(1)} %copy-done.9), channel_id=1, source_target_pairs={{0,1},{1,0},{2,3},{3,2},{4,5},{5,4},{6,7},{7,6},{8,9},{9,8},{10,11... | collective-permute-start | bytes 3145736 | tf_op jit(solution)/shard_map/ppermute | solution.py:451
  144.8 16.9 %collective-permute-start.24 = (bf16[320,1024]{1,0:T(8,128)(2,1)}, bf16[320,1024]{1,0:T(8,128)(2,1)}, u32[]{:S(2)}, u32[]{:S(2)}) collective-permute-start(bf16[320,1024]{1,0:T(8,128)(2,1)} %get-tuple-element.22.refs_0_), channel_id=1, source_target_pairs={{0,2},{2,0},{4,6},{6,4},{8,10},{10,8},{12,14},{14,12},{16,18},{18,... | collective-permute-start | bytes 1966088 | tf_op jit(solution)/shard_map/ppermute | solution.py:454
  145.0 18.8 %collective-permute-start.35 = (bf16[512,128]{1,0:T(8,128)(2,1)S(1)}, bf16[512,128]{1,0:T(8,128)(2,1)S(1)}, u32[]{:S(2)}, u32[]{:S(2)}) collective-permute-start(bf16[512,128]{1,0:T(8,128)(2,1)S(1)} %pad.22.refs_18_), channel_id=1, source_target_pairs={{0,1},{1,0},{2,3},{3,2},{4,5},{5,4},{6,7},{7,6},{8,9},{9,8},{10,11... | collective-permute-start | bytes 393224 | tf_op jit(solution)/shard_map/ppermute | solution.py:451
  145.2 29.9 %collective-permute-start.33 = (bf16[1024,512]{1,0:T(8,128)(2,1)S(1)}, bf16[1024,512]{1,0:T(8,128)(2,1)}, u32[]{:S(2)}, u32[]{:S(2)}) collective-permute-start(bf16[1024,512]{1,0:T(8,128)(2,1)S(1)} %copy-done.14), channel_id=1, source_target_pairs={{0,1},{1,0},{2,3},{3,2},{4,5},{5,4},{6,7},{7,6},{8,9},{9,8},{10,11... | collective-permute-start | bytes 3145736 | tf_op jit(solution)/shard_map/ppermute | solution.py:451
  145.6 29.6 %collective-permute-start.34 = (bf16[1024,512]{1,0:T(8,128)(2,1)}, bf16[1024,512]{1,0:T(8,128)(2,1)}, u32[]{:S(2)}, u32[]{:S(2)}) collective-permute-start(bf16[1024,512]{1,0:T(8,128)(2,1)} %refs_16_.1), channel_id=1, source_target_pairs={{0,1},{1,0},{2,3},{3,2},{4,5},{5,4},{6,7},{7,6},{8,9},{9,8},{10,11... | collective-permute-start | bytes 3145736 | tf_op jit(solution)/shard_map/ppermute | solution.py:451
  159.9 11.3 %collective-permute-start.28 = (bf16[192,1024]{1,0:T(8,128)(2,1)}, bf16[192,1024]{1,0:T(8,128)(2,1)S(1)}, u32[]{:S(2)}, u32[]{:S(2)}) collective-permute-start(bf16[192,1024]{1,0:T(8,128)(2,1)} %get-tuple-element.23.refs_2_), channel_id=1, source_target_pairs={{0,2},{2,0},{4,6},{6,4},{8,10},{10,8},{12,14},{14,12},{16,18},{18,... | collective-permute-start | bytes 1179656 | tf_op jit(solution)/shard_map/ppermute | solution.py:454
  161.8 18.9 %collective-permute-start.26 = (bf16[320,1024]{1,0:T(8,128)(2,1)}, bf16[320,1024]{1,0:T(8,128)(2,1)}, u32[]{:S(2)}, u32[]{:S(2)}) collective-permute-start(bf16[320,1024]{1,0:T(8,128)(2,1)} %collective-permute-done.24.refs_4_), channel_id=1, source_target_pairs={{0,4},{4,8},{8,12},{12,16},{16,20},{20,24},{24,28},{6,2},{10,6},{1... | collective-permute-start | bytes 1966088 | tf_op jit(solution)/shard_map/ppermute | solution.py:458
  167.0 10.6 %collective-permute-start.37 = (bf16[192,512]{1,0:T(8,128)(2,1)}, bf16[192,512]{1,0:T(8,128)(2,1)}, u32[]{:S(2)}, u32[]{:S(2)}) collective-permute-start(bf16[192,512]{1,0:T(8,128)(2,1)} %get-tuple-element.33), channel_id=1, source_target_pairs={{0,1},{1,0},{2,3},{3,2},{4,5},{5,4},{6,7},{7,6},{8,9},{9,8},{10,11... | collective-permute-start | bytes 589832 | tf_op jit(solution)/shard_map/ppermute | solution.py:451
  171.3 7.2 %collective-permute-start.36 = (bf16[320,512]{1,0:T(8,128)(2,1)}, bf16[320,512]{1,0:T(8,128)(2,1)}, u32[]{:S(2)}, u32[]{:S(2)}) collective-permute-start(bf16[320,512]{1,0:T(8,128)(2,1)} %get-tuple-element.31), channel_id=1, source_target_pairs={{0,1},{1,0},{2,3},{3,2},{4,5},{5,4},{6,7},{7,6},{8,9},{9,8},{10,11... | collective-permute-start | bytes 983048 | tf_op jit(solution)/shard_map/ppermute | solution.py:451
  175.2 7.3 %collective-permute-start.23 = (bf16[192,1024]{1,0:T(8,128)(2,1)S(1)}, bf16[192,1024]{1,0:T(8,128)(2,1)S(1)}, u32[]{:S(2)}, u32[]{:S(2)}) collective-permute-start(bf16[192,1024]{1,0:T(8,128)(2,1)S(1)} %copy-done.23), channel_id=1, source_target_pairs={{0,1},{1,0},{2,3},{3,2},{4,5},{5,4},{6,7},{7,6},{8,9},{9,8},{10,11... | collective-permute-start | bytes 1179656 | tf_op jit(solution)/shard_map/ppermute | solution.py:451
  175.2 14.2 %collective-permute-start.30 = (bf16[192,1024]{1,0:T(8,128)(2,1)}, bf16[192,1024]{1,0:T(8,128)(2,1)S(1)}, u32[]{:S(2)}, u32[]{:S(2)}) collective-permute-start(bf16[192,1024]{1,0:T(8,128)(2,1)} %hold.1.refs_8_), channel_id=1, source_target_pairs={{0,4},{4,8},{8,12},{12,16},{16,20},{20,24},{24,28},{6,2},{10,6},{1... | collective-permute-start | bytes 1179656 | tf_op jit(solution)/shard_map/ppermute | solution.py:458
  177.6 15.3 %collective-permute-start.22 = (bf16[320,1024]{1,0:T(8,128)(2,1)S(1)}, bf16[320,1024]{1,0:T(8,128)(2,1)S(1)}, u32[]{:S(2)}, u32[]{:S(2)}) collective-permute-start(bf16[320,1024]{1,0:T(8,128)(2,1)S(1)} %copy-done.17), channel_id=1, source_target_pairs={{0,1},{1,0},{2,3},{3,2},{4,5},{5,4},{6,7},{7,6},{8,9},{9,8},{10,11... | collective-permute-start | bytes 1966088 | tf_op jit(solution)/shard_map/ppermute | solution.py:451
  178.5 14.6 %collective-permute-start.25 = (bf16[320,1024]{1,0:T(8,128)(2,1)}, bf16[320,1024]{1,0:T(8,128)(2,1)S(1)}, u32[]{:S(2)}, u32[]{:S(2)}) collective-permute-start(bf16[320,1024]{1,0:T(8,128)(2,1)} %collective-permute-done.24.refs_4_), channel_id=1, source_target_pairs={{0,1},{1,0},{2,3},{3,2},{4,5},{5,4},{6,7},{7,6},{8,9},{9,8},{10,11... | collective-permute-start | bytes 1966088 | tf_op jit(solution)/shard_map/ppermute | solution.py:451
  180.6 12.4 %collective-permute-start.27 = (bf16[320,1024]{1,0:T(8,128)(2,1)}, bf16[320,1024]{1,0:T(8,128)(2,1)S(1)}, u32[]{:S(2)}, u32[]{:S(2)}) collective-permute-start(bf16[320,1024]{1,0:T(8,128)(2,1)} %collective-permute-done.26.refs_6_), channel_id=1, source_target_pairs={{0,1},{1,0},{2,3},{3,2},{4,5},{5,4},{6,7},{7,6},{8,9},{9,8},{10,11... | collective-permute-start | bytes 1966088 | tf_op jit(solution)/shard_map/ppermute | solution.py:451
  182.5 10.5 %collective-permute-start.29 = (bf16[192,1024]{1,0:T(8,128)(2,1)}, bf16[192,1024]{1,0:T(8,128)(2,1)S(1)}, u32[]{:S(2)}, u32[]{:S(2)}) collective-permute-start(bf16[192,1024]{1,0:T(8,128)(2,1)} %hold.1.refs_8_), channel_id=1, source_target_pairs={{0,1},{1,0},{2,3},{3,2},{4,5},{5,4},{6,7},{7,6},{8,9},{9,8},{10,11... | collective-permute-start | bytes 1179656 | tf_op jit(solution)/shard_map/ppermute | solution.py:451
  189.4 3.5 %collective-permute-start.31 = (bf16[192,1024]{1,0:T(8,128)(2,1)S(1)}, bf16[192,1024]{1,0:T(8,128)(2,1)S(1)}, u32[]{:S(2)}, u32[]{:S(2)}) collective-permute-start(bf16[192,1024]{1,0:T(8,128)(2,1)S(1)} %collective-permute-done.30.refs_10_), channel_id=1, source_target_pairs={{0,1},{1,0},{2,3},{3,2},{4,5},{5,4},{6,7},{7,6},{8,9},{9,8},{10,11... | collective-permute-start | bytes 1179656 | tf_op jit(solution)/shard_map/ppermute | solution.py:451
  (55 other events, 424.3 us)

commit v4 on v3

--- a/solution.py
+++ b/solution.py
@@ -63,7 +63,7 @@
 
 GRID_CHUNKS = 2
 GROUP = 8
-CHAINS = 4
+CHAINS = 8
 
 
 def encoder_kernel(

time: 244 us -> 241 us (0.988)
  Pallas kernels: 155 us -> 152 us
    pallas_call x1, Pallas kernels: 29.8 us -> 26.9 us  [local(): pl.pallas_call(functools.partial(encoder_kernel, spots=tuple(grid_spots))...]
  transfers between devices with their start and end apart: 38 -> 38, of which waited for: 12 -> 12; matrix products, arithmetic and copies ran while one was open for 8% -> 8% of each run, Pallas kernels for 37% -> 36%
where the time goes in v4:
time: 241 us
  Pallas kernels  152 us (63%)
  starting transfers between devices  32.7 us (14%)
  waiting for transfers between devices  28.2 us (12%)
  local copies, waits for them, and re-layouts  19.3 us (8%)
  other arithmetic  6.59 us (3%)
    pallas_call x1, Pallas kernels, local(): pl.pallas_call(functools.partial(decoder_kernel, spots=tuple(node_spots))...  48.3 us
    pallas_call x2, Pallas kernels, feed(): pl.pallas_call(functools.partial(feed_kernel, start=start), grid=(2 * ste...  30.3 us
    pallas_call x1, Pallas kernels, local(): pl.pallas_call(functools.partial(encoder_kernel, spots=tuple(grid_spots))...  26.9 us
    pallas_call x1, Pallas kernels, local(): pl.pallas_call(near_window_kernel, out_shape=(jax.ShapeDtypeStruct((pairs...  23.4 us
    pallas_call x1, Pallas kernels, local(): pl.pallas_call(far_window_kernel, out_shape=jax.ShapeDtypeStruct((pairs,...  17.6 us
    ppermute x29, starting transfers between devices, swap(): return lax.ppermute(x, 'head', [(0, 1), (1, 0)])  15 us
    ppermute x4, waiting for transfers between devices, pass_on(): return lax.ppermute(x, 'band', jumps)  13.7 us
    ppermute x4, starting transfers between devices, pass_on(): return lax.ppermute(x, 'band', jumps)  9.61 us
  transfers between devices with their start and end apart: 38, of which 12 were waited for; matrix products, arithmetic and copies ran while one was open for 8% of the time, Pallas kernels for 36%

profile of v4, /device:TPU:23, one launch (start us, length us, event | category | flops | bytes accessed | tf_op | source)
XLA Modules:
  0.0 240.7 jit_solution(2821865285162571968)
XLA Ops:
  1.4 2.1 constant_dynamic-slice_fusion.7
  5.3 1.2 collective-permute-start.3
  9.0 2.9 %collective-permute-done.4.refs_0_ = bf16[1024,100]{1,0:T(8,128)(2,1)S(1)} collective-permute-done((bf16[1024,100]{1,0:T(8,128)(2,1)S(1)}, bf16[1024,100]{1,0:T(8,128)(2,1)S(1)}, u32[]{:S(2)}, u32[]{:S(2)}) %collective-permute-start.4) | collective-permute-done | bytes 204832 | tf_op jit(solution)/shard_map/ppermute | solution.py:454
  11.9 2.0 collective-permute-start.2
  14.0 2.1 collective-permute-start.6
  16.1 1.3 maximum_select_fusion.state.refs_12_
  18.0 5.5 %queries.1 = (bf16[16,512,128]{2,1,0:T(8,128)(2,1)}, bf16[1024,100]{1,0:T(8,128)(2,1)}) custom-call(bf16[512,1024]{1,0:T(8,128)(2,1)} %maximum_select_fusion.state.refs_12_, bf16[1024,512]{1,0:T(8,128)(2,1)} %wq_mine.1, bf16[1024,512]{1,0:T(8,128)(2,1)} %collective-permute-done.1.wq_other, ...), custom_call_target="tpu_custom_call", output_to_operand_aliasing={{1}: (5, {})} | custom-call | flops 3221225472 | bytes 12582912 | tf_op jit(solution)/shard_map/queries/pallas_call | solution.py:507
  23.6 3.0 %collective-permute-start.9 = (bf16[1024,100]{1,0:T(8,128)(2,1)}, bf16[1024,100]{1,0:T(8,128)(2,1)S(1)}, u32[]{:S(2)}, u32[]{:S(2)}) collective-permute-start(bf16[1024,100]{1,0:T(8,128)(2,1)} %get-tuple-element.15.refs_4_), channel_id=1, source_target_pairs={{0,4},{4,8},{8,12},{12,16},{16,20},{20,24},{24,28},{6,2},{10,6},{1... | collective-permute-start | bytes 614408 | tf_op jit(solution)/shard_map/ppermute | solution.py:458
  28.6 4.9 %collective-permute-done.9.refs_6_ = bf16[1024,100]{1,0:T(8,128)(2,1)S(1)} collective-permute-done((bf16[1024,100]{1,0:T(8,128)(2,1)}, bf16[1024,100]{1,0:T(8,128)(2,1)S(1)}, u32[]{:S(2)}, u32[]{:S(2)}) %collective-permute-start.9) | collective-permute-done | bytes 204832 | tf_op jit(solution)/shard_map/ppermute | solution.py:458
  33.6 1.7 collective-permute-start.10
  37.2 26.9 %encoder.1 = (bf16[512,1024]{1,0:T(8,128)(2,1)}, bf16[512,1024]{1,0:T(8,128)(2,1)}) custom-call(s32[13]{0:T(128)} %stack.51.refs_0_.info, s32[16384]{0:T(1024)} %reshape.11.refs_1_.sources, s32[512,1]{1,0:T(8,128)} %copy.31.refs_2_.counts, bf16[16,512,128]{2,1,0:T(8,128)(2,1)} %get-tuple-element.14.query, bf16[4096,100]{1,0:T(8,128)(2,1)} %copy-done.2, ...), custom_call_target="tpu_custom_call" | custom-call | flops 8589934592 | bytes 33554432 | tf_op jit(solution)/shard_map/encoder/pallas_call | solution.py:528
  64.6 2.5 %collective-permute-done.13.refs_1_ = bf16[512,1024]{1,0:T(8,128)(2,1)S(1)} collective-permute-done((bf16[512,1024]{1,0:T(8,128)(2,1)}, bf16[512,1024]{1,0:T(8,128)(2,1)S(1)}, u32[]{:S(2)}, u32[]{:S(2)}) %collective-permute-start.13) | collective-permute-done | bytes 1048608 | tf_op jit(solution)/shard_map/ppermute | solution.py:451
  67.2 1.7 pad_maximum_fusion
  68.9 4.7 %collective-permute-start.17 = (bf16[560,1024]{1,0:T(8,128)(2,1)S(1)}, bf16[560,1024]{1,0:T(8,128)(2,1)}, u32[]{:S(2)}, u32[]{:S(2)}) collective-permute-start(bf16[560,1024]{1,0:T(8,128)(2,1)S(1)} %pad_maximum_fusion), channel_id=1, source_target_pairs={{1,2},{3,4},{5,6},{7,8},{9,10},{11,12},{13,14},{15,16},{17,18},{19... | collective-permute-start | bytes 3440648 | tf_op jit(solution)/shard_map/ppermute | solution.py:549
  74.2 2.1 collective-permute-done.16.refs_7_.refs_5_
  77.8 1.0 copy-done.13
  78.9 23.4 %near_window.1 = (bf16[8,512,128]{2,1,0:T(8,128)(2,1)}, f32[8,512,128]{2,1,0:T(8,128)}, f32[8,512,128]{2,1,0:T(8,128)}, s32[8,128]{1,0:T(8,128)}) custom-call(s32[13]{0:T(128)} %stack.51.refs_0_.info, bf16[512,1024]{1,0:T(8,128)(2,1)} %get-tuple-element.16.refs_0_, bf16[512,1024]{1,0:T(8,128)(2,1)} %copy-done.5, bf16[1024,512]{1,0:T(8,128)(2,1)} %refs_2_.2, ...), custom_call_target="tpu_custom_call" | custom-call | flops 1024 | bytes 4 | tf_op jit(solution)/shard_map/near_window/pallas_call | solution.py:554
  102.2 1.2 slice.25
  107.1 17.6 %far_window.1.mix = bf16[8,512,128]{2,1,0:T(8,128)(2,1)} custom-call(s32[13]{0:T(128)} %stack.51.refs_0_.info, bf16[8,512,128]{2,1,0:T(8,128)(2,1)} %get-tuple-element.17.query, f32[8,512,128]{2,1,0:T(8,128)} %get-tuple-element.18.near_mix, f32[8,512,128]{2,1,0:T(8,128)} %get-tuple-element.19.near_total, bf16[560,1024]{1,0:T(8,128)(2,1)} %collective-permute-done.17.refs_0_, ...), custom_call_target="tpu_custom_call" | custom-call | flops 10737418240 | bytes 41943040 | tf_op jit(solution)/shard_map/far_window/pallas_call | solution.py:579
  125.7 16.2 %feed.2 = (bf16[320,1024]{1,0:T(8,128)(2,1)}, bf16[320,1024]{1,0:T(8,128)(2,1)}) custom-call(bf16[8,512,128]{2,1,0:T(8,128)(2,1)} %far_window.1.mix, bf16[512,1024]{1,0:T(8,128)(2,1)} %get-tuple-element.21.mid, bf16[512,1024]{1,0:T(8,128)(2,1)} %wo_mine.3, bf16[512,1024]{1,0:T(8,128)(2,1)} %copy-done.12, bf16[1024,2048]{1,0:T(8,128)(2,1)} %up_mine.3, ...), custom_call_target="tpu_custom_call" | custom-call | flops 6039797760 | bytes 23592960 | tf_op jit(solution)/shard_map/feed/pallas_call | solution.py:605
  142.8 14.1 %feed.3 = (bf16[192,1024]{1,0:T(8,128)(2,1)}, bf16[192,1024]{1,0:T(8,128)(2,1)}) custom-call(bf16[8,512,128]{2,1,0:T(8,128)(2,1)} %far_window.1.mix, bf16[512,1024]{1,0:T(8,128)(2,1)} %get-tuple-element.21.mid, bf16[512,1024]{1,0:T(8,128)(2,1)} %wo_mine.3, bf16[512,1024]{1,0:T(8,128)(2,1)} %copy-done.12, bf16[1024,2048]{1,0:T(8,128)(2,1)} %up_mine.3, ...), custom_call_target="tpu_custom_call" | custom-call | flops 3623878656 | bytes 14155776 | tf_op jit(solution)/shard_map/feed/pallas_call | solution.py:605
  157.0 1.8 collective-permute-start.28
  158.8 1.9 collective-permute-start.26
  161.4 1.8 constant_dynamic-slice_fusion.4
  164.0 4.3 %collective-permute-done.28.refs_0_ = bf16[192,1024]{1,0:T(8,128)(2,1)S(1)} collective-permute-done((bf16[192,1024]{1,0:T(8,128)(2,1)}, bf16[192,1024]{1,0:T(8,128)(2,1)S(1)}, u32[]{:S(2)}, u32[]{:S(2)}) %collective-permute-start.28) | collective-permute-done | bytes 393248 | tf_op jit(solution)/shard_map/ppermute | solution.py:454
  169.4 1.2 reshape.10.refs_1_.sources
  172.3 2.5 %collective-permute-start.30 = (bf16[192,1024]{1,0:T(8,128)(2,1)}, bf16[192,1024]{1,0:T(8,128)(2,1)S(1)}, u32[]{:S(2)}, u32[]{:S(2)}) collective-permute-start(bf16[192,1024]{1,0:T(8,128)(2,1)} %hold.1.refs_8_), channel_id=1, source_target_pairs={{0,4},{4,8},{8,12},{12,16},{16,20},{20,24},{24,28},{6,2},{10,6},{1... | collective-permute-start | bytes 1179656 | tf_op jit(solution)/shard_map/ppermute | solution.py:458
  175.8 1.9 collective-permute-done.26.refs_6_
  177.7 1.8 collective-permute-start.27
  179.6 6.9 %collective-permute-done.30.refs_10_ = bf16[192,1024]{1,0:T(8,128)(2,1)S(1)} collective-permute-done((bf16[192,1024]{1,0:T(8,128)(2,1)}, bf16[192,1024]{1,0:T(8,128)(2,1)S(1)}, u32[]{:S(2)}, u32[]{:S(2)}) %collective-permute-start.30) | collective-permute-done | bytes 393248 | tf_op jit(solution)/shard_map/ppermute | solution.py:458
  187.4 2.6 %maximum_select_fusion.1 = bf16[1024,512]{1,0:T(8,128)(2,1)} fusion(bf16[192,512]{1,0:T(8,128)(2,1)} %collective-permute-done.37, bf16[320,512]{1,0:T(8,128)(2,1)} %collective-permute-done.36, bf16[192,512]{1,0:T(8,128)(2,1)} %get-tuple-element.32, bf16[320,512]{1,0:T(8,128)(2,1)S(1)} %get-tuple-element.30, pred[]{:T(512)S(6)} %eq.14), kind=kLoop, calls=%fused_computation.2 | loop fusion | flops 8912896 | bytes 2097153 | tf_op jit(solution)/shard_map/jit(_where)/select_n | solution.py:648
  192.2 48.3 %decoder.1 = bf16[100,2048]{1,0:T(8,128)(2,1)} custom-call(s32[13]{0:T(128)} %stack.51.refs_0_.info, s32[8192]{0:T(1024)} %reshape.10.refs_1_.sources, s32[2048]{0:T(1024)} %dynamic_slice.34.refs_2_.counts, bf16[2048,128]{1,0:T(8,128)(2,1)} %pad.18.refs_3_.grid, bf16[320,1024]{1,0:T(8,128)(2,1)} %get-tuple-element.22.refs_0_, bf16[320,1024]{1,0:T(8,128)(2,1)} %copy-done.18, ...), custom_call_target="tpu_custom_call" | custom-call | tf_op jit(solution)/shard_map/decoder/pallas_call | solution.py:668
  (178 shorter events, 25.3 us)
Async XLA Ops:
  0.7 17.0 %collective-permute-start.1 = (bf16[1024,512]{1,0:T(8,128)(2,1)}, bf16[1024,512]{1,0:T(8,128)(2,1)}, u32[]{:S(2)}, u32[]{:S(2)}) collective-permute-start(bf16[1024,512]{1,0:T(8,128)(2,1)} %wq_mine.1), channel_id=1, source_target_pairs={{0,1},{1,0},{2,3},{3,2},{4,5},{5,4},{6,7},{7,6},{8,9},{9,8},{10,11... | collective-permute-start | bytes 3145736 | tf_op jit(solution)/shard_map/ppermute | solution.py:451
  3.5 10.5 %collective-permute-start = (bf16[512,512]{1,0:T(8,128)(2,1)}, bf16[512,512]{1,0:T(8,128)(2,1)S(1)}, u32[]{:S(2)}, u32[]{:S(2)}) collective-permute-start(bf16[512,512]{1,0:T(8,128)(2,1)} %get-tuple-element.29), channel_id=1, source_target_pairs={{0,1},{1,0},{2,3},{3,2},{4,5},{5,4},{6,7},{7,6},{8,9},{9,8},{10,11... | collective-permute-start | bytes 1572872 | tf_op jit(solution)/shard_map/ppermute | solution.py:451
  4.4 7.6 %collective-permute-start.4 = (bf16[1024,100]{1,0:T(8,128)(2,1)S(1)}, bf16[1024,100]{1,0:T(8,128)(2,1)S(1)}, u32[]{:S(2)}, u32[]{:S(2)}) collective-permute-start(bf16[1024,100]{1,0:T(8,128)(2,1)S(1)} %get-tuple-element.26), channel_id=1, source_target_pairs={{0,2},{2,0},{4,6},{6,4},{8,10},{10,8},{12,14},{14,12},{16,18},{18,... | collective-permute-start | bytes 614408 | tf_op jit(solution)/shard_map/ppermute | solution.py:454
  4.7 31.1 %collective-permute-start.12 = (bf16[512,1024]{1,0:T(8,128)(2,1)}, bf16[512,1024]{1,0:T(8,128)(2,1)}, u32[]{:S(2)}, u32[]{:S(2)}) collective-permute-start(bf16[512,1024]{1,0:T(8,128)(2,1)} %refs_10_.1), channel_id=1, source_target_pairs={{0,1},{1,0},{2,3},{3,2},{4,5},{5,4},{6,7},{7,6},{8,9},{9,8},{10,11... | collective-permute-start | bytes 3145736 | tf_op jit(solution)/shard_map/ppermute | solution.py:451
  5.3 12.3 %collective-permute-start.3 = (bf16[1024,100]{1,0:T(8,128)(2,1)S(1)}, bf16[1024,100]{1,0:T(8,128)(2,1)}, u32[]{:S(2)}, u32[]{:S(2)}) collective-permute-start(bf16[1024,100]{1,0:T(8,128)(2,1)S(1)} %get-tuple-element.27), channel_id=1, source_target_pairs={{0,2},{2,0},{4,6},{6,4},{8,10},{10,8},{12,14},{14,12},{16,18},{18,... | collective-permute-start | bytes 614408 | tf_op jit(solution)/shard_map/ppermute | solution.py:454
  11.9 5.5 %collective-permute-start.2 = (bf16[128,512]{1,0:T(8,128)(2,1)S(1)}, bf16[128,512]{1,0:T(8,128)(2,1)S(1)}, u32[]{:S(2)}, u32[]{:S(2)}) collective-permute-start(bf16[128,512]{1,0:T(8,128)(2,1)S(1)} %pad.19.keys_mine), channel_id=1, source_target_pairs={{0,1},{1,0},{2,3},{3,2},{4,5},{5,4},{6,7},{7,6},{8,9},{9,8},{10,11... | collective-permute-start | bytes 393224 | tf_op jit(solution)/shard_map/ppermute | solution.py:451
  14.0 13.4 %collective-permute-start.6 = (bf16[1024,100]{1,0:T(8,128)(2,1)S(1)}, bf16[1024,100]{1,0:T(8,128)(2,1)S(1)}, u32[]{:S(2)}, u32[]{:S(2)}) collective-permute-start(bf16[1024,100]{1,0:T(8,128)(2,1)S(1)} %collective-permute-done.4.refs_0_), channel_id=1, source_target_pairs={{0,4},{4,8},{8,12},{12,16},{16,20},{20,24},{24,28},{6,2},{10,6},{1... | collective-permute-start | bytes 614408 | tf_op jit(solution)/shard_map/ppermute | solution.py:458
  23.6 10.0 %collective-permute-start.9 = (bf16[1024,100]{1,0:T(8,128)(2,1)}, bf16[1024,100]{1,0:T(8,128)(2,1)S(1)}, u32[]{:S(2)}, u32[]{:S(2)}) collective-permute-start(bf16[1024,100]{1,0:T(8,128)(2,1)} %get-tuple-element.15.refs_4_), channel_id=1, source_target_pairs={{0,4},{4,8},{8,12},{12,16},{16,20},{20,24},{24,28},{6,2},{10,6},{1... | collective-permute-start | bytes 614408 | tf_op jit(solution)/shard_map/ppermute | solution.py:458
  27.3 8.0 %collective-permute-start.5 = (bf16[1024,100]{1,0:T(8,128)(2,1)S(1)}, bf16[1024,100]{1,0:T(8,128)(2,1)S(1)}, u32[]{:S(2)}, u32[]{:S(2)}) collective-permute-start(bf16[1024,100]{1,0:T(8,128)(2,1)S(1)} %collective-permute-done.4.refs_0_), channel_id=1, source_target_pairs={{0,1},{1,0},{2,3},{3,2},{4,5},{5,4},{6,7},{7,6},{8,9},{9,8},{10,11... | collective-permute-start | bytes 614408 | tf_op jit(solution)/shard_map/ppermute | solution.py:451
  27.4 8.0 %collective-permute-start.7 = (bf16[1024,100]{1,0:T(8,128)(2,1)S(1)}, bf16[1024,100]{1,0:T(8,128)(2,1)S(1)}, u32[]{:S(2)}, u32[]{:S(2)}) collective-permute-start(bf16[1024,100]{1,0:T(8,128)(2,1)S(1)} %collective-permute-done.6.refs_2_), channel_id=1, source_target_pairs={{0,1},{1,0},{2,3},{3,2},{4,5},{5,4},{6,7},{7,6},{8,9},{9,8},{10,11... | collective-permute-start | bytes 614408 | tf_op jit(solution)/shard_map/ppermute | solution.py:451
  28.3 7.5 %collective-permute-start.8 = (bf16[1024,100]{1,0:T(8,128)(2,1)}, bf16[1024,100]{1,0:T(8,128)(2,1)S(1)}, u32[]{:S(2)}, u32[]{:S(2)}) collective-permute-start(bf16[1024,100]{1,0:T(8,128)(2,1)} %get-tuple-element.15.refs_4_), channel_id=1, source_target_pairs={{0,1},{1,0},{2,3},{3,2},{4,5},{5,4},{6,7},{7,6},{8,9},{9,8},{10,11... | collective-permute-start | bytes 614408 | tf_op jit(solution)/shard_map/ppermute | solution.py:451
  35.3 89.4 %collective-permute-start.20 = (bf16[1024,2048]{1,0:T(8,128)(2,1)}, bf16[1024,2048]{1,0:T(8,128)(2,1)}, u32[]{:S(2)}, u32[]{:S(2)}) collective-permute-start(bf16[1024,2048]{1,0:T(8,128)(2,1)} %up_mine.3), channel_id=1, source_target_pairs={{0,1},{1,0},{2,3},{3,2},{4,5},{5,4},{6,7},{7,6},{8,9},{9,8},{10,11... | collective-permute-start | bytes 12582920 | tf_op jit(solution)/shard_map/ppermute | solution.py:451
  35.4 89.3 %collective-permute-start.21 = (bf16[2048,1024]{1,0:T(8,128)(2,1)}, bf16[2048,1024]{1,0:T(8,128)(2,1)}, u32[]{:S(2)}, u32[]{:S(2)}) collective-permute-start(bf16[2048,1024]{1,0:T(8,128)(2,1)} %down_mine.3), channel_id=1, source_target_pairs={{0,1},{1,0},{2,3},{3,2},{4,5},{5,4},{6,7},{7,6},{8,9},{9,8},{10,11... | collective-permute-start | bytes 12582920 | tf_op jit(solution)/shard_map/ppermute | solution.py:451
  64.5 9.2 %collective-permute-start.15 = (bf16[1024,512]{1,0:T(8,128)(2,1)S(1)}, bf16[1024,512]{1,0:T(8,128)(2,1)S(1)}, u32[]{:S(2)}, u32[]{:S(2)}) collective-permute-start(bf16[1024,512]{1,0:T(8,128)(2,1)S(1)} %copy-done.7), channel_id=1, source_target_pairs={{0,1},{1,0},{2,3},{3,2},{4,5},{5,4},{6,7},{7,6},{8,9},{9,8},{10,11... | collective-permute-start | bytes 3145736 | tf_op jit(solution)/shard_map/ppermute | solution.py:451
  68.9 35.2 %collective-permute-start.17 = (bf16[560,1024]{1,0:T(8,128)(2,1)S(1)}, bf16[560,1024]{1,0:T(8,128)(2,1)}, u32[]{:S(2)}, u32[]{:S(2)}) collective-permute-start(bf16[560,1024]{1,0:T(8,128)(2,1)S(1)} %pad_maximum_fusion), channel_id=1, source_target_pairs={{1,2},{3,4},{5,6},{7,8},{9,10},{11,12},{13,14},{15,16},{17,18},{19... | collective-permute-start | bytes 3440648 | tf_op jit(solution)/shard_map/ppermute | solution.py:549
  73.7 4.1 %collective-permute-start.14 = (bf16[1024,512]{1,0:T(8,128)(2,1)S(1)}, bf16[1024,512]{1,0:T(8,128)(2,1)S(1)}, u32[]{:S(2)}, u32[]{:S(2)}) collective-permute-start(bf16[1024,512]{1,0:T(8,128)(2,1)S(1)} %copy-done.6), channel_id=1, source_target_pairs={{0,1},{1,0},{2,3},{3,2},{4,5},{5,4},{6,7},{7,6},{8,9},{9,8},{10,11... | collective-permute-start | bytes 3145736 | tf_op jit(solution)/shard_map/ppermute | solution.py:451
  105.3 19.4 %collective-permute-start.19 = (bf16[512,1024]{1,0:T(8,128)(2,1)S(1)}, bf16[512,1024]{1,0:T(8,128)(2,1)S(1)}, u32[]{:S(2)}, u32[]{:S(2)}) collective-permute-start(bf16[512,1024]{1,0:T(8,128)(2,1)S(1)} %copy-done.9), channel_id=1, source_target_pairs={{0,1},{1,0},{2,3},{3,2},{4,5},{5,4},{6,7},{7,6},{8,9},{9,8},{10,11... | collective-permute-start | bytes 3145736 | tf_op jit(solution)/shard_map/ppermute | solution.py:451
  141.9 16.9 %collective-permute-start.24 = (bf16[320,1024]{1,0:T(8,128)(2,1)}, bf16[320,1024]{1,0:T(8,128)(2,1)}, u32[]{:S(2)}, u32[]{:S(2)}) collective-permute-start(bf16[320,1024]{1,0:T(8,128)(2,1)} %get-tuple-element.22.refs_0_), channel_id=1, source_target_pairs={{0,2},{2,0},{4,6},{6,4},{8,10},{10,8},{12,14},{14,12},{16,18},{18,... | collective-permute-start | bytes 1966088 | tf_op jit(solution)/shard_map/ppermute | solution.py:454
  142.1 18.7 %collective-permute-start.35 = (bf16[512,128]{1,0:T(8,128)(2,1)S(1)}, bf16[512,128]{1,0:T(8,128)(2,1)S(1)}, u32[]{:S(2)}, u32[]{:S(2)}) collective-permute-start(bf16[512,128]{1,0:T(8,128)(2,1)S(1)} %pad.22.refs_18_), channel_id=1, source_target_pairs={{0,1},{1,0},{2,3},{3,2},{4,5},{5,4},{6,7},{7,6},{8,9},{9,8},{10,11... | collective-permute-start | bytes 393224 | tf_op jit(solution)/shard_map/ppermute | solution.py:451
  142.3 29.9 %collective-permute-start.33 = (bf16[1024,512]{1,0:T(8,128)(2,1)S(1)}, bf16[1024,512]{1,0:T(8,128)(2,1)}, u32[]{:S(2)}, u32[]{:S(2)}) collective-permute-start(bf16[1024,512]{1,0:T(8,128)(2,1)S(1)} %copy-done.14), channel_id=1, source_target_pairs={{0,1},{1,0},{2,3},{3,2},{4,5},{5,4},{6,7},{7,6},{8,9},{9,8},{10,11... | collective-permute-start | bytes 3145736 | tf_op jit(solution)/shard_map/ppermute | solution.py:451
  142.7 29.6 %collective-permute-start.34 = (bf16[1024,512]{1,0:T(8,128)(2,1)}, bf16[1024,512]{1,0:T(8,128)(2,1)}, u32[]{:S(2)}, u32[]{:S(2)}) collective-permute-start(bf16[1024,512]{1,0:T(8,128)(2,1)} %refs_16_.1), channel_id=1, source_target_pairs={{0,1},{1,0},{2,3},{3,2},{4,5},{5,4},{6,7},{7,6},{8,9},{9,8},{10,11... | collective-permute-start | bytes 3145736 | tf_op jit(solution)/shard_map/ppermute | solution.py:451
  157.0 11.3 %collective-permute-start.28 = (bf16[192,1024]{1,0:T(8,128)(2,1)}, bf16[192,1024]{1,0:T(8,128)(2,1)S(1)}, u32[]{:S(2)}, u32[]{:S(2)}) collective-permute-start(bf16[192,1024]{1,0:T(8,128)(2,1)} %get-tuple-element.23.refs_2_), channel_id=1, source_target_pairs={{0,2},{2,0},{4,6},{6,4},{8,10},{10,8},{12,14},{14,12},{16,18},{18,... | collective-permute-start | bytes 1179656 | tf_op jit(solution)/shard_map/ppermute | solution.py:454
  158.8 18.9 %collective-permute-start.26 = (bf16[320,1024]{1,0:T(8,128)(2,1)}, bf16[320,1024]{1,0:T(8,128)(2,1)}, u32[]{:S(2)}, u32[]{:S(2)}) collective-permute-start(bf16[320,1024]{1,0:T(8,128)(2,1)} %collective-permute-done.24.refs_4_), channel_id=1, source_target_pairs={{0,4},{4,8},{8,12},{12,16},{16,20},{20,24},{24,28},{6,2},{10,6},{1... | collective-permute-start | bytes 1966088 | tf_op jit(solution)/shard_map/ppermute | solution.py:458
  164.0 10.8 %collective-permute-start.37 = (bf16[192,512]{1,0:T(8,128)(2,1)}, bf16[192,512]{1,0:T(8,128)(2,1)}, u32[]{:S(2)}, u32[]{:S(2)}) collective-permute-start(bf16[192,512]{1,0:T(8,128)(2,1)} %get-tuple-element.33), channel_id=1, source_target_pairs={{0,1},{1,0},{2,3},{3,2},{4,5},{5,4},{6,7},{7,6},{8,9},{9,8},{10,11... | collective-permute-start | bytes 589832 | tf_op jit(solution)/shard_map/ppermute | solution.py:451
  168.3 7.4 %collective-permute-start.36 = (bf16[320,512]{1,0:T(8,128)(2,1)}, bf16[320,512]{1,0:T(8,128)(2,1)}, u32[]{:S(2)}, u32[]{:S(2)}) collective-permute-start(bf16[320,512]{1,0:T(8,128)(2,1)} %get-tuple-element.31), channel_id=1, source_target_pairs={{0,1},{1,0},{2,3},{3,2},{4,5},{5,4},{6,7},{7,6},{8,9},{9,8},{10,11... | collective-permute-start | bytes 983048 | tf_op jit(solution)/shard_map/ppermute | solution.py:451
  172.2 7.3 %collective-permute-start.23 = (bf16[192,1024]{1,0:T(8,128)(2,1)S(1)}, bf16[192,1024]{1,0:T(8,128)(2,1)S(1)}, u32[]{:S(2)}, u32[]{:S(2)}) collective-permute-start(bf16[192,1024]{1,0:T(8,128)(2,1)S(1)} %copy-done.23), channel_id=1, source_target_pairs={{0,1},{1,0},{2,3},{3,2},{4,5},{5,4},{6,7},{7,6},{8,9},{9,8},{10,11... | collective-permute-start | bytes 1179656 | tf_op jit(solution)/shard_map/ppermute | solution.py:451
  172.3 14.2 %collective-permute-start.30 = (bf16[192,1024]{1,0:T(8,128)(2,1)}, bf16[192,1024]{1,0:T(8,128)(2,1)S(1)}, u32[]{:S(2)}, u32[]{:S(2)}) collective-permute-start(bf16[192,1024]{1,0:T(8,128)(2,1)} %hold.1.refs_8_), channel_id=1, source_target_pairs={{0,4},{4,8},{8,12},{12,16},{16,20},{20,24},{24,28},{6,2},{10,6},{1... | collective-permute-start | bytes 1179656 | tf_op jit(solution)/shard_map/ppermute | solution.py:458
  174.9 15.1 %collective-permute-start.22 = (bf16[320,1024]{1,0:T(8,128)(2,1)S(1)}, bf16[320,1024]{1,0:T(8,128)(2,1)S(1)}, u32[]{:S(2)}, u32[]{:S(2)}) collective-permute-start(bf16[320,1024]{1,0:T(8,128)(2,1)S(1)} %copy-done.17), channel_id=1, source_target_pairs={{0,1},{1,0},{2,3},{3,2},{4,5},{5,4},{6,7},{7,6},{8,9},{9,8},{10,11... | collective-permute-start | bytes 1966088 | tf_op jit(solution)/shard_map/ppermute | solution.py:451
  175.7 14.4 %collective-permute-start.25 = (bf16[320,1024]{1,0:T(8,128)(2,1)}, bf16[320,1024]{1,0:T(8,128)(2,1)S(1)}, u32[]{:S(2)}, u32[]{:S(2)}) collective-permute-start(bf16[320,1024]{1,0:T(8,128)(2,1)} %collective-permute-done.24.refs_4_), channel_id=1, source_target_pairs={{0,1},{1,0},{2,3},{3,2},{4,5},{5,4},{6,7},{7,6},{8,9},{9,8},{10,11... | collective-permute-start | bytes 1966088 | tf_op jit(solution)/shard_map/ppermute | solution.py:451
  177.7 12.4 %collective-permute-start.27 = (bf16[320,1024]{1,0:T(8,128)(2,1)}, bf16[320,1024]{1,0:T(8,128)(2,1)S(1)}, u32[]{:S(2)}, u32[]{:S(2)}) collective-permute-start(bf16[320,1024]{1,0:T(8,128)(2,1)} %collective-permute-done.26.refs_6_), channel_id=1, source_target_pairs={{0,1},{1,0},{2,3},{3,2},{4,5},{5,4},{6,7},{7,6},{8,9},{9,8},{10,11... | collective-permute-start | bytes 1966088 | tf_op jit(solution)/shard_map/ppermute | solution.py:451
  179.5 10.5 %collective-permute-start.29 = (bf16[192,1024]{1,0:T(8,128)(2,1)}, bf16[192,1024]{1,0:T(8,128)(2,1)S(1)}, u32[]{:S(2)}, u32[]{:S(2)}) collective-permute-start(bf16[192,1024]{1,0:T(8,128)(2,1)} %hold.1.refs_8_), channel_id=1, source_target_pairs={{0,1},{1,0},{2,3},{3,2},{4,5},{5,4},{6,7},{7,6},{8,9},{9,8},{10,11... | collective-permute-start | bytes 1179656 | tf_op jit(solution)/shard_map/ppermute | solution.py:451
  186.5 3.5 %collective-permute-start.31 = (bf16[192,1024]{1,0:T(8,128)(2,1)S(1)}, bf16[192,1024]{1,0:T(8,128)(2,1)S(1)}, u32[]{:S(2)}, u32[]{:S(2)}) collective-permute-start(bf16[192,1024]{1,0:T(8,128)(2,1)S(1)} %collective-permute-done.30.refs_10_), channel_id=1, source_target_pairs={{0,1},{1,0},{2,3},{3,2},{4,5},{5,4},{6,7},{7,6},{8,9},{9,8},{10,11... | collective-permute-start | bytes 1179656 | tf_op jit(solution)/shard_map/ppermute | solution.py:451
  (55 other events, 421.6 us)

commit v5 on v4

--- a/solution.py
+++ b/solution.py
@@ -63,7 +63,7 @@
 
 GRID_CHUNKS = 2
 GROUP = 8
-CHAINS = 8
+CHAINS = 16
 
 
 def encoder_kernel(

time: 241 us -> 240 us (level)
  no operation moved by 1% of the time
where the time goes in v5:
time: 240 us; the launch traced here: 239 us
  Pallas kernels  151 us (63%)
  starting transfers between devices  32.5 us (14%)
  waiting for transfers between devices  28.2 us (12%)
  local copies, waits for them, and re-layouts  19.3 us (8%)
  other arithmetic  6.59 us (3%)
    pallas_call x1, Pallas kernels, local(): pl.pallas_call(functools.partial(decoder_kernel, spots=tuple(node_spots))...  48.3 us
    pallas_call x2, Pallas kernels, feed(): pl.pallas_call(functools.partial(feed_kernel, start=start), grid=(2 * ste...  30.3 us
    pallas_call x1, Pallas kernels, local(): pl.pallas_call(functools.partial(encoder_kernel, spots=tuple(grid_spots))...  25.5 us
    pallas_call x1, Pallas kernels, local(): pl.pallas_call(near_window_kernel, out_shape=(jax.ShapeDtypeStruct((pairs...  23.4 us
    pallas_call x1, Pallas kernels, local(): pl.pallas_call(far_window_kernel, out_shape=jax.ShapeDtypeStruct((pairs,...  17.6 us
    ppermute x29, starting transfers between devices, swap(): return lax.ppermute(x, 'head', [(0, 1), (1, 0)])  15 us
    ppermute x4, waiting for transfers between devices, pass_on(): return lax.ppermute(x, 'band', jumps)  13.8 us
    ppermute x4, starting transfers between devices, pass_on(): return lax.ppermute(x, 'band', jumps)  9.47 us
  transfers between devices with their start and end apart: 38, of which 12 were waited for; matrix products, arithmetic and copies ran while one was open for 8% of the time, Pallas kernels for 36%

profile of v5, /device:TPU:23, one launch (start us, length us, event | category | flops | bytes accessed | tf_op | source)
XLA Modules:
  0.0 239.2 jit_solution(9283401121713656547)
XLA Ops:
  1.4 2.1 constant_dynamic-slice_fusion.7
  5.3 1.2 collective-permute-start.3
  9.0 2.9 %collective-permute-done.4.refs_0_ = bf16[1024,100]{1,0:T(8,128)(2,1)S(1)} collective-permute-done((bf16[1024,100]{1,0:T(8,128)(2,1)S(1)}, bf16[1024,100]{1,0:T(8,128)(2,1)S(1)}, u32[]{:S(2)}, u32[]{:S(2)}) %collective-permute-start.4) | collective-permute-done | bytes 204832 | tf_op jit(solution)/shard_map/ppermute | solution.py:454
  11.9 2.0 collective-permute-start.2
  14.0 2.1 collective-permute-start.6
  16.1 1.3 maximum_select_fusion.state.refs_12_
  18.0 5.5 %queries.1 = (bf16[16,512,128]{2,1,0:T(8,128)(2,1)}, bf16[1024,100]{1,0:T(8,128)(2,1)}) custom-call(bf16[512,1024]{1,0:T(8,128)(2,1)} %maximum_select_fusion.state.refs_12_, bf16[1024,512]{1,0:T(8,128)(2,1)} %wq_mine.1, bf16[1024,512]{1,0:T(8,128)(2,1)} %collective-permute-done.1.wq_other, ...), custom_call_target="tpu_custom_call", output_to_operand_aliasing={{1}: (5, {})} | custom-call | flops 3221225472 | bytes 12582912 | tf_op jit(solution)/shard_map/queries/pallas_call | solution.py:507
  23.6 3.0 %collective-permute-start.9 = (bf16[1024,100]{1,0:T(8,128)(2,1)}, bf16[1024,100]{1,0:T(8,128)(2,1)S(1)}, u32[]{:S(2)}, u32[]{:S(2)}) collective-permute-start(bf16[1024,100]{1,0:T(8,128)(2,1)} %get-tuple-element.15.refs_4_), channel_id=1, source_target_pairs={{0,4},{4,8},{8,12},{12,16},{16,20},{20,24},{24,28},{6,2},{10,6},{1... | collective-permute-start | bytes 614408 | tf_op jit(solution)/shard_map/ppermute | solution.py:458
  28.6 4.9 %collective-permute-done.9.refs_6_ = bf16[1024,100]{1,0:T(8,128)(2,1)S(1)} collective-permute-done((bf16[1024,100]{1,0:T(8,128)(2,1)}, bf16[1024,100]{1,0:T(8,128)(2,1)S(1)}, u32[]{:S(2)}, u32[]{:S(2)}) %collective-permute-start.9) | collective-permute-done | bytes 204832 | tf_op jit(solution)/shard_map/ppermute | solution.py:458
  33.6 1.7 collective-permute-start.10
  37.2 25.5 %encoder.1 = (bf16[512,1024]{1,0:T(8,128)(2,1)}, bf16[512,1024]{1,0:T(8,128)(2,1)}) custom-call(s32[13]{0:T(128)} %stack.51.refs_0_.info, s32[16384]{0:T(1024)} %reshape.11.refs_1_.sources, s32[512,1]{1,0:T(8,128)} %copy.31.refs_2_.counts, bf16[16,512,128]{2,1,0:T(8,128)(2,1)} %get-tuple-element.14.query, bf16[4096,100]{1,0:T(8,128)(2,1)} %copy-done.2, ...), custom_call_target="tpu_custom_call" | custom-call | flops 8589934592 | bytes 33554432 | tf_op jit(solution)/shard_map/encoder/pallas_call | solution.py:528
  63.3 2.5 %collective-permute-done.13.refs_1_ = bf16[512,1024]{1,0:T(8,128)(2,1)S(1)} collective-permute-done((bf16[512,1024]{1,0:T(8,128)(2,1)}, bf16[512,1024]{1,0:T(8,128)(2,1)S(1)}, u32[]{:S(2)}, u32[]{:S(2)}) %collective-permute-start.13) | collective-permute-done | bytes 1048608 | tf_op jit(solution)/shard_map/ppermute | solution.py:451
  65.7 1.7 pad_maximum_fusion
  67.4 4.7 %collective-permute-start.17 = (bf16[560,1024]{1,0:T(8,128)(2,1)S(1)}, bf16[560,1024]{1,0:T(8,128)(2,1)}, u32[]{:S(2)}, u32[]{:S(2)}) collective-permute-start(bf16[560,1024]{1,0:T(8,128)(2,1)S(1)} %pad_maximum_fusion), channel_id=1, source_target_pairs={{1,2},{3,4},{5,6},{7,8},{9,10},{11,12},{13,14},{15,16},{17,18},{19... | collective-permute-start | bytes 3440648 | tf_op jit(solution)/shard_map/ppermute | solution.py:549
  72.8 2.1 collective-permute-done.16.refs_7_.refs_5_
  76.3 1.0 copy-done.13
  77.4 23.4 %near_window.1 = (bf16[8,512,128]{2,1,0:T(8,128)(2,1)}, f32[8,512,128]{2,1,0:T(8,128)}, f32[8,512,128]{2,1,0:T(8,128)}, s32[8,128]{1,0:T(8,128)}) custom-call(s32[13]{0:T(128)} %stack.51.refs_0_.info, bf16[512,1024]{1,0:T(8,128)(2,1)} %get-tuple-element.16.refs_0_, bf16[512,1024]{1,0:T(8,128)(2,1)} %copy-done.5, bf16[1024,512]{1,0:T(8,128)(2,1)} %refs_2_.2, ...), custom_call_target="tpu_custom_call" | custom-call | flops 1024 | bytes 4 | tf_op jit(solution)/shard_map/near_window/pallas_call | solution.py:554
  100.7 1.2 slice.25
  105.6 17.6 %far_window.1.mix = bf16[8,512,128]{2,1,0:T(8,128)(2,1)} custom-call(s32[13]{0:T(128)} %stack.51.refs_0_.info, bf16[8,512,128]{2,1,0:T(8,128)(2,1)} %get-tuple-element.17.query, f32[8,512,128]{2,1,0:T(8,128)} %get-tuple-element.18.near_mix, f32[8,512,128]{2,1,0:T(8,128)} %get-tuple-element.19.near_total, bf16[560,1024]{1,0:T(8,128)(2,1)} %collective-permute-done.17.refs_0_, ...), custom_call_target="tpu_custom_call" | custom-call | flops 10737418240 | bytes 41943040 | tf_op jit(solution)/shard_map/far_window/pallas_call | solution.py:579
  124.2 16.2 %feed.2 = (bf16[320,1024]{1,0:T(8,128)(2,1)}, bf16[320,1024]{1,0:T(8,128)(2,1)}) custom-call(bf16[8,512,128]{2,1,0:T(8,128)(2,1)} %far_window.1.mix, bf16[512,1024]{1,0:T(8,128)(2,1)} %get-tuple-element.21.mid, bf16[512,1024]{1,0:T(8,128)(2,1)} %wo_mine.3, bf16[512,1024]{1,0:T(8,128)(2,1)} %copy-done.12, bf16[1024,2048]{1,0:T(8,128)(2,1)} %up_mine.3, ...), custom_call_target="tpu_custom_call" | custom-call | flops 6039797760 | bytes 23592960 | tf_op jit(solution)/shard_map/feed/pallas_call | solution.py:605
  141.3 14.1 %feed.3 = (bf16[192,1024]{1,0:T(8,128)(2,1)}, bf16[192,1024]{1,0:T(8,128)(2,1)}) custom-call(bf16[8,512,128]{2,1,0:T(8,128)(2,1)} %far_window.1.mix, bf16[512,1024]{1,0:T(8,128)(2,1)} %get-tuple-element.21.mid, bf16[512,1024]{1,0:T(8,128)(2,1)} %wo_mine.3, bf16[512,1024]{1,0:T(8,128)(2,1)} %copy-done.12, bf16[1024,2048]{1,0:T(8,128)(2,1)} %up_mine.3, ...), custom_call_target="tpu_custom_call" | custom-call | flops 3623878656 | bytes 14155776 | tf_op jit(solution)/shard_map/feed/pallas_call | solution.py:605
  155.5 1.8 collective-permute-start.28
  157.3 1.9 collective-permute-start.26
  159.9 1.8 constant_dynamic-slice_fusion.4
  162.6 4.3 %collective-permute-done.28.refs_0_ = bf16[192,1024]{1,0:T(8,128)(2,1)S(1)} collective-permute-done((bf16[192,1024]{1,0:T(8,128)(2,1)}, bf16[192,1024]{1,0:T(8,128)(2,1)S(1)}, u32[]{:S(2)}, u32[]{:S(2)}) %collective-permute-start.28) | collective-permute-done | bytes 393248 | tf_op jit(solution)/shard_map/ppermute | solution.py:454
  168.0 1.2 reshape.10.refs_1_.sources
  170.8 2.4 %collective-permute-start.30 = (bf16[192,1024]{1,0:T(8,128)(2,1)}, bf16[192,1024]{1,0:T(8,128)(2,1)S(1)}, u32[]{:S(2)}, u32[]{:S(2)}) collective-permute-start(bf16[192,1024]{1,0:T(8,128)(2,1)} %hold.1.refs_8_), channel_id=1, source_target_pairs={{0,4},{4,8},{8,12},{12,16},{16,20},{20,24},{24,28},{6,2},{10,6},{1... | collective-permute-start | bytes 1179656 | tf_op jit(solution)/shard_map/ppermute | solution.py:458
  174.2 2.0 collective-permute-done.26.refs_6_
  176.2 1.8 collective-permute-start.27
  178.1 6.9 %collective-permute-done.30.refs_10_ = bf16[192,1024]{1,0:T(8,128)(2,1)S(1)} collective-permute-done((bf16[192,1024]{1,0:T(8,128)(2,1)}, bf16[192,1024]{1,0:T(8,128)(2,1)S(1)}, u32[]{:S(2)}, u32[]{:S(2)}) %collective-permute-start.30) | collective-permute-done | bytes 393248 | tf_op jit(solution)/shard_map/ppermute | solution.py:458
  185.9 2.6 %maximum_select_fusion.1 = bf16[1024,512]{1,0:T(8,128)(2,1)} fusion(bf16[192,512]{1,0:T(8,128)(2,1)} %collective-permute-done.37, bf16[320,512]{1,0:T(8,128)(2,1)} %collective-permute-done.36, bf16[192,512]{1,0:T(8,128)(2,1)} %get-tuple-element.32, bf16[320,512]{1,0:T(8,128)(2,1)S(1)} %get-tuple-element.30, pred[]{:T(512)S(6)} %eq.14), kind=kLoop, calls=%fused_computation.2 | loop fusion | flops 8912896 | bytes 2097153 | tf_op jit(solution)/shard_map/jit(_where)/select_n | solution.py:648
  190.7 48.3 %decoder.1 = bf16[100,2048]{1,0:T(8,128)(2,1)} custom-call(s32[13]{0:T(128)} %stack.51.refs_0_.info, s32[8192]{0:T(1024)} %reshape.10.refs_1_.sources, s32[2048]{0:T(1024)} %dynamic_slice.34.refs_2_.counts, bf16[2048,128]{1,0:T(8,128)(2,1)} %pad.18.refs_3_.grid, bf16[320,1024]{1,0:T(8,128)(2,1)} %get-tuple-element.22.refs_0_, bf16[320,1024]{1,0:T(8,128)(2,1)} %copy-done.18, ...), custom_call_target="tpu_custom_call" | custom-call | tf_op jit(solution)/shard_map/decoder/pallas_call | solution.py:668
  (178 shorter events, 25.3 us)
Async XLA Ops:
  0.7 17.0 %collective-permute-start.1 = (bf16[1024,512]{1,0:T(8,128)(2,1)}, bf16[1024,512]{1,0:T(8,128)(2,1)}, u32[]{:S(2)}, u32[]{:S(2)}) collective-permute-start(bf16[1024,512]{1,0:T(8,128)(2,1)} %wq_mine.1), channel_id=1, source_target_pairs={{0,1},{1,0},{2,3},{3,2},{4,5},{5,4},{6,7},{7,6},{8,9},{9,8},{10,11... | collective-permute-start | bytes 3145736 | tf_op jit(solution)/shard_map/ppermute | solution.py:451
  3.5 10.5 %collective-permute-start = (bf16[512,512]{1,0:T(8,128)(2,1)}, bf16[512,512]{1,0:T(8,128)(2,1)S(1)}, u32[]{:S(2)}, u32[]{:S(2)}) collective-permute-start(bf16[512,512]{1,0:T(8,128)(2,1)} %get-tuple-element.29), channel_id=1, source_target_pairs={{0,1},{1,0},{2,3},{3,2},{4,5},{5,4},{6,7},{7,6},{8,9},{9,8},{10,11... | collective-permute-start | bytes 1572872 | tf_op jit(solution)/shard_map/ppermute | solution.py:451
  4.4 7.6 %collective-permute-start.4 = (bf16[1024,100]{1,0:T(8,128)(2,1)S(1)}, bf16[1024,100]{1,0:T(8,128)(2,1)S(1)}, u32[]{:S(2)}, u32[]{:S(2)}) collective-permute-start(bf16[1024,100]{1,0:T(8,128)(2,1)S(1)} %get-tuple-element.26), channel_id=1, source_target_pairs={{0,2},{2,0},{4,6},{6,4},{8,10},{10,8},{12,14},{14,12},{16,18},{18,... | collective-permute-start | bytes 614408 | tf_op jit(solution)/shard_map/ppermute | solution.py:454
  4.7 31.1 %collective-permute-start.12 = (bf16[512,1024]{1,0:T(8,128)(2,1)}, bf16[512,1024]{1,0:T(8,128)(2,1)}, u32[]{:S(2)}, u32[]{:S(2)}) collective-permute-start(bf16[512,1024]{1,0:T(8,128)(2,1)} %refs_10_.1), channel_id=1, source_target_pairs={{0,1},{1,0},{2,3},{3,2},{4,5},{5,4},{6,7},{7,6},{8,9},{9,8},{10,11... | collective-permute-start | bytes 3145736 | tf_op jit(solution)/shard_map/ppermute | solution.py:451
  5.3 12.3 %collective-permute-start.3 = (bf16[1024,100]{1,0:T(8,128)(2,1)S(1)}, bf16[1024,100]{1,0:T(8,128)(2,1)}, u32[]{:S(2)}, u32[]{:S(2)}) collective-permute-start(bf16[1024,100]{1,0:T(8,128)(2,1)S(1)} %get-tuple-element.27), channel_id=1, source_target_pairs={{0,2},{2,0},{4,6},{6,4},{8,10},{10,8},{12,14},{14,12},{16,18},{18,... | collective-permute-start | bytes 614408 | tf_op jit(solution)/shard_map/ppermute | solution.py:454
  11.9 5.5 %collective-permute-start.2 = (bf16[128,512]{1,0:T(8,128)(2,1)S(1)}, bf16[128,512]{1,0:T(8,128)(2,1)S(1)}, u32[]{:S(2)}, u32[]{:S(2)}) collective-permute-start(bf16[128,512]{1,0:T(8,128)(2,1)S(1)} %pad.19.keys_mine), channel_id=1, source_target_pairs={{0,1},{1,0},{2,3},{3,2},{4,5},{5,4},{6,7},{7,6},{8,9},{9,8},{10,11... | collective-permute-start | bytes 393224 | tf_op jit(solution)/shard_map/ppermute | solution.py:451
  14.0 13.4 %collective-permute-start.6 = (bf16[1024,100]{1,0:T(8,128)(2,1)S(1)}, bf16[1024,100]{1,0:T(8,128)(2,1)S(1)}, u32[]{:S(2)}, u32[]{:S(2)}) collective-permute-start(bf16[1024,100]{1,0:T(8,128)(2,1)S(1)} %collective-permute-done.4.refs_0_), channel_id=1, source_target_pairs={{0,4},{4,8},{8,12},{12,16},{16,20},{20,24},{24,28},{6,2},{10,6},{1... | collective-permute-start | bytes 614408 | tf_op jit(solution)/shard_map/ppermute | solution.py:458
  23.6 10.0 %collective-permute-start.9 = (bf16[1024,100]{1,0:T(8,128)(2,1)}, bf16[1024,100]{1,0:T(8,128)(2,1)S(1)}, u32[]{:S(2)}, u32[]{:S(2)}) collective-permute-start(bf16[1024,100]{1,0:T(8,128)(2,1)} %get-tuple-element.15.refs_4_), channel_id=1, source_target_pairs={{0,4},{4,8},{8,12},{12,16},{16,20},{20,24},{24,28},{6,2},{10,6},{1... | collective-permute-start | bytes 614408 | tf_op jit(solution)/shard_map/ppermute | solution.py:458
  27.3 8.0 %collective-permute-start.5 = (bf16[1024,100]{1,0:T(8,128)(2,1)S(1)}, bf16[1024,100]{1,0:T(8,128)(2,1)S(1)}, u32[]{:S(2)}, u32[]{:S(2)}) collective-permute-start(bf16[1024,100]{1,0:T(8,128)(2,1)S(1)} %collective-permute-done.4.refs_0_), channel_id=1, source_target_pairs={{0,1},{1,0},{2,3},{3,2},{4,5},{5,4},{6,7},{7,6},{8,9},{9,8},{10,11... | collective-permute-start | bytes 614408 | tf_op jit(solution)/shard_map/ppermute | solution.py:451
  27.4 8.0 %collective-permute-start.7 = (bf16[1024,100]{1,0:T(8,128)(2,1)S(1)}, bf16[1024,100]{1,0:T(8,128)(2,1)S(1)}, u32[]{:S(2)}, u32[]{:S(2)}) collective-permute-start(bf16[1024,100]{1,0:T(8,128)(2,1)S(1)} %collective-permute-done.6.refs_2_), channel_id=1, source_target_pairs={{0,1},{1,0},{2,3},{3,2},{4,5},{5,4},{6,7},{7,6},{8,9},{9,8},{10,11... | collective-permute-start | bytes 614408 | tf_op jit(solution)/shard_map/ppermute | solution.py:451
  28.3 7.5 %collective-permute-start.8 = (bf16[1024,100]{1,0:T(8,128)(2,1)}, bf16[1024,100]{1,0:T(8,128)(2,1)S(1)}, u32[]{:S(2)}, u32[]{:S(2)}) collective-permute-start(bf16[1024,100]{1,0:T(8,128)(2,1)} %get-tuple-element.15.refs_4_), channel_id=1, source_target_pairs={{0,1},{1,0},{2,3},{3,2},{4,5},{5,4},{6,7},{7,6},{8,9},{9,8},{10,11... | collective-permute-start | bytes 614408 | tf_op jit(solution)/shard_map/ppermute | solution.py:451
  35.3 87.9 %collective-permute-start.20 = (bf16[1024,2048]{1,0:T(8,128)(2,1)}, bf16[1024,2048]{1,0:T(8,128)(2,1)}, u32[]{:S(2)}, u32[]{:S(2)}) collective-permute-start(bf16[1024,2048]{1,0:T(8,128)(2,1)} %up_mine.3), channel_id=1, source_target_pairs={{0,1},{1,0},{2,3},{3,2},{4,5},{5,4},{6,7},{7,6},{8,9},{9,8},{10,11... | collective-permute-start | bytes 12582920 | tf_op jit(solution)/shard_map/ppermute | solution.py:451
  35.4 87.8 %collective-permute-start.21 = (bf16[2048,1024]{1,0:T(8,128)(2,1)}, bf16[2048,1024]{1,0:T(8,128)(2,1)}, u32[]{:S(2)}, u32[]{:S(2)}) collective-permute-start(bf16[2048,1024]{1,0:T(8,128)(2,1)} %down_mine.3), channel_id=1, source_target_pairs={{0,1},{1,0},{2,3},{3,2},{4,5},{5,4},{6,7},{7,6},{8,9},{9,8},{10,11... | collective-permute-start | bytes 12582920 | tf_op jit(solution)/shard_map/ppermute | solution.py:451
  63.1 9.1 %collective-permute-start.15 = (bf16[1024,512]{1,0:T(8,128)(2,1)S(1)}, bf16[1024,512]{1,0:T(8,128)(2,1)S(1)}, u32[]{:S(2)}, u32[]{:S(2)}) collective-permute-start(bf16[1024,512]{1,0:T(8,128)(2,1)S(1)} %copy-done.7), channel_id=1, source_target_pairs={{0,1},{1,0},{2,3},{3,2},{4,5},{5,4},{6,7},{7,6},{8,9},{9,8},{10,11... | collective-permute-start | bytes 3145736 | tf_op jit(solution)/shard_map/ppermute | solution.py:451
  67.4 35.2 %collective-permute-start.17 = (bf16[560,1024]{1,0:T(8,128)(2,1)S(1)}, bf16[560,1024]{1,0:T(8,128)(2,1)}, u32[]{:S(2)}, u32[]{:S(2)}) collective-permute-start(bf16[560,1024]{1,0:T(8,128)(2,1)S(1)} %pad_maximum_fusion), channel_id=1, source_target_pairs={{1,2},{3,4},{5,6},{7,8},{9,10},{11,12},{13,14},{15,16},{17,18},{19... | collective-permute-start | bytes 3440648 | tf_op jit(solution)/shard_map/ppermute | solution.py:549
  72.2 4.1 %collective-permute-start.14 = (bf16[1024,512]{1,0:T(8,128)(2,1)S(1)}, bf16[1024,512]{1,0:T(8,128)(2,1)S(1)}, u32[]{:S(2)}, u32[]{:S(2)}) collective-permute-start(bf16[1024,512]{1,0:T(8,128)(2,1)S(1)} %copy-done.6), channel_id=1, source_target_pairs={{0,1},{1,0},{2,3},{3,2},{4,5},{5,4},{6,7},{7,6},{8,9},{9,8},{10,11... | collective-permute-start | bytes 3145736 | tf_op jit(solution)/shard_map/ppermute | solution.py:451
  103.8 19.4 %collective-permute-start.19 = (bf16[512,1024]{1,0:T(8,128)(2,1)S(1)}, bf16[512,1024]{1,0:T(8,128)(2,1)S(1)}, u32[]{:S(2)}, u32[]{:S(2)}) collective-permute-start(bf16[512,1024]{1,0:T(8,128)(2,1)S(1)} %copy-done.9), channel_id=1, source_target_pairs={{0,1},{1,0},{2,3},{3,2},{4,5},{5,4},{6,7},{7,6},{8,9},{9,8},{10,11... | collective-permute-start | bytes 3145736 | tf_op jit(solution)/shard_map/ppermute | solution.py:451
  140.4 16.9 %collective-permute-start.24 = (bf16[320,1024]{1,0:T(8,128)(2,1)}, bf16[320,1024]{1,0:T(8,128)(2,1)}, u32[]{:S(2)}, u32[]{:S(2)}) collective-permute-start(bf16[320,1024]{1,0:T(8,128)(2,1)} %get-tuple-element.22.refs_0_), channel_id=1, source_target_pairs={{0,2},{2,0},{4,6},{6,4},{8,10},{10,8},{12,14},{14,12},{16,18},{18,... | collective-permute-start | bytes 1966088 | tf_op jit(solution)/shard_map/ppermute | solution.py:454
  140.6 18.7 %collective-permute-start.35 = (bf16[512,128]{1,0:T(8,128)(2,1)S(1)}, bf16[512,128]{1,0:T(8,128)(2,1)S(1)}, u32[]{:S(2)}, u32[]{:S(2)}) collective-permute-start(bf16[512,128]{1,0:T(8,128)(2,1)S(1)} %pad.22.refs_18_), channel_id=1, source_target_pairs={{0,1},{1,0},{2,3},{3,2},{4,5},{5,4},{6,7},{7,6},{8,9},{9,8},{10,11... | collective-permute-start | bytes 393224 | tf_op jit(solution)/shard_map/ppermute | solution.py:451
  140.8 29.9 %collective-permute-start.33 = (bf16[1024,512]{1,0:T(8,128)(2,1)S(1)}, bf16[1024,512]{1,0:T(8,128)(2,1)}, u32[]{:S(2)}, u32[]{:S(2)}) collective-permute-start(bf16[1024,512]{1,0:T(8,128)(2,1)S(1)} %copy-done.14), channel_id=1, source_target_pairs={{0,1},{1,0},{2,3},{3,2},{4,5},{5,4},{6,7},{7,6},{8,9},{9,8},{10,11... | collective-permute-start | bytes 3145736 | tf_op jit(solution)/shard_map/ppermute | solution.py:451
  141.2 29.6 %collective-permute-start.34 = (bf16[1024,512]{1,0:T(8,128)(2,1)}, bf16[1024,512]{1,0:T(8,128)(2,1)}, u32[]{:S(2)}, u32[]{:S(2)}) collective-permute-start(bf16[1024,512]{1,0:T(8,128)(2,1)} %refs_16_.1), channel_id=1, source_target_pairs={{0,1},{1,0},{2,3},{3,2},{4,5},{5,4},{6,7},{7,6},{8,9},{9,8},{10,11... | collective-permute-start | bytes 3145736 | tf_op jit(solution)/shard_map/ppermute | solution.py:451
  155.5 11.3 %collective-permute-start.28 = (bf16[192,1024]{1,0:T(8,128)(2,1)}, bf16[192,1024]{1,0:T(8,128)(2,1)S(1)}, u32[]{:S(2)}, u32[]{:S(2)}) collective-permute-start(bf16[192,1024]{1,0:T(8,128)(2,1)} %get-tuple-element.23.refs_2_), channel_id=1, source_target_pairs={{0,2},{2,0},{4,6},{6,4},{8,10},{10,8},{12,14},{14,12},{16,18},{18,... | collective-permute-start | bytes 1179656 | tf_op jit(solution)/shard_map/ppermute | solution.py:454
  157.3 18.9 %collective-permute-start.26 = (bf16[320,1024]{1,0:T(8,128)(2,1)}, bf16[320,1024]{1,0:T(8,128)(2,1)}, u32[]{:S(2)}, u32[]{:S(2)}) collective-permute-start(bf16[320,1024]{1,0:T(8,128)(2,1)} %collective-permute-done.24.refs_4_), channel_id=1, source_target_pairs={{0,4},{4,8},{8,12},{12,16},{16,20},{20,24},{24,28},{6,2},{10,6},{1... | collective-permute-start | bytes 1966088 | tf_op jit(solution)/shard_map/ppermute | solution.py:458
  162.5 10.7 %collective-permute-start.37 = (bf16[192,512]{1,0:T(8,128)(2,1)}, bf16[192,512]{1,0:T(8,128)(2,1)}, u32[]{:S(2)}, u32[]{:S(2)}) collective-permute-start(bf16[192,512]{1,0:T(8,128)(2,1)} %get-tuple-element.33), channel_id=1, source_target_pairs={{0,1},{1,0},{2,3},{3,2},{4,5},{5,4},{6,7},{7,6},{8,9},{9,8},{10,11... | collective-permute-start | bytes 589832 | tf_op jit(solution)/shard_map/ppermute | solution.py:451
  166.8 7.3 %collective-permute-start.36 = (bf16[320,512]{1,0:T(8,128)(2,1)}, bf16[320,512]{1,0:T(8,128)(2,1)}, u32[]{:S(2)}, u32[]{:S(2)}) collective-permute-start(bf16[320,512]{1,0:T(8,128)(2,1)} %get-tuple-element.31), channel_id=1, source_target_pairs={{0,1},{1,0},{2,3},{3,2},{4,5},{5,4},{6,7},{7,6},{8,9},{9,8},{10,11... | collective-permute-start | bytes 983048 | tf_op jit(solution)/shard_map/ppermute | solution.py:451
  170.7 7.3 %collective-permute-start.23 = (bf16[192,1024]{1,0:T(8,128)(2,1)S(1)}, bf16[192,1024]{1,0:T(8,128)(2,1)S(1)}, u32[]{:S(2)}, u32[]{:S(2)}) collective-permute-start(bf16[192,1024]{1,0:T(8,128)(2,1)S(1)} %copy-done.23), channel_id=1, source_target_pairs={{0,1},{1,0},{2,3},{3,2},{4,5},{5,4},{6,7},{7,6},{8,9},{9,8},{10,11... | collective-permute-start | bytes 1179656 | tf_op jit(solution)/shard_map/ppermute | solution.py:451
  170.8 14.2 %collective-permute-start.30 = (bf16[192,1024]{1,0:T(8,128)(2,1)}, bf16[192,1024]{1,0:T(8,128)(2,1)S(1)}, u32[]{:S(2)}, u32[]{:S(2)}) collective-permute-start(bf16[192,1024]{1,0:T(8,128)(2,1)} %hold.1.refs_8_), channel_id=1, source_target_pairs={{0,4},{4,8},{8,12},{12,16},{16,20},{20,24},{24,28},{6,2},{10,6},{1... | collective-permute-start | bytes 1179656 | tf_op jit(solution)/shard_map/ppermute | solution.py:458
  173.3 15.3 %collective-permute-start.22 = (bf16[320,1024]{1,0:T(8,128)(2,1)S(1)}, bf16[320,1024]{1,0:T(8,128)(2,1)S(1)}, u32[]{:S(2)}, u32[]{:S(2)}) collective-permute-start(bf16[320,1024]{1,0:T(8,128)(2,1)S(1)} %copy-done.17), channel_id=1, source_target_pairs={{0,1},{1,0},{2,3},{3,2},{4,5},{5,4},{6,7},{7,6},{8,9},{9,8},{10,11... | collective-permute-start | bytes 1966088 | tf_op jit(solution)/shard_map/ppermute | solution.py:451
  174.1 14.5 %collective-permute-start.25 = (bf16[320,1024]{1,0:T(8,128)(2,1)}, bf16[320,1024]{1,0:T(8,128)(2,1)S(1)}, u32[]{:S(2)}, u32[]{:S(2)}) collective-permute-start(bf16[320,1024]{1,0:T(8,128)(2,1)} %collective-permute-done.24.refs_4_), channel_id=1, source_target_pairs={{0,1},{1,0},{2,3},{3,2},{4,5},{5,4},{6,7},{7,6},{8,9},{9,8},{10,11... | collective-permute-start | bytes 1966088 | tf_op jit(solution)/shard_map/ppermute | solution.py:451
  176.2 12.4 %collective-permute-start.27 = (bf16[320,1024]{1,0:T(8,128)(2,1)}, bf16[320,1024]{1,0:T(8,128)(2,1)S(1)}, u32[]{:S(2)}, u32[]{:S(2)}) collective-permute-start(bf16[320,1024]{1,0:T(8,128)(2,1)} %collective-permute-done.26.refs_6_), channel_id=1, source_target_pairs={{0,1},{1,0},{2,3},{3,2},{4,5},{5,4},{6,7},{7,6},{8,9},{9,8},{10,11... | collective-permute-start | bytes 1966088 | tf_op jit(solution)/shard_map/ppermute | solution.py:451
  178.0 10.5 %collective-permute-start.29 = (bf16[192,1024]{1,0:T(8,128)(2,1)}, bf16[192,1024]{1,0:T(8,128)(2,1)S(1)}, u32[]{:S(2)}, u32[]{:S(2)}) collective-permute-start(bf16[192,1024]{1,0:T(8,128)(2,1)} %hold.1.refs_8_), channel_id=1, source_target_pairs={{0,1},{1,0},{2,3},{3,2},{4,5},{5,4},{6,7},{7,6},{8,9},{9,8},{10,11... | collective-permute-start | bytes 1179656 | tf_op jit(solution)/shard_map/ppermute | solution.py:451
  185.0 3.5 %collective-permute-start.31 = (bf16[192,1024]{1,0:T(8,128)(2,1)S(1)}, bf16[192,1024]{1,0:T(8,128)(2,1)S(1)}, u32[]{:S(2)}, u32[]{:S(2)}) collective-permute-start(bf16[192,1024]{1,0:T(8,128)(2,1)S(1)} %collective-permute-done.30.refs_10_), channel_id=1, source_target_pairs={{0,1},{1,0},{2,3},{3,2},{4,5},{5,4},{6,7},{7,6},{8,9},{9,8},{10,11... | collective-permute-start | bytes 1179656 | tf_op jit(solution)/shard_map/ppermute | solution.py:451
  (55 other events, 419.6 us)
